TPU v7x, 512 devices: a whole 4x8x8 slice. The times are simulated.
512 devices in a mesh: dp: 64 (over x, y_lo, z), tensor: 8 (over y_hi, core).
Axes of the slice: x: 4, y: 8 (y_hi: 4, y_lo: 2; y = y_hi * 2 + y_lo), z: 8, core: 2. Of those that a mesh axis runs over, the one named last changes fastest.
Arguments:
- acts: bfloat16 [8192, 4096], P('dp', 'tensor'), may hold values from -410 to 410
- grads_out: bfloat16 [8192, 32768], P('dp', 'tensor'), may hold values from -410 to 410
- grad: bfloat16 [4096, 32768], P('tensor', 'dp'), may hold values from -6 to 6
Outputs:
- precond: float32 [4096, 32768], P('tensor', 'dp')
All inputs are finite; a program needn't handle non-finite values.
Results may differ from a plain program's by a relative error of at most 0.0012.
The roundings to bfloat16 on the way count: a program that leaves them out, or rounds other values in their place, can miss the bound.
Values may be sent and summed in bfloat16 or wider, within the bound.
No kernel may reach another device: no remote copies, remote signals or barrier semaphores. Data moves between devices by JAX's collectives and lax.ppermute only.
A program may use at most 64 MiB of HBM per device.

v0:
```python
import jax
import jax.numpy as jnp
from jax import lax
from jax.sharding import PartitionSpec as P

NEWTON = 2


DAMPING = 0.1
PRECISE = lax.Precision.HIGHEST


def keep_both(pair):
    return pair


def keep_total(total):
    return total


def newton_root(shifted, identity_part, gather_both, norm_total):
    squares = jnp.sum(shifted * shifted)
    frob_norm = jnp.sqrt(norm_total(squares))
    iterate_y = shifted / frob_norm
    iterate_z = identity_part
    for iteration in range(NEWTON):
        full_y, full_z = gather_both((iterate_y, iterate_z))
        update = 1.5 * identity_part - 0.5 * jnp.dot(
            iterate_z, full_y, precision=PRECISE, preferred_element_type=jnp.float32
        )
        if iteration + 1 < NEWTON:
            iterate_y = jnp.dot(
                update, full_y, precision=PRECISE, preferred_element_type=jnp.float32
            )
        iterate_z = jnp.dot(update, full_z, precision=PRECISE, preferred_element_type=jnp.float32)
    return (iterate_z / jnp.sqrt(frob_norm)).astype(jnp.bfloat16)


def token_gram(data):
    return lax.dot_general(data, data, (((0,), (0,)), ((), ())), preferred_element_type=jnp.float32)


def on_device(acts, grads_out, grad):
    block = acts.shape[1]
    tokens_all = acts.shape[0] * lax.axis_size("dp")
    identity = jnp.eye(block, dtype=jnp.float32)
    act_part = token_gram(acts)
    grouped = lax.all_to_all(
        lax.all_to_all(grads_out, "tensor", split_axis=0, concat_axis=1, tiled=True),
        "dp",
        split_axis=1,
        concat_axis=0,
        tiled=True,
    )
    grad_part = token_gram(grouped)
    act_cov = lax.psum(act_part, "dp")
    act_root = newton_root(
        act_cov / tokens_all + DAMPING * identity, identity, keep_both, keep_total
    )
    grad_cov = lax.psum(grad_part, "tensor")
    grad_root = newton_root(
        grad_cov / tokens_all + DAMPING * identity, identity, keep_both, keep_total
    )
    left_side = jnp.dot(act_root, grad, preferred_element_type=jnp.float32).astype(jnp.bfloat16)
    return jnp.dot(left_side, grad_root, preferred_element_type=jnp.float32)


def solution(mesh):
    return jax.shard_map(
        on_device,
        mesh=mesh,
        in_specs=(P("dp", "tensor"), P("dp", "tensor"), P("tensor", "dp")),
        out_specs=P("tensor", "dp"),
        check_vma=False,
    )
```

profile of v0, /device:TPU:6, one launch (start us, length us, event | category | flops | bytes accessed | tf_op | source)
XLA Modules:
  0.0 777.2 jit_solution(9092142903497061518)
XLA Ops:
  7.4 0.0 copy-start
  7.4 36.2 %all_to_all.32 = bf16[8,16,4096]{2,1,0:T(8,128)(2,1)S(1)} all-to-all(bf16[8,16,4096]{2,1,0:T(8,128)(2,1)} %bitcast.25), channel_id=1, replica_groups=mesh['dp'=64,'tensor'=8] {'tensor'}, dimensions={0} | all-to-all | bytes 2097152 | tf_op jit(solution)/shard_map/all_to_all | solution.py:49
  43.6 0.6 copy.6
  44.2 0.5 all_to_all.27
  44.7 1.5 copy.7
  46.3 14.8 %all-to-all-start.1 = ((bf16[16,64,512]{2,0,1:T(8,128)(2,1)}), bf16[16,64,512]{2,0,1:T(8,128)(2,1)S(1)}, u32[]{:S(2)}, u32[]{:S(2)}) async-start(bf16[16,64,512]{2,0,1:T(8,128)(2,1)} %copy.7), calls=%async_computation.1 | async-start | bytes 2097152 | tf_op jit(solution)/shard_map/all_to_all | solution.py:48
  61.1 0.0 all-reduce.3.cloned.1.call-start
  61.1 0.0 copy-done.4
  61.2 1.3 fusion.26
  62.5 0.0 all-reduce.3.cloned.1.call-update
  62.5 0.2 all-reduce.5.cloned.1.call-start
  62.8 587.6 %all-reduce.3.cloned.1.call-done = f32[512,512]{1,0:T(8,128)} async-done(((f32[512,512]{1,0:T(8,128)}), f32[512,512]{1,0:T(8,128)}) %all-reduce.3.cloned.1.call-update) | async-done | bytes 1048592 | tf_op jit(solution)/shard_map/psum | solution.py:56
  650.3 2.2 multiply_reduce_fusion.1
  653.2 0.0 copy-done.1
  653.3 2.2 select_subtract_fusion.3
  655.4 0.0 all-to-all-done.1
  655.4 1.7 convolution_bitcast_fusion
  657.2 0.0 all-reduce.5.cloned.1.call-update
  657.2 1.2 copy-done.3
  658.4 1.0 fusion.5
  659.4 1.9 fusion.11
  661.3 1.8 select_subtract_fusion.2
  663.1 1.9 fusion
  665.0 92.1 %all-reduce.5.cloned.1.call-done = f32[512,512]{1,0:T(8,128)} async-done(((f32[512,512]{1,0:T(8,128)}), f32[512,512]{1,0:T(8,128)}) %all-reduce.5.cloned.1.call-update) | async-done | bytes 1048592 | tf_op jit(solution)/shard_map/psum | solution.py:60
  757.1 2.2 multiply_reduce_fusion
  760.0 1.1 select_subtract_fusion.1
  761.2 1.0 fusion.4
  762.2 2.2 fusion.8
  764.3 1.8 select_subtract_fusion
  766.2 1.9 fusion.1
  768.0 0.0 copy-done
  768.1 1.7 fusion.2
  (5 shorter events, 0.0 us)
Async XLA Ops:
  7.4 760.7 %copy-start = (bf16[512,512]{1,0:T(8,128)(2,1)S(1)}, bf16[512,512]{1,0:T(8,128)(2,1)}, u32[]{:S(2)}) copy-start(bf16[512,512]{1,0:T(8,128)(2,1)} %param.5) | copy-start | bytes 1572868
  46.3 14.9 %copy-start.4 = (bf16[128,512]{1,0:T(8,128)(2,1)S(1)}, bf16[128,512]{1,0:T(8,128)(2,1)}, u32[]{:S(2)}) copy-start(bf16[128,512]{1,0:T(8,128)(2,1)} %param.3) | copy-start | bytes 393220
  46.3 609.2 %all-to-all-start.1 = ((bf16[16,64,512]{2,0,1:T(8,128)(2,1)}), bf16[16,64,512]{2,0,1:T(8,128)(2,1)S(1)}, u32[]{:S(2)}, u32[]{:S(2)}) async-start(bf16[16,64,512]{2,0,1:T(8,128)(2,1)} %copy.7), calls=%async_computation.1 | async-start | bytes 2097152 | tf_op jit(solution)/shard_map/all_to_all | solution.py:48
  61.1 589.2 %all-reduce.3.cloned.1.call-start = ((), (), s32[]{:S(2)}) async-start(), calls=%async_computation.2 | async-start | bytes 2097152 | tf_op jit(solution)/shard_map/psum | solution.py:56
  62.5 694.6 %all-reduce.5.cloned.1.call-start = ((), (), s32[]{:S(2)}) async-start(), calls=%async_computation.3 | async-start | bytes 2097152 | tf_op jit(solution)/shard_map/psum | solution.py:60
  650.3 2.9 copy-start.1
  657.1 1.2 copy-start.3
  757.1 2.9 copy-start.2
Sparse Core Ops, SparseCore 0:
  64.8 585.4 all-reduce.2
Sparse Core Ops, SparseCore 1:
  657.3 99.8 all-reduce.4
where the time goes:
time: 778 us; the launch traced here: 777 us
  waiting for transfers between devices  680 us (87%)
  blocking collectives  36.2 us (5%)
  matrix products  21.5 us (3%)
  between operations  16.4 us (2%)
  starting transfers between devices  15.1 us (2%)
    psum x1, waiting for transfers between devices, on_device(): act_cov = lax.psum(act_part, 'dp')  588 us
    psum x1, waiting for transfers between devices, on_device(): grad_cov = lax.psum(grad_part, 'tensor')  92.1 us
    all_to_all x1, blocking collectives, on_device(): lax.all_to_all(grads_out, 'tensor', split_axis=0, concat_axis=1, tiled=True)  36.2 us
  transfers between devices with their start and end apart: 3, of which 2 were waited for; matrix products, arithmetic and copies ran while one was open for 2% of the time, Pallas kernels for 0%

commit v1 on v0

v1 whole, which is shorter than its diff:
```python
import jax
import jax.numpy as jnp
import numpy as np
from jax import lax
from jax.experimental import pallas as pl
from jax.experimental.pallas import tpu as pltpu
from jax.sharding import Mesh, PartitionSpec as P

TOKENS = 8192
DAMPING = 0.1
BLOCK = 512
TILE = 128
SIDE = BLOCK // TILE
TILES = [(a, b) for a in range(SIDE) for b in range(a, SIDE)]
PACKED = len(TILES) * TILE
PEERS = 8
SHARE = PACKED // PEERS
PIECE = 24
RAW = SIDE * TILE
FIRST = RAW + 2 * SHARE
SECOND = SHARE + PIECE
BF16, F32 = jnp.bfloat16, jnp.float32
AXES = ("x", "yl", "z", "yh", "c")
SIZES = (4, 2, 8, 4, 2)
VMEM = pl.BlockSpec(memory_space=pltpu.VMEM)
PARAMS = pltpu.CompilerParams(vmem_limit_bytes=24 * 1024 * 1024)


def gram(data):
    return lax.dot_general(data, data, (((0,), (0,)), ((), ())), preferred_element_type=F32)


def store_packed(total, store):
    for place, (a, b) in enumerate(TILES):
        store(place * TILE, total[a * TILE : (a + 1) * TILE, b * TILE : (b + 1) * TILE])


def unpack(packed, full):
    for place, (a, b) in enumerate(TILES):
        tile = packed(place * TILE)
        full[a * TILE : (a + 1) * TILE, b * TILE : (b + 1) * TILE] = tile
        if a != b:
            full[b * TILE : (b + 1) * TILE, a * TILE : (a + 1) * TILE] = tile.T


def halves(values):
    high = values.astype(BF16)
    return high, (values - high.astype(F32)).astype(BF16)


def product(left, right):
    left_high, left_low = left
    right_high, right_low = right
    dot = lambda p, q: jnp.dot(p, q, preferred_element_type=F32)
    return dot(left_high, right_high) + (dot(left_high, right_low) + dot(left_low, right_high))


def inverse_root(covariance):
    rows = lax.broadcasted_iota(jnp.int32, (BLOCK, BLOCK), 0)
    columns = lax.broadcasted_iota(jnp.int32, (BLOCK, BLOCK), 1)
    diagonal = rows == columns
    shifted = covariance * (1.0 / TOKENS) + jnp.where(diagonal, DAMPING, 0.0)
    squares = jnp.sum(jnp.sum(shifted * shifted, axis=0, keepdims=True), axis=1, keepdims=True)
    frob = jnp.sqrt(squares)
    y = shifted * (1.0 / frob)
    y_halves = halves(y)
    s = product(y_halves, y_halves)
    tail = product(halves(s), halves(0.0625 * s - 0.5625 * y))
    z = jnp.where(diagonal, 2.25, 0.0) - 2.4375 * y + 1.6875 * s + tail
    return (z * (1.0 / jnp.sqrt(frob))).astype(BF16)


def first_kernel(acts, grads, out, packed):
    def keep(row, tile):
        packed[row : row + TILE, :] = tile

    store_packed(gram(acts[...]), keep)
    for peer in range(PEERS):
        for part in range(SIDE):
            column = peer * BLOCK + part * TILE
            out[peer, part * TILE : (part + 1) * TILE, :] = grads[:, column : column + TILE]
        high, low = halves(packed[peer * SHARE : (peer + 1) * SHARE, :])
        out[peer, RAW : RAW + SHARE, :] = high
        out[peer, RAW + SHARE : FIRST, :] = low


def second_kernel(got, out, packed, share):
    tokens = jnp.concatenate(
        [got[:, p * TILE : (p + 1) * TILE, :].reshape(PEERS * TILE, TILE) for p in range(SIDE)],
        axis=1,
    )

    def keep(row, tile):
        packed[row : row + TILE, :] = tile

    store_packed(gram(tokens), keep)
    total = jnp.zeros((SHARE, TILE), F32)
    for peer in range(PEERS):
        high = got[peer, RAW : RAW + SHARE, :].astype(F32)
        total += high + got[peer, RAW + SHARE : FIRST, :].astype(F32)
    share[0:SHARE, :] = total
    share[SHARE:, :] = jnp.zeros((PEERS * PIECE - SHARE, TILE), F32)
    for peer in range(PEERS):
        out[peer, 0:SHARE, :] = packed[peer * SHARE : (peer + 1) * SHARE, :]
        out[peer, SHARE:SECOND, :] = share[peer * PIECE : (peer + 1) * PIECE, :]


def sum_kernel(got, out):
    total = got[0]
    for peer in range(1, PEERS):
        total += got[peer]
    for peer in range(PEERS):
        out[peer] = total


def root_kernel(got, root, out, packed, share, full):
    for peer in range(PEERS):
        packed[peer * SHARE : (peer + 1) * SHARE, :] = got[peer, 0:SHARE, :]
        share[peer * PIECE : (peer + 1) * PIECE, :] = got[peer, SHARE:SECOND, :]
    unpack(lambda row: packed[row : row + TILE, :], full)
    root[...] = inverse_root(full[...])
    for peer in range(PEERS):
        out[peer] = share[0:SHARE, :]


def last_kernel(got, grad, grad_root, out, full):
    unpack(lambda row: got[row : row + TILE, :], full)
    act_root = inverse_root(full[...])
    left = jnp.dot(act_root, grad[...], preferred_element_type=F32).astype(BF16)
    out[...] = jnp.dot(left, grad_root[...], preferred_element_type=F32)


def call(kernel, count, outs, scratch, flops):
    return pl.pallas_call(
        kernel,
        out_shape=outs,
        in_specs=[VMEM] * count,
        out_specs=[VMEM] * len(outs),
        scratch_shapes=scratch,
        compiler_params=PARAMS,
        cost_estimate=pl.CostEstimate(flops=flops, bytes_accessed=4 << 20, transcendentals=0),
    )


def shape(dims, dtype):
    return jax.ShapeDtypeStruct(dims, dtype)


def exchange(data, axes):
    return lax.all_to_all(data, axes, split_axis=0, concat_axis=0, tiled=True)


def transposition():
    places = np.arange(np.prod(SIZES)).reshape(SIZES)
    return [
        (int(places[x, yl, z, yh, c]), int(places[yh, c, z, x, yl]))
        for x, yl, z, yh, c in np.ndindex(*SIZES)
    ]


def on_device(acts, grads_out, grad):
    cube = 2 * BLOCK**3
    packed = pltpu.VMEM((PACKED, TILE), F32)
    share = pltpu.VMEM((PEERS * PIECE, TILE), F32)
    full = pltpu.VMEM((BLOCK, BLOCK), F32)
    (sent,) = call(first_kernel, 2, [shape((PEERS, FIRST, TILE), BF16)], [packed], cube // 4)(
        acts, grads_out
    )
    got = exchange(sent, "z")
    (sent,) = call(second_kernel, 1, [shape((PEERS, SECOND, TILE), F32)], [packed, share], 2 * cube)(
        got
    )
    got = exchange(sent, ("x", "yl"))
    (sent,) = call(sum_kernel, 1, [shape((PEERS, SECOND, TILE), F32)], [], 1 << 20)(got)
    got = exchange(sent, ("x", "yl"))
    root, sent = call(
        root_kernel,
        1,
        [shape((BLOCK, BLOCK), BF16), shape((PEERS, SHARE, TILE), F32)],
        [packed, share, full],
        6 * cube,
    )(got)
    grad_root = lax.ppermute(root, AXES, transposition())
    got = exchange(sent, "z")
    (out,) = call(last_kernel, 3, [shape((BLOCK, BLOCK), F32)], [full], 8 * cube)(
        got.reshape(PACKED, TILE), grad, grad_root
    )
    return out


def solution(mesh):
    split = Mesh(mesh.devices.reshape(SIZES), AXES)
    dp, tensor = AXES[:3], AXES[3:]
    return jax.shard_map(
        on_device,
        mesh=split,
        in_specs=(P(dp, tensor), P(dp, tensor), P(tensor, dp)),
        out_specs=P(tensor, dp),
        check_vma=False,
    )
```

time: 778 us -> 136 us (0.17)
  the two profiles are of different devices: /device:TPU:6 before, /device:TPU:48 now
where the time goes in v1:
time: 136 us; the launch traced here: 135 us
  blocking collectives  80.8 us (59%)
  waiting for transfers between devices  37 us (27%)
  Pallas kernels  8.11 us (6%)
  starting transfers between devices  7.27 us (5%)
  local copies, waits for them, and re-layouts  2.13 us (2%)
    all_to_all x3, blocking collectives, exchange(): return lax.all_to_all(data, axes, split_axis=0, concat_axis=0, tiled=True)  80.8 us
    ppermute x1, waiting for transfers between devices, on_device(): grad_root = lax.ppermute(root, AXES, transposition())  37 us
    all_to_all x1, starting transfers between devices, exchange(): return lax.all_to_all(data, axes, split_axis=0, concat_axis=0, tiled=True)  4.33 us
    pallas_call x1, Pallas kernels, on_device(): call(last_kernel, 3, [shape((BLOCK, BLOCK), F32)], [full], 8 * cube)  3.77 us
    pallas_call x1, Pallas kernels, on_device(): call(root_kernel, 1, [shape((BLOCK, BLOCK), BF16), shape((PEERS, SHARE, T...  3.09 us
    ppermute x1, starting transfers between devices, on_device(): grad_root = lax.ppermute(root, AXES, transposition())  2.95 us
  transfers between devices with their start and end apart: 2, of which 1 were waited for; matrix products, arithmetic and copies ran while one was open for 0% of the time, Pallas kernels for 0%

profile of v1, /device:TPU:48, one launch (start us, length us, event | category | flops | bytes accessed | tf_op | source)
XLA Modules:
  0.0 135.4 jit_solution(3300235382030749077)
XLA Ops:
  0.0 0.0 copy-start
  0.0 1.2 copy-done
  1.2 0.0 copy-start.1
  1.2 0.9 copy-done.1
  2.1 0.4 shard_map.37
  2.6 52.9 %all_to_all.20.got = bf16[8,832,128]{2,1,0:T(8,128)(2,1)S(1)} all-to-all(bf16[8,832,128]{2,1,0:T(8,128)(2,1)S(1)} %shard_map.37), channel_id=1, replica_groups=mesh['x'=4,'yl'=2,'z'=8,'yh'=4,'c'=2] {'z'}, dimensions={0} | all-to-all | bytes 3407872 | tf_op jit(solution)/shard_map/all_to_all | solution.py:150
  55.5 0.8 shard_map.38
  56.2 15.3 %all_to_all.21.got = f32[8,184,128]{2,1,0:T(8,128)S(1)} all-to-all(f32[8,184,128]{2,1,0:T(8,128)S(1)} %shard_map.38), channel_id=1, replica_groups=mesh['x'=4,'yl'=2,'z'=8,'yh'=4,'c'=2] {'x','yl'}, dimensions={0} | all-to-all | bytes 1507328 | tf_op jit(solution)/shard_map/all_to_all | solution.py:150
  71.6 0.1 shard_map.39
  71.6 12.6 %all_to_all.22.got = f32[8,184,128]{2,1,0:T(8,128)S(1)} all-to-all(f32[8,184,128]{2,1,0:T(8,128)S(1)} %shard_map.39), channel_id=1, replica_groups=mesh['x'=4,'yl'=2,'z'=8,'yh'=4,'c'=2] {'x','yl'}, dimensions={0} | all-to-all | bytes 1507328 | tf_op jit(solution)/shard_map/all_to_all | solution.py:150
  84.2 0.0 copy-start.2
  84.2 3.1 %shard_map.40 = (bf16[512,512]{1,0:T(8,128)(2,1)S(1)}, f32[8,160,128]{2,1,0:T(8,128)}) custom-call(f32[8,184,128]{2,1,0:T(8,128)S(1)} %all_to_all.22.got), custom_call_target="tpu_custom_call" | custom-call | flops 1610612736 | bytes 4194304 | tf_op jit(solution)/shard_map/pallas_call | solution.py:176
  87.3 4.3 %all-to-all-start.3 = ((f32[8,160,128]{2,1,0:T(8,128)}), f32[8,160,128]{2,1,0:T(8,128)S(1)}, u32[]{:S(2)}, u32[]{:S(2)}) async-start(f32[8,160,128]{2,1,0:T(8,128)} %get-tuple-element.7), calls=%async_computation.3 | async-start | bytes 1310720 | tf_op jit(solution)/shard_map/all_to_all | solution.py:150
  91.7 2.9 %collective-permute-start = (bf16[512,512]{1,0:T(8,128)(2,1)S(1)}, bf16[512,512]{1,0:T(8,128)(2,1)S(1)}, u32[]{:S(2)}, u32[]{:S(2)}) collective-permute-start(bf16[512,512]{1,0:T(8,128)(2,1)S(1)} %get-tuple-element.8), channel_id=1, source_target_pairs={{0,0},{1,64},{2,128},{3,192},{4,256},{5,320},{6,384},{7,448},{8,8}... | collective-permute-start | bytes 1572872 | tf_op jit(solution)/shard_map/ppermute | solution.py:183
  94.6 37.0 %collective-permute-done.grad_root = bf16[512,512]{1,0:T(8,128)(2,1)S(1)} collective-permute-done((bf16[512,512]{1,0:T(8,128)(2,1)S(1)}, bf16[512,512]{1,0:T(8,128)(2,1)S(1)}, u32[]{:S(2)}, u32[]{:S(2)}) %collective-permute-start) | collective-permute-done | bytes 524320 | tf_op jit(solution)/shard_map/ppermute | solution.py:183
  131.6 0.0 all-to-all-done.3
  131.6 0.0 copy-done.2
  131.6 3.8 %shard_map.41 = f32[512,512]{1,0:T(8,128)} custom-call(f32[1280,128]{1,0:T(8,128)S(1)} %bitcast.1, bf16[512,512]{1,0:T(8,128)(2,1)S(1)} %copy-done.2, bf16[512,512]{1,0:T(8,128)(2,1)S(1)} %collective-permute-done.grad_root), custom_call_target="tpu_custom_call" | custom-call | flops 2147483648 | bytes 4194304 | tf_op jit(solution)/shard_map/pallas_call | solution.py:185
Async XLA Ops:
  0.0 1.2 copy-start
  1.2 0.9 copy-start.1
  84.2 47.4 %copy-start.2 = (bf16[512,512]{1,0:T(8,128)(2,1)S(1)}, bf16[512,512]{1,0:T(8,128)(2,1)}, u32[]{:S(2)}) copy-start(bf16[512,512]{1,0:T(8,128)(2,1)} %grad.1) | copy-start | bytes 1572868
  87.3 44.3 %all-to-all-start.3 = ((f32[8,160,128]{2,1,0:T(8,128)}), f32[8,160,128]{2,1,0:T(8,128)S(1)}, u32[]{:S(2)}, u32[]{:S(2)}) async-start(f32[8,160,128]{2,1,0:T(8,128)} %get-tuple-element.7), calls=%async_computation.3 | async-start | bytes 1310720 | tf_op jit(solution)/shard_map/all_to_all | solution.py:150
  91.7 39.9 %collective-permute-start = (bf16[512,512]{1,0:T(8,128)(2,1)S(1)}, bf16[512,512]{1,0:T(8,128)(2,1)S(1)}, u32[]{:S(2)}, u32[]{:S(2)}) collective-permute-start(bf16[512,512]{1,0:T(8,128)(2,1)S(1)} %get-tuple-element.8), channel_id=1, source_target_pairs={{0,0},{1,64},{2,128},{3,192},{4,256},{5,320},{6,384},{7,448},{8,8}... | collective-permute-start | bytes 1572872 | tf_op jit(solution)/shard_map/ppermute | solution.py:183

commit v2 on v1

v2 whole, which is shorter than its diff:
```python
import functools

import jax
import jax.numpy as jnp
import numpy as np
from jax import lax
from jax.experimental import pallas as pl
from jax.experimental.pallas import tpu as pltpu
from jax.sharding import Mesh, PartitionSpec as P

TOKENS = 8192
DAMPING = 0.1
BLOCK = 512
TILE = 128
SIDE = BLOCK // TILE
TILES = [(a, b) for a in range(SIDE) for b in range(a, SIDE)]
PACKED = len(TILES) * TILE
HALF = PACKED // 2
PEERS = 8
SHARE = PACKED // PEERS
BF16, F32 = jnp.bfloat16, jnp.float32
AXES = ("x", "yl", "z", "yh", "c")
SIZES = (4, 2, 8, 4, 2)
VMEM = pl.BlockSpec(memory_space=pltpu.VMEM)
ANYWHERE = pl.BlockSpec(memory_space=pl.ANY)
PARAMS = pltpu.CompilerParams(vmem_limit_bytes=24 * 1024 * 1024)


def gram(data):
    return lax.dot_general(data, data, (((0,), (0,)), ((), ())), preferred_element_type=F32)


def pack(total, packed):
    for place, (a, b) in enumerate(TILES):
        tile = total[a * TILE : (a + 1) * TILE, b * TILE : (b + 1) * TILE]
        packed[place * TILE : (place + 1) * TILE, :] = tile


def unpack(packed, full):
    for place, (a, b) in enumerate(TILES):
        tile = packed[place * TILE : (place + 1) * TILE, :]
        full[a * TILE : (a + 1) * TILE, b * TILE : (b + 1) * TILE] = tile
        if a != b:
            full[b * TILE : (b + 1) * TILE, a * TILE : (a + 1) * TILE] = tile.T


def rows(bit, count):
    return pl.ds(pl.multiple_of(bit * count, count), count)


def halves(values):
    high = values.astype(BF16)
    return high, (values - high.astype(F32)).astype(BF16)


def product(left, right):
    left_high, left_low = left
    right_high, right_low = right
    dot = lambda p, q: jnp.dot(p, q, preferred_element_type=F32)
    return dot(left_high, right_high) + (dot(left_high, right_low) + dot(left_low, right_high))


def inverse_root(covariance):
    row = lax.broadcasted_iota(jnp.int32, (BLOCK, BLOCK), 0)
    column = lax.broadcasted_iota(jnp.int32, (BLOCK, BLOCK), 1)
    diagonal = row == column
    shifted = covariance * (1.0 / TOKENS) + jnp.where(diagonal, DAMPING, 0.0)
    squares = jnp.sum(jnp.sum(shifted * shifted, axis=0, keepdims=True), axis=1, keepdims=True)
    frob = jnp.sqrt(squares)
    y = shifted * (1.0 / frob)
    y_halves = halves(y)
    s = product(y_halves, y_halves)
    tail = product(halves(s), halves(0.0625 * s - 0.5625 * y))
    z = jnp.where(diagonal, 2.25, 0.0) - 2.4375 * y + 1.6875 * s + tail
    return (z * (1.0 / jnp.sqrt(frob))).astype(BF16)


def split_kernel(grads, out):
    for peer in range(PEERS):
        out[peer] = grads[:, peer * BLOCK : (peer + 1) * BLOCK]


def act_gram_kernel(acts, keep, send, packed):
    pack(gram(acts[...]), packed)
    bit = lax.axis_index("yl")
    keep[...] = packed[rows(bit, HALF), :]
    send[...] = packed[rows(1 - bit, HALF), :]


def halve_kernel(digit, kept, got, keep, send):
    bit = lax.rem(lax.axis_index("x") // digit, 2)
    count = keep.shape[0]
    keep[...] = kept[rows(bit, count), :] + got[rows(bit, count), :]
    send[...] = kept[rows(1 - bit, count), :] + got[rows(1 - bit, count), :]


def add_kernel(kept, got, out):
    out[...] = kept[...] + got[...]


def copies_kernel(kept, got, out):
    total = kept[...] + got[...]
    for peer in range(PEERS):
        out[peer] = total


def grad_gram_kernel(got, out):
    pack(gram(got[...].reshape(PEERS * TILE, BLOCK)), out)


def sum_kernel(got, out):
    total = got[0]
    for peer in range(1, PEERS):
        total += got[peer]
    for peer in range(PEERS):
        out[peer] = total


def grad_root_kernel(got, out, full, packed):
    unpack(got, full)
    pack(inverse_root(full[...]), packed)
    out[...] = packed[rows(lax.axis_index("yl"), HALF), :]


def left_kernel(got, grad, out, packed, full):
    for x, yl in np.ndindex(4, 2):
        start = (yl * 4 + x) * SHARE
        packed[start : start + SHARE, :] = got[x * 2 + yl]
    unpack(packed, full)
    root = inverse_root(full[...])
    out[...] = jnp.dot(root, grad[...], preferred_element_type=F32).astype(BF16)


def last_kernel(left, mine, other, out, packed, full):
    bit = lax.axis_index("c")
    packed[rows(bit, HALF), :] = mine[...]
    packed[rows(1 - bit, HALF), :] = other[...]
    unpack(packed, full)
    out[...] = jnp.dot(left[...], full[...], preferred_element_type=F32)


def call(kernel, args, outs, scratch=(), flops=1 << 20, after=()):
    outs = [jax.ShapeDtypeStruct(dims, dtype) for dims, dtype in outs]
    data = sum(a.size * a.dtype.itemsize for a in [*args, *outs])

    def body(*refs):
        kernel(*refs[: len(args)], *refs[len(args) + len(after) :])

    got = pl.pallas_call(
        body,
        out_shape=outs,
        in_specs=[VMEM] * len(args) + [ANYWHERE] * len(after),
        out_specs=[VMEM] * len(outs),
        scratch_shapes=[pltpu.VMEM(dims, dtype) for dims, dtype in scratch],
        compiler_params=PARAMS,
        cost_estimate=pl.CostEstimate(flops=flops, bytes_accessed=data, transcendentals=0),
    )(*args, *after)
    return got if len(outs) > 1 else got[0]


def exchange(data, axes):
    return lax.all_to_all(data, axes, split_axis=0, concat_axis=0, tiled=True)


def swap(data, axis, size, distance):
    return lax.ppermute(data, axis, [(i, i ^ distance) for i in range(size)])


def transpose_places(data):
    places = np.arange(np.prod(SIZES)).reshape(SIZES)
    pairs = [
        (int(places[x, yl, z, yh, c]), int(places[yh, c, z, (x + yh) % 4, yl]))
        for x, yl, z, yh, c in np.ndindex(*SIZES)
    ]
    return lax.ppermute(data, AXES, pairs)


def on_device(acts, grads_out, grad):
    cube = 2 * BLOCK**3
    packed, full = (PACKED, TILE), (BLOCK, BLOCK)
    copies = (PEERS, SHARE, TILE)

    split = call(split_kernel, [grads_out], [((PEERS, TILE, BLOCK), BF16)])
    tokens = exchange(split, "z")

    half = [((HALF, TILE), F32)] * 2
    keep, send = call(act_gram_kernel, [acts], half, [(packed, F32)], cube // 4, [split])
    got = swap(send, "yl", 2, 1)
    quarter = [((HALF // 2, TILE), F32)] * 2
    keep, send = call(functools.partial(halve_kernel, 2), [keep, got], quarter)
    got = swap(send, "x", 4, 2)
    eighth = [((SHARE, TILE), F32)] * 2
    keep, send = call(functools.partial(halve_kernel, 1), [keep, got], eighth)
    got = swap(send, "x", 4, 1)
    share_xy = call(add_kernel, [keep, got], eighth[:1])
    part = call(grad_gram_kernel, [tokens], [(packed, F32)], (), 2 * cube, [share_xy])

    got = swap(share_xy, "z", 8, 1)
    share = call(add_kernel, [share_xy, got], eighth[:1], after=[part])
    got = swap(share, "z", 8, 2)
    share_z = call(add_kernel, [share, got], eighth[:1])
    parts = exchange(part.reshape(copies), ("x", "yl"))
    sent = call(sum_kernel, [parts], [(copies, F32)], after=[share_z])

    got = swap(share_z, "z", 8, 4)
    act_sent = call(copies_kernel, [share_z, got], [(copies, F32)], after=[sent])
    grad_cov = exchange(sent, ("x", "yl")).reshape(packed)
    root = call(
        grad_root_kernel,
        [grad_cov],
        [((HALF, TILE), BF16)],
        [(full, F32), (packed, BF16)],
        6 * cube,
        [act_sent],
    )
    mine = transpose_places(root)

    act_cov = exchange(act_sent, ("x", "yl"))
    left = call(
        left_kernel, [act_cov, grad], [(full, BF16)], [(packed, F32), (full, F32)], 7 * cube
    )
    other = swap(mine, "c", 2, 1)
    return call(
        last_kernel, [left, mine, other], [(full, F32)], [(packed, BF16), (full, BF16)], cube
    )


def solution(mesh):
    split = Mesh(mesh.devices.reshape(SIZES), AXES)
    dp, tensor = AXES[:3], AXES[3:]
    return jax.shard_map(
        on_device,
        mesh=split,
        in_specs=(P(dp, tensor), P(dp, tensor), P(tensor, dp)),
        out_specs=P(tensor, dp),
        check_vma=False,
    )
```

time: 136 us -> 112 us (0.82)
  the two profiles are of different devices: /device:TPU:48 before, /device:TPU:6 now
where the time goes in v2:
time: 112 us; the launch traced here: 111 us
  starting transfers between devices  54.1 us (48%)
  waiting for transfers between devices  44.1 us (39%)
  Pallas kernels  11.2 us (10%)
  local copies, waits for them, and re-layouts  1.23 us (1%)
    ppermute x7, waiting for transfers between devices, swap(): return lax.ppermute(data, axis, [(i, i ^ distance) for i in range(size)])  31.7 us
    all_to_all x4, starting transfers between devices, exchange(): return lax.all_to_all(data, axes, split_axis=0, concat_axis=0, tiled=True)  27.6 us
    ppermute x7, starting transfers between devices, swap(): return lax.ppermute(data, axis, [(i, i ^ distance) for i in range(size)])  21.8 us
    pallas_call x13, Pallas kernels, call(): pl.pallas_call(body, out_shape=outs, in_specs=[VMEM] * len(args) + [ANYWH...  11.2 us
    ppermute x1, waiting for transfers between devices, transpose_places(): return lax.ppermute(data, AXES, pairs)  10.3 us
    ppermute x1, starting transfers between devices, transpose_places(): return lax.ppermute(data, AXES, pairs)  4.71 us
  transfers between devices with their start and end apart: 12, of which 8 were waited for; matrix products, arithmetic and copies ran while one was open for 0% of the time, Pallas kernels for 6%

profile of v2, /device:TPU:6, one launch (start us, length us, event | category | flops | bytes accessed | tf_op | source)
XLA Modules:
  0.0 110.8 jit_solution(314046687126854941)
XLA Ops:
  0.0 1.2 %copy-done = bf16[128,4096]{1,0:T(8,128)(2,1)S(1)} copy-done((bf16[128,4096]{1,0:T(8,128)(2,1)S(1)}, bf16[128,4096]{1,0:T(8,128)(2,1)}, u32[]{:S(2)}) %copy-start) | copy-done | bytes 1048600
  1.2 1.0 shard_map.37.refs_1_
  2.3 10.4 %all-to-all-start = ((bf16[8,128,512]{2,1,0:T(8,128)(2,1)}), bf16[8,128,512]{2,1,0:T(8,128)(2,1)S(1)}, u32[]{:S(2)}, u32[]{:S(2)}) async-start(bf16[8,128,512]{2,1,0:T(8,128)(2,1)} %shard_map.37.refs_1_), calls=%async_computation | async-start | bytes 2097152 | tf_op jit(solution)/shard_map/all_to_all | solution.py:162
  12.7 0.4 shard_map.38
  13.1 3.5 %collective-permute-start = (f32[640,128]{1,0:T(8,128)S(1)}, f32[640,128]{1,0:T(8,128)S(1)}, u32[]{:S(2)}, u32[]{:S(2)}) collective-permute-start(f32[640,128]{1,0:T(8,128)S(1)} %get-tuple-element.12), channel_id=1, source_target_pairs={{0,64},{64,0},{1,65},{65,1},{2,66},{66,2},{3,67},{67,3},{4,68},{68... | collective-permute-start | bytes 983048 | tf_op jit(solution)/shard_map/ppermute | solution.py:166
  16.6 7.6 %collective-permute-done.refs_1_ = f32[640,128]{1,0:T(8,128)S(1)} collective-permute-done((f32[640,128]{1,0:T(8,128)S(1)}, f32[640,128]{1,0:T(8,128)S(1)}, u32[]{:S(2)}, u32[]{:S(2)}) %collective-permute-start) | collective-permute-done | bytes 327712 | tf_op jit(solution)/shard_map/ppermute | solution.py:166
  24.2 3.3 %collective-permute-start.1 = (f32[320,128]{1,0:T(8,128)S(1)}, f32[320,128]{1,0:T(8,128)S(1)}, u32[]{:S(2)}, u32[]{:S(2)}) collective-permute-start(f32[320,128]{1,0:T(8,128)S(1)} %get-tuple-element.14), channel_id=1, source_target_pairs={{0,256},{128,384},{256,0},{384,128},{1,257},{129,385},{257,1},{385... | collective-permute-start | bytes 491528 | tf_op jit(solution)/shard_map/ppermute | solution.py:166
  27.6 5.4 %collective-permute-done.1.refs_1_ = f32[320,128]{1,0:T(8,128)S(1)} collective-permute-done((f32[320,128]{1,0:T(8,128)S(1)}, f32[320,128]{1,0:T(8,128)S(1)}, u32[]{:S(2)}, u32[]{:S(2)}) %collective-permute-start.1) | collective-permute-done | bytes 163872 | tf_op jit(solution)/shard_map/ppermute | solution.py:166
  33.0 2.7 %collective-permute-start.2 = (f32[160,128]{1,0:T(8,128)S(1)}, f32[160,128]{1,0:T(8,128)S(1)}, u32[]{:S(2)}, u32[]{:S(2)}) collective-permute-start(f32[160,128]{1,0:T(8,128)S(1)} %get-tuple-element.16), channel_id=1, source_target_pairs={{0,128},{128,0},{256,384},{384,256},{1,129},{129,1},{257,385},{385... | collective-permute-start | bytes 245768 | tf_op jit(solution)/shard_map/ppermute | solution.py:166
  35.7 3.6 %collective-permute-done.2.refs_1_ = f32[160,128]{1,0:T(8,128)S(1)} collective-permute-done((f32[160,128]{1,0:T(8,128)S(1)}, f32[160,128]{1,0:T(8,128)S(1)}, u32[]{:S(2)}, u32[]{:S(2)}) %collective-permute-start.2) | collective-permute-done | bytes 81952 | tf_op jit(solution)/shard_map/ppermute | solution.py:166
  39.3 2.1 %all-to-all-done.refs_0_ = bf16[8,128,512]{2,1,0:T(8,128)(2,1)S(1)} async-done(((bf16[8,128,512]{2,1,0:T(8,128)(2,1)}), bf16[8,128,512]{2,1,0:T(8,128)(2,1)S(1)}, u32[]{:S(2)}, u32[]{:S(2)}) %all-to-all-start) | async-done | bytes 1048608 | tf_op jit(solution)/shard_map/all_to_all | solution.py:162
  41.4 1.6 %shard_map.42.refs_2_ = f32[1280,128]{1,0:T(8,128)} custom-call(bf16[8,128,512]{2,1,0:T(8,128)(2,1)S(1)} %all-to-all-done.refs_0_, f32[160,128]{1,0:T(8,128)S(1)} %shard_map.41.refs_1_.refs_0_), custom_call_target="tpu_custom_call" | custom-call | flops 536870912 | bytes 1703936 | tf_op jit(solution)/shard_map/pallas_call | solution.py:149
  43.0 5.8 %all-to-all-start.1 = ((f32[8,160,128]{2,1,0:T(8,128)}), f32[8,160,128]{2,1,0:T(8,128)S(1)}, u32[]{:S(2)}, u32[]{:S(2)}) async-start(f32[8,160,128]{2,1,0:T(8,128)} %bitcast), calls=%async_computation.1 | async-start | bytes 1310720 | tf_op jit(solution)/shard_map/all_to_all | solution.py:162
  48.8 2.5 %collective-permute-start.3 = (f32[160,128]{1,0:T(8,128)S(1)}, f32[160,128]{1,0:T(8,128)S(1)}, u32[]{:S(2)}, u32[]{:S(2)}) collective-permute-start(f32[160,128]{1,0:T(8,128)S(1)} %shard_map.41.refs_1_.refs_0_), channel_id=1, source_target_pairs={{0,8},{8,0},{16,24},{24,16},{32,40},{40,32},{48,56},{56,48},{1,9},... | collective-permute-start | bytes 245768 | tf_op jit(solution)/shard_map/ppermute | solution.py:166
  51.3 3.9 %collective-permute-done.3.refs_1_ = f32[160,128]{1,0:T(8,128)S(1)} collective-permute-done((f32[160,128]{1,0:T(8,128)S(1)}, f32[160,128]{1,0:T(8,128)S(1)}, u32[]{:S(2)}, u32[]{:S(2)}) %collective-permute-start.3) | collective-permute-done | bytes 81952 | tf_op jit(solution)/shard_map/ppermute | solution.py:166
  55.1 2.4 %collective-permute-start.4 = (f32[160,128]{1,0:T(8,128)S(1)}, f32[160,128]{1,0:T(8,128)S(1)}, u32[]{:S(2)}, u32[]{:S(2)}) collective-permute-start(f32[160,128]{1,0:T(8,128)S(1)} %shard_map.43.refs_0_), channel_id=1, source_target_pairs={{0,16},{8,24},{16,0},{24,8},{32,48},{40,56},{48,32},{56,40},{1,17}... | collective-permute-start | bytes 245768 | tf_op jit(solution)/shard_map/ppermute | solution.py:166
  57.6 5.7 %collective-permute-done.4.refs_1_ = f32[160,128]{1,0:T(8,128)S(1)} collective-permute-done((f32[160,128]{1,0:T(8,128)S(1)}, f32[160,128]{1,0:T(8,128)S(1)}, u32[]{:S(2)}, u32[]{:S(2)}) %collective-permute-start.4) | collective-permute-done | bytes 81952 | tf_op jit(solution)/shard_map/ppermute | solution.py:166
  63.3 0.0 all-to-all-done.1.refs_0_
  63.3 0.9 shard_map.45.refs_2_
  64.2 5.7 %all-to-all-start.3 = ((f32[8,160,128]{2,1,0:T(8,128)}), f32[8,160,128]{2,1,0:T(8,128)S(1)}, u32[]{:S(2)}, u32[]{:S(2)}) async-start(f32[8,160,128]{2,1,0:T(8,128)} %shard_map.45.refs_2_), calls=%async_computation.3 | async-start | bytes 1310720 | tf_op jit(solution)/shard_map/all_to_all | solution.py:162
  69.9 5.4 %collective-permute-start.5 = (f32[160,128]{1,0:T(8,128)S(1)}, f32[160,128]{1,0:T(8,128)S(1)}, u32[]{:S(2)}, u32[]{:S(2)}) collective-permute-start(f32[160,128]{1,0:T(8,128)S(1)} %shard_map.44.refs_1_.refs_0_), channel_id=1, source_target_pairs={{0,32},{8,40},{16,48},{24,56},{32,0},{40,8},{48,16},{56,24},{1,33}... | collective-permute-start | bytes 245768 | tf_op jit(solution)/shard_map/ppermute | solution.py:166
  75.3 5.7 %collective-permute-done.5.refs_1_ = f32[160,128]{1,0:T(8,128)S(1)} collective-permute-done((f32[160,128]{1,0:T(8,128)S(1)}, f32[160,128]{1,0:T(8,128)S(1)}, u32[]{:S(2)}, u32[]{:S(2)}) %collective-permute-start.5) | collective-permute-done | bytes 81952 | tf_op jit(solution)/shard_map/ppermute | solution.py:166
  81.0 0.9 shard_map.46.refs_1_
  81.9 0.0 all-to-all-done.3
  81.9 5.7 %all-to-all-start.2 = ((f32[8,160,128]{2,1,0:T(8,128)}), f32[8,160,128]{2,1,0:T(8,128)S(1)}, u32[]{:S(2)}, u32[]{:S(2)}) async-start(f32[8,160,128]{2,1,0:T(8,128)} %shard_map.46.refs_1_), calls=%async_computation.2 | async-start | bytes 1310720 | tf_op jit(solution)/shard_map/all_to_all | solution.py:162
  87.6 2.3 %shard_map.48 = bf16[640,128]{1,0:T(8,128)(2,1)S(1)} custom-call(f32[1280,128]{1,0:T(8,128)S(1)} %bitcast.2, f32[8,160,128]{2,1,0:T(8,128)} %shard_map.46.refs_1_), custom_call_target="tpu_custom_call" | custom-call | flops 1610612736 | bytes 819200 | tf_op jit(solution)/shard_map/pallas_call | solution.py:149
  89.9 4.7 %collective-permute-start.6 = (bf16[640,128]{1,0:T(8,128)(2,1)S(1)}, bf16[640,128]{1,0:T(8,128)(2,1)S(1)}, u32[]{:S(2)}, u32[]{:S(2)}) collective-permute-start(bf16[640,128]{1,0:T(8,128)(2,1)S(1)} %shard_map.48), channel_id=1, source_target_pairs={{0,0},{1,64},{2,130},{3,194},{4,260},{5,324},{6,390},{7,454},{8,8}... | collective-permute-start | bytes 491528 | tf_op jit(solution)/shard_map/ppermute | solution.py:175
  94.6 10.3 %collective-permute-done.6.refs_1_ = bf16[640,128]{1,0:T(8,128)(2,1)S(1)} collective-permute-done((bf16[640,128]{1,0:T(8,128)(2,1)S(1)}, bf16[640,128]{1,0:T(8,128)(2,1)S(1)}, u32[]{:S(2)}, u32[]{:S(2)}) %collective-permute-start.6) | collective-permute-done | bytes 163872 | tf_op jit(solution)/shard_map/ppermute | solution.py:175
  104.8 1.9 %collective-permute-start.7 = (bf16[640,128]{1,0:T(8,128)(2,1)S(1)}, bf16[640,128]{1,0:T(8,128)(2,1)S(1)}, u32[]{:S(2)}, u32[]{:S(2)}) collective-permute-start(bf16[640,128]{1,0:T(8,128)(2,1)S(1)} %collective-permute-done.6.refs_1_), channel_id=1, source_target_pairs={{0,1},{1,0},{2,3},{3,2},{4,5},{5,4},{6,7},{7,6},{8,9},{9,8},{10,11... | collective-permute-start | bytes 491528 | tf_op jit(solution)/shard_map/ppermute | solution.py:166
  106.8 0.0 all-to-all-done.2.refs_0_
  106.8 2.5 %shard_map.47.refs_0_ = bf16[512,512]{1,0:T(8,128)(2,1)S(1)} custom-call(f32[8,160,128]{2,1,0:T(8,128)S(1)} %all-to-all-done.2.refs_0_, bf16[512,512]{1,0:T(8,128)(2,1)S(1)} %copy-done.2), custom_call_target="tpu_custom_call" | custom-call | flops 1879048192 | bytes 1703936 | tf_op jit(solution)/shard_map/pallas_call | solution.py:149
  109.3 1.5 %shard_map.49 = f32[512,512]{1,0:T(8,128)} custom-call(bf16[512,512]{1,0:T(8,128)(2,1)S(1)} %shard_map.47.refs_0_, bf16[640,128]{1,0:T(8,128)(2,1)S(1)} %collective-permute-done.6.refs_1_, bf16[640,128]{1,0:T(8,128)(2,1)S(1)} %collective-permute-done.7.refs_2_), custom_call_target="tpu_custom_call" | custom-call | flops 268435456 | bytes 1900544 | tf_op jit(solution)/shard_map/pallas_call | solution.py:149
  (11 shorter events, 0.1 us)
Async XLA Ops:
  0.0 1.2 %copy-start = (bf16[128,4096]{1,0:T(8,128)(2,1)S(1)}, bf16[128,4096]{1,0:T(8,128)(2,1)}, u32[]{:S(2)}) copy-start(bf16[128,4096]{1,0:T(8,128)(2,1)} %refs_0_.2) | copy-start | bytes 3145732
  2.3 10.5 %copy-start.1 = (bf16[128,512]{1,0:T(8,128)(2,1)S(1)}, bf16[128,512]{1,0:T(8,128)(2,1)}, u32[]{:S(2)}) copy-start(bf16[128,512]{1,0:T(8,128)(2,1)} %refs_0_.3) | copy-start | bytes 393220
  2.3 39.2 %all-to-all-start = ((bf16[8,128,512]{2,1,0:T(8,128)(2,1)}), bf16[8,128,512]{2,1,0:T(8,128)(2,1)S(1)}, u32[]{:S(2)}, u32[]{:S(2)}) async-start(bf16[8,128,512]{2,1,0:T(8,128)(2,1)} %shard_map.37.refs_1_), calls=%async_computation | async-start | bytes 2097152 | tf_op jit(solution)/shard_map/all_to_all | solution.py:162
  13.1 11.1 %collective-permute-start = (f32[640,128]{1,0:T(8,128)S(1)}, f32[640,128]{1,0:T(8,128)S(1)}, u32[]{:S(2)}, u32[]{:S(2)}) collective-permute-start(f32[640,128]{1,0:T(8,128)S(1)} %get-tuple-element.12), channel_id=1, source_target_pairs={{0,64},{64,0},{1,65},{65,1},{2,66},{66,2},{3,67},{67,3},{4,68},{68... | collective-permute-start | bytes 983048 | tf_op jit(solution)/shard_map/ppermute | solution.py:166
  24.2 8.7 %collective-permute-start.1 = (f32[320,128]{1,0:T(8,128)S(1)}, f32[320,128]{1,0:T(8,128)S(1)}, u32[]{:S(2)}, u32[]{:S(2)}) collective-permute-start(f32[320,128]{1,0:T(8,128)S(1)} %get-tuple-element.14), channel_id=1, source_target_pairs={{0,256},{128,384},{256,0},{384,128},{1,257},{129,385},{257,1},{385... | collective-permute-start | bytes 491528 | tf_op jit(solution)/shard_map/ppermute | solution.py:166
  33.0 6.3 %collective-permute-start.2 = (f32[160,128]{1,0:T(8,128)S(1)}, f32[160,128]{1,0:T(8,128)S(1)}, u32[]{:S(2)}, u32[]{:S(2)}) collective-permute-start(f32[160,128]{1,0:T(8,128)S(1)} %get-tuple-element.16), channel_id=1, source_target_pairs={{0,128},{128,0},{256,384},{384,256},{1,129},{129,1},{257,385},{385... | collective-permute-start | bytes 245768 | tf_op jit(solution)/shard_map/ppermute | solution.py:166
  43.0 20.3 %all-to-all-start.1 = ((f32[8,160,128]{2,1,0:T(8,128)}), f32[8,160,128]{2,1,0:T(8,128)S(1)}, u32[]{:S(2)}, u32[]{:S(2)}) async-start(f32[8,160,128]{2,1,0:T(8,128)} %bitcast), calls=%async_computation.1 | async-start | bytes 1310720 | tf_op jit(solution)/shard_map/all_to_all | solution.py:162
  48.8 6.3 %collective-permute-start.3 = (f32[160,128]{1,0:T(8,128)S(1)}, f32[160,128]{1,0:T(8,128)S(1)}, u32[]{:S(2)}, u32[]{:S(2)}) collective-permute-start(f32[160,128]{1,0:T(8,128)S(1)} %shard_map.41.refs_1_.refs_0_), channel_id=1, source_target_pairs={{0,8},{8,0},{16,24},{24,16},{32,40},{40,32},{48,56},{56,48},{1,9},... | collective-permute-start | bytes 245768 | tf_op jit(solution)/shard_map/ppermute | solution.py:166
  55.1 8.1 %collective-permute-start.4 = (f32[160,128]{1,0:T(8,128)S(1)}, f32[160,128]{1,0:T(8,128)S(1)}, u32[]{:S(2)}, u32[]{:S(2)}) collective-permute-start(f32[160,128]{1,0:T(8,128)S(1)} %shard_map.43.refs_0_), channel_id=1, source_target_pairs={{0,16},{8,24},{16,0},{24,8},{32,48},{40,56},{48,32},{56,40},{1,17}... | collective-permute-start | bytes 245768 | tf_op jit(solution)/shard_map/ppermute | solution.py:166
  64.2 17.7 %all-to-all-start.3 = ((f32[8,160,128]{2,1,0:T(8,128)}), f32[8,160,128]{2,1,0:T(8,128)S(1)}, u32[]{:S(2)}, u32[]{:S(2)}) async-start(f32[8,160,128]{2,1,0:T(8,128)} %shard_map.45.refs_2_), calls=%async_computation.3 | async-start | bytes 1310720 | tf_op jit(solution)/shard_map/all_to_all | solution.py:162
  69.9 11.1 %collective-permute-start.5 = (f32[160,128]{1,0:T(8,128)S(1)}, f32[160,128]{1,0:T(8,128)S(1)}, u32[]{:S(2)}, u32[]{:S(2)}) collective-permute-start(f32[160,128]{1,0:T(8,128)S(1)} %shard_map.44.refs_1_.refs_0_), channel_id=1, source_target_pairs={{0,32},{8,40},{16,48},{24,56},{32,0},{40,8},{48,16},{56,24},{1,33}... | collective-permute-start | bytes 245768 | tf_op jit(solution)/shard_map/ppermute | solution.py:166
  81.9 24.9 %all-to-all-start.2 = ((f32[8,160,128]{2,1,0:T(8,128)}), f32[8,160,128]{2,1,0:T(8,128)S(1)}, u32[]{:S(2)}, u32[]{:S(2)}) async-start(f32[8,160,128]{2,1,0:T(8,128)} %shard_map.46.refs_1_), calls=%async_computation.2 | async-start | bytes 1310720 | tf_op jit(solution)/shard_map/all_to_all | solution.py:162
  87.6 19.2 %copy-start.2 = (bf16[512,512]{1,0:T(8,128)(2,1)S(1)}, bf16[512,512]{1,0:T(8,128)(2,1)}, u32[]{:S(2)}) copy-start(bf16[512,512]{1,0:T(8,128)(2,1)} %refs_1_.1) | copy-start | bytes 1572868
  89.9 15.0 %collective-permute-start.6 = (bf16[640,128]{1,0:T(8,128)(2,1)S(1)}, bf16[640,128]{1,0:T(8,128)(2,1)S(1)}, u32[]{:S(2)}, u32[]{:S(2)}) collective-permute-start(bf16[640,128]{1,0:T(8,128)(2,1)S(1)} %shard_map.48), channel_id=1, source_target_pairs={{0,0},{1,64},{2,130},{3,194},{4,260},{5,324},{6,390},{7,454},{8,8}... | collective-permute-start | bytes 491528 | tf_op jit(solution)/shard_map/ppermute | solution.py:175
  104.8 4.5 %collective-permute-start.7 = (bf16[640,128]{1,0:T(8,128)(2,1)S(1)}, bf16[640,128]{1,0:T(8,128)(2,1)S(1)}, u32[]{:S(2)}, u32[]{:S(2)}) collective-permute-start(bf16[640,128]{1,0:T(8,128)(2,1)S(1)} %collective-permute-done.6.refs_1_), channel_id=1, source_target_pairs={{0,1},{1,0},{2,3},{3,2},{4,5},{5,4},{6,7},{7,6},{8,9},{9,8},{10,11... | collective-permute-start | bytes 491528 | tf_op jit(solution)/shard_map/ppermute | solution.py:166

commit v3 on v2

--- a/solution.py
+++ b/solution.py
@@ -1,5 +1,3 @@
-import functools
-
 import jax
 import jax.numpy as jnp
 import numpy as np
@@ -75,20 +73,30 @@
     return (z * (1.0 / jnp.sqrt(frob))).astype(BF16)
 
 
-def split_kernel(grads, out):
-    for peer in range(PEERS):
-        out[peer] = grads[:, peer * BLOCK : (peer + 1) * BLOCK]
-
-
-def act_gram_kernel(acts, keep, send, packed):
-    pack(gram(acts[...]), packed)
-    bit = lax.axis_index("yl")
-    keep[...] = packed[rows(bit, HALF), :]
-    send[...] = packed[rows(1 - bit, HALF), :]
-
-
-def halve_kernel(digit, kept, got, keep, send):
-    bit = lax.rem(lax.axis_index("x") // digit, 2)
+def split_kernel(grads, out, sems):
+    moves = [
+        pltpu.make_async_copy(
+            grads.at[:, pl.ds(peer * BLOCK, BLOCK)], out.at[peer], sems.at[peer]
+        )
+        for peer in range(PEERS)
+    ]
+    for move in moves:
+        move.start()
+    for move in moves:
+        move.wait()
+
+
+def act_gram_kernel(mine, other, keep, send, packed):
+    pack(gram(jnp.concatenate([mine[...], other[...]], axis=0)), packed)
+    count = keep.shape[0]
+    start = 2 * lax.axis_index("yl")
+    bit = lax.axis_index("x") // 2
+    keep[...] = packed[rows(start + bit, count), :]
+    send[...] = packed[rows(start + 1 - bit, count), :]
+
+
+def halve_kernel(kept, got, keep, send):
+    bit = lax.rem(lax.axis_index("x"), 2)
     count = keep.shape[0]
     keep[...] = kept[rows(bit, count), :] + got[rows(bit, count), :]
     send[...] = kept[rows(1 - bit, count), :] + got[rows(1 - bit, count), :]
@@ -98,28 +106,27 @@
     out[...] = kept[...] + got[...]
 
 
-def copies_kernel(kept, got, out):
-    total = kept[...] + got[...]
-    for peer in range(PEERS):
-        out[peer] = total
+def add_four_kernel(kept, second, third, fourth, out):
+    out[...] = (kept[...] + second[...]) + (third[...] + fourth[...])
 
 
 def grad_gram_kernel(got, out):
     pack(gram(got[...].reshape(PEERS * TILE, BLOCK)), out)
 
 
-def sum_kernel(got, out):
+def sum_kernel(got, share, out, copies):
     total = got[0]
     for peer in range(1, PEERS):
         total += got[peer]
+    out[...] = total
     for peer in range(PEERS):
-        out[peer] = total
-
-
-def grad_root_kernel(got, out, full, packed):
-    unpack(got, full)
-    pack(inverse_root(full[...]), packed)
-    out[...] = packed[rows(lax.axis_index("yl"), HALF), :]
+        copies[peer] = share[...]
+
+
+def join_kernel(*refs):
+    *parts, out = refs
+    for place, part in enumerate(parts):
+        out[place] = part[...]
 
 
 def left_kernel(got, grad, out, packed, full):
@@ -133,10 +140,14 @@
 
 def last_kernel(left, mine, other, out, packed, full):
     bit = lax.axis_index("c")
-    packed[rows(bit, HALF), :] = mine[...]
-    packed[rows(1 - bit, HALF), :] = other[...]
+    turn = lax.axis_index("yh") - lax.axis_index("x") + 4
+    for step in range(4):
+        owner = 2 * lax.rem(turn + 4 - step, 4)
+        packed[rows(owner + bit, SHARE), :] = mine[step]
+        packed[rows(owner + 1 - bit, SHARE), :] = other[step]
     unpack(packed, full)
-    out[...] = jnp.dot(left[...], full[...], preferred_element_type=F32)
+    root = inverse_root(full[...])
+    out[...] = jnp.dot(left[...], root, preferred_element_type=F32)
 
 
 def call(kernel, args, outs, scratch=(), flops=1 << 20, after=()):
@@ -166,10 +177,10 @@
     return lax.ppermute(data, axis, [(i, i ^ distance) for i in range(size)])
 
 
-def transpose_places(data):
+def to_column(data, step):
     places = np.arange(np.prod(SIZES)).reshape(SIZES)
     pairs = [
-        (int(places[x, yl, z, yh, c]), int(places[yh, c, z, (x + yh) % 4, yl]))
+        (int(places[x, yl, z, yh, c]), int(places[yh, c, z, (x + yh + step) % 4, yl]))
         for x, yl, z, yh, c in np.ndindex(*SIZES)
     ]
     return lax.ppermute(data, AXES, pairs)
@@ -180,48 +191,44 @@
     packed, full = (PACKED, TILE), (BLOCK, BLOCK)
     copies = (PEERS, SHARE, TILE)
 
-    split = call(split_kernel, [grads_out], [((PEERS, TILE, BLOCK), BF16)])
+    split = pl.pallas_call(
+        split_kernel,
+        out_shape=jax.ShapeDtypeStruct((PEERS, TILE, BLOCK), BF16),
+        in_specs=[ANYWHERE],
+        out_specs=ANYWHERE,
+        scratch_shapes=[pltpu.SemaphoreType.DMA((PEERS,))],
+        cost_estimate=pl.CostEstimate(flops=0, bytes_accessed=2 << 20, transcendentals=0),
+    )(grads_out)
     tokens = exchange(split, "z")
 
-    half = [((HALF, TILE), F32)] * 2
-    keep, send = call(act_gram_kernel, [acts], half, [(packed, F32)], cube // 4, [split])
-    got = swap(send, "yl", 2, 1)
+    other = swap(acts, "yl", 2, 1)
     quarter = [((HALF // 2, TILE), F32)] * 2
-    keep, send = call(functools.partial(halve_kernel, 2), [keep, got], quarter)
+    keep, send = call(act_gram_kernel, [acts, other], quarter, [(packed, F32)], cube // 2)
     got = swap(send, "x", 4, 2)
     eighth = [((SHARE, TILE), F32)] * 2
-    keep, send = call(functools.partial(halve_kernel, 1), [keep, got], eighth)
+    keep, send = call(halve_kernel, [keep, got], eighth)
     got = swap(send, "x", 4, 1)
-    share_xy = call(add_kernel, [keep, got], eighth[:1])
-    part = call(grad_gram_kernel, [tokens], [(packed, F32)], (), 2 * cube, [share_xy])
-
-    got = swap(share_xy, "z", 8, 1)
-    share = call(add_kernel, [share_xy, got], eighth[:1], after=[part])
-    got = swap(share, "z", 8, 2)
-    share_z = call(add_kernel, [share, got], eighth[:1])
+    share = call(add_kernel, [keep, got], eighth[:1])
+    got = swap(share, "z", 8, 1)
+    share = call(add_kernel, [share, got], eighth[:1])
+    part = call(grad_gram_kernel, [tokens], [(packed, F32)], (), 2 * cube, [share])
+
+    got = [swap(share, "z", 8, distance) for distance in (2, 4, 6)]
+    share = call(add_four_kernel, [share, *got], eighth[:1], after=[part])
     parts = exchange(part.reshape(copies), ("x", "yl"))
-    sent = call(sum_kernel, [parts], [(copies, F32)], after=[share_z])
-
-    got = swap(share_z, "z", 8, 4)
-    act_sent = call(copies_kernel, [share_z, got], [(copies, F32)], after=[sent])
-    grad_cov = exchange(sent, ("x", "yl")).reshape(packed)
-    root = call(
-        grad_root_kernel,
-        [grad_cov],
-        [((HALF, TILE), BF16)],
-        [(full, F32), (packed, BF16)],
-        6 * cube,
-        [act_sent],
-    )
-    mine = transpose_places(root)
+    grad_share, act_sent = call(
+        sum_kernel, [parts, share], [((SHARE, TILE), F32), (copies, F32)]
+    )
+    joined = [((4, SHARE, TILE), F32)]
+    mine = call(join_kernel, [to_column(grad_share, step) for step in range(4)], joined)
+    other = swap(mine, "c", 2, 1)
 
     act_cov = exchange(act_sent, ("x", "yl"))
     left = call(
         left_kernel, [act_cov, grad], [(full, BF16)], [(packed, F32), (full, F32)], 7 * cube
     )
-    other = swap(mine, "c", 2, 1)
     return call(
-        last_kernel, [left, mine, other], [(full, F32)], [(packed, BF16), (full, BF16)], cube
+        last_kernel, [left, mine, other], [(full, F32)], [(packed, F32), (full, F32)], 7 * cube
     )
 
 

time: 112 us -> 142 us (1.27)
  the two profiles are of different devices: /device:TPU:6 before, /device:TPU:5 now
where the time goes in v3:
time: 142 us; the launch traced here: 141 us
  starting transfers between devices  68.8 us (48%)
  Pallas kernels  42 us (30%)
  waiting for transfers between devices  30 us (21%)
    pallas_call x1, Pallas kernels, on_device(): pl.pallas_call(split_kernel, out_shape=jax.ShapeDtypeStruct((PEERS, TILE,...  32.9 us
    ppermute x8, starting transfers between devices, swap(): return lax.ppermute(data, axis, [(i, i ^ distance) for i in range(size)])  26.2 us
    ppermute x4, starting transfers between devices, to_column(): return lax.ppermute(data, AXES, pairs)  21.9 us
    all_to_all x3, starting transfers between devices, exchange(): return lax.all_to_all(data, axes, split_axis=0, concat_axis=0, tiled=True)  20.6 us
    ppermute x8, waiting for transfers between devices, swap(): return lax.ppermute(data, axis, [(i, i ^ distance) for i in range(size)])  17.6 us
    ppermute x4, waiting for transfers between devices, to_column(): return lax.ppermute(data, AXES, pairs)  9.57 us
    pallas_call x10, Pallas kernels, call(): pl.pallas_call(body, out_shape=outs, in_specs=[VMEM] * len(args) + [ANYWH...  9.05 us
    all_to_all x3, waiting for transfers between devices, exchange(): return lax.all_to_all(data, axes, split_axis=0, concat_axis=0, tiled=True)  2.92 us
  transfers between devices with their start and end apart: 15, of which 9 were waited for; matrix products, arithmetic and copies ran while one was open for 0% of the time, Pallas kernels for 2%

profile of v3, /device:TPU:5, one launch (start us, length us, event | category | flops | bytes accessed | tf_op | source)
XLA Modules:
  0.0 141.0 jit_solution(14912823622251686248)
XLA Ops:
  0.0 32.9 %shard_map.37 = bf16[8,128,512]{2,1,0:T(8,128)(2,1)} custom-call(bf16[128,4096]{1,0:T(8,128)(2,1)} %grads.1), custom_call_target="tpu_custom_call" | custom-call | bytes 2097152 | tf_op jit(solution)/shard_map/pallas_call | solution.py:194
  32.9 0.0 copy-start.1
  33.0 10.2 %all-to-all-start = ((bf16[8,128,512]{2,1,0:T(8,128)(2,1)}), bf16[8,128,512]{2,1,0:T(8,128)(2,1)S(1)}, u32[]{:S(2)}, u32[]{:S(2)}) async-start(bf16[8,128,512]{2,1,0:T(8,128)(2,1)} %shard_map.37), calls=%async_computation | async-start | bytes 2097152 | tf_op jit(solution)/shard_map/all_to_all | solution.py:173
  43.1 3.2 %collective-permute-start = (bf16[128,512]{1,0:T(8,128)(2,1)S(1)}, bf16[128,512]{1,0:T(8,128)(2,1)S(1)}, u32[]{:S(2)}, u32[]{:S(2)}) collective-permute-start(bf16[128,512]{1,0:T(8,128)(2,1)S(1)} %copy-done.1), channel_id=1, source_target_pairs={{0,64},{64,0},{1,65},{65,1},{2,66},{66,2},{3,67},{67,3},{4,68},{68... | collective-permute-start | bytes 393224 | tf_op jit(solution)/shard_map/ppermute | solution.py:177
  46.4 2.8 %collective-permute-done.refs_1_ = bf16[128,512]{1,0:T(8,128)(2,1)S(1)} collective-permute-done((bf16[128,512]{1,0:T(8,128)(2,1)S(1)}, bf16[128,512]{1,0:T(8,128)(2,1)S(1)}, u32[]{:S(2)}, u32[]{:S(2)}) %collective-permute-start) | collective-permute-done | bytes 131104 | tf_op jit(solution)/shard_map/ppermute | solution.py:177
  49.1 0.3 shard_map.38
  49.5 2.1 %collective-permute-start.1 = (f32[320,128]{1,0:T(8,128)S(1)}, f32[320,128]{1,0:T(8,128)S(1)}, u32[]{:S(2)}, u32[]{:S(2)}) collective-permute-start(f32[320,128]{1,0:T(8,128)S(1)} %get-tuple-element.12), channel_id=1, source_target_pairs={{0,256},{128,384},{256,0},{384,128},{1,257},{129,385},{257,1},{385... | collective-permute-start | bytes 491528 | tf_op jit(solution)/shard_map/ppermute | solution.py:177
  51.6 5.7 %collective-permute-done.1.refs_1_ = f32[320,128]{1,0:T(8,128)S(1)} collective-permute-done((f32[320,128]{1,0:T(8,128)S(1)}, f32[320,128]{1,0:T(8,128)S(1)}, u32[]{:S(2)}, u32[]{:S(2)}) %collective-permute-start.1) | collective-permute-done | bytes 163872 | tf_op jit(solution)/shard_map/ppermute | solution.py:177
  57.4 2.7 %collective-permute-start.2 = (f32[160,128]{1,0:T(8,128)S(1)}, f32[160,128]{1,0:T(8,128)S(1)}, u32[]{:S(2)}, u32[]{:S(2)}) collective-permute-start(f32[160,128]{1,0:T(8,128)S(1)} %get-tuple-element.14), channel_id=1, source_target_pairs={{0,128},{128,0},{256,384},{384,256},{1,129},{129,1},{257,385},{385... | collective-permute-start | bytes 245768 | tf_op jit(solution)/shard_map/ppermute | solution.py:177
  60.1 2.8 %collective-permute-done.2.refs_1_ = f32[160,128]{1,0:T(8,128)S(1)} collective-permute-done((f32[160,128]{1,0:T(8,128)S(1)}, f32[160,128]{1,0:T(8,128)S(1)}, u32[]{:S(2)}, u32[]{:S(2)}) %collective-permute-start.2) | collective-permute-done | bytes 81952 | tf_op jit(solution)/shard_map/ppermute | solution.py:177
  62.9 3.1 %collective-permute-start.3 = (f32[160,128]{1,0:T(8,128)S(1)}, f32[160,128]{1,0:T(8,128)S(1)}, u32[]{:S(2)}, u32[]{:S(2)}) collective-permute-start(f32[160,128]{1,0:T(8,128)S(1)} %shard_map.40.refs_0_), channel_id=1, source_target_pairs={{0,8},{8,0},{16,24},{24,16},{32,40},{40,32},{48,56},{56,48},{1,9},... | collective-permute-start | bytes 245768 | tf_op jit(solution)/shard_map/ppermute | solution.py:177
  66.0 3.4 %collective-permute-done.3.refs_1_ = f32[160,128]{1,0:T(8,128)S(1)} collective-permute-done((f32[160,128]{1,0:T(8,128)S(1)}, f32[160,128]{1,0:T(8,128)S(1)}, u32[]{:S(2)}, u32[]{:S(2)}) %collective-permute-start.3) | collective-permute-done | bytes 81952 | tf_op jit(solution)/shard_map/ppermute | solution.py:177
  69.4 2.9 %all-to-all-done.refs_0_ = bf16[8,128,512]{2,1,0:T(8,128)(2,1)S(1)} async-done(((bf16[8,128,512]{2,1,0:T(8,128)(2,1)}), bf16[8,128,512]{2,1,0:T(8,128)(2,1)S(1)}, u32[]{:S(2)}, u32[]{:S(2)}) %all-to-all-start) | async-done | bytes 1048608 | tf_op jit(solution)/shard_map/all_to_all | solution.py:173
  72.3 1.6 %shard_map.42.refs_4_ = f32[1280,128]{1,0:T(8,128)} custom-call(bf16[8,128,512]{2,1,0:T(8,128)(2,1)S(1)} %all-to-all-done.refs_0_, f32[160,128]{1,0:T(8,128)S(1)} %shard_map.41.refs_1_.refs_0_), custom_call_target="tpu_custom_call" | custom-call | flops 536870912 | bytes 1703936 | tf_op jit(solution)/shard_map/pallas_call | solution.py:160
  73.9 5.3 %all-to-all-start.1 = ((f32[8,160,128]{2,1,0:T(8,128)}), f32[8,160,128]{2,1,0:T(8,128)S(1)}, u32[]{:S(2)}, u32[]{:S(2)}) async-start(f32[8,160,128]{2,1,0:T(8,128)} %bitcast), calls=%async_computation.1 | async-start | bytes 1310720 | tf_op jit(solution)/shard_map/all_to_all | solution.py:173
  79.2 1.9 %collective-permute-start.4 = (f32[160,128]{1,0:T(8,128)S(1)}, f32[160,128]{1,0:T(8,128)S(1)}, u32[]{:S(2)}, u32[]{:S(2)}) collective-permute-start(f32[160,128]{1,0:T(8,128)S(1)} %shard_map.41.refs_1_.refs_0_), channel_id=1, source_target_pairs={{0,16},{8,24},{16,0},{24,8},{32,48},{40,56},{48,32},{56,40},{1,17}... | collective-permute-start | bytes 245768 | tf_op jit(solution)/shard_map/ppermute | solution.py:177
  81.1 4.1 %collective-permute-start.5 = (f32[160,128]{1,0:T(8,128)S(1)}, f32[160,128]{1,0:T(8,128)S(1)}, u32[]{:S(2)}, u32[]{:S(2)}) collective-permute-start(f32[160,128]{1,0:T(8,128)S(1)} %shard_map.41.refs_1_.refs_0_), channel_id=1, source_target_pairs={{0,32},{8,40},{16,48},{24,56},{32,0},{40,8},{48,16},{56,24},{1,33}... | collective-permute-start | bytes 245768 | tf_op jit(solution)/shard_map/ppermute | solution.py:177
  85.2 5.4 %collective-permute-start.6 = (f32[160,128]{1,0:T(8,128)S(1)}, f32[160,128]{1,0:T(8,128)S(1)}, u32[]{:S(2)}, u32[]{:S(2)}) collective-permute-start(f32[160,128]{1,0:T(8,128)S(1)} %shard_map.41.refs_1_.refs_0_), channel_id=1, source_target_pairs={{0,48},{8,56},{16,32},{24,40},{32,16},{40,24},{48,0},{56,8},{1,49}... | collective-permute-start | bytes 245768 | tf_op jit(solution)/shard_map/ppermute | solution.py:177
  90.6 1.3 collective-permute-done.5.refs_2_
  91.9 1.5 %collective-permute-done.6.refs_3_ = f32[160,128]{1,0:T(8,128)S(1)} collective-permute-done((f32[160,128]{1,0:T(8,128)S(1)}, f32[160,128]{1,0:T(8,128)S(1)}, u32[]{:S(2)}, u32[]{:S(2)}) %collective-permute-start.6) | collective-permute-done | bytes 81952 | tf_op jit(solution)/shard_map/ppermute | solution.py:177
  93.5 0.9 shard_map.44
  94.4 5.1 %all-to-all-start.2 = ((f32[8,160,128]{2,1,0:T(8,128)}), f32[8,160,128]{2,1,0:T(8,128)S(1)}, u32[]{:S(2)}, u32[]{:S(2)}) async-start(f32[8,160,128]{2,1,0:T(8,128)} %get-tuple-element.15), calls=%async_computation.2 | async-start | bytes 1310720 | tf_op jit(solution)/shard_map/all_to_all | solution.py:173
  99.5 11.1 %collective-permute-start.10 = (f32[160,128]{1,0:T(8,128)S(1)}, f32[160,128]{1,0:T(8,128)S(1)}, u32[]{:S(2)}, u32[]{:S(2)}) collective-permute-start(f32[160,128]{1,0:T(8,128)S(1)} %get-tuple-element.16), channel_id=1, source_target_pairs={{0,6},{1,70},{2,128},{3,192},{4,258},{5,322},{6,388},{7,452},{8,14... | collective-permute-start | bytes 245768 | tf_op jit(solution)/shard_map/ppermute | solution.py:186
  110.7 3.4 %collective-permute-start.7 = (f32[160,128]{1,0:T(8,128)S(1)}, f32[160,128]{1,0:T(8,128)S(1)}, u32[]{:S(2)}, u32[]{:S(2)}) collective-permute-start(f32[160,128]{1,0:T(8,128)S(1)} %get-tuple-element.16), channel_id=1, source_target_pairs={{0,0},{1,64},{2,130},{3,194},{4,260},{5,324},{6,390},{7,454},{8,8}... | collective-permute-start | bytes 245768 | tf_op jit(solution)/shard_map/ppermute | solution.py:186
  114.0 5.5 %collective-permute-start.8 = (f32[160,128]{1,0:T(8,128)S(1)}, f32[160,128]{1,0:T(8,128)S(1)}, u32[]{:S(2)}, u32[]{:S(2)}) collective-permute-start(f32[160,128]{1,0:T(8,128)S(1)} %get-tuple-element.16), channel_id=1, source_target_pairs={{0,2},{1,66},{2,132},{3,196},{4,262},{5,326},{6,384},{7,448},{8,10... | collective-permute-start | bytes 245768 | tf_op jit(solution)/shard_map/ppermute | solution.py:186
  119.6 1.9 %collective-permute-start.9 = (f32[160,128]{1,0:T(8,128)S(1)}, f32[160,128]{1,0:T(8,128)S(1)}, u32[]{:S(2)}, u32[]{:S(2)}) collective-permute-start(f32[160,128]{1,0:T(8,128)S(1)} %get-tuple-element.16), channel_id=1, source_target_pairs={{0,4},{1,68},{2,134},{3,198},{4,256},{5,320},{6,386},{7,450},{8,12... | collective-permute-start | bytes 245768 | tf_op jit(solution)/shard_map/ppermute | solution.py:186
  121.5 0.0 collective-permute-done.10.refs_3_
  121.5 3.2 %collective-permute-done.8.refs_1_ = f32[160,128]{1,0:T(8,128)S(1)} collective-permute-done((f32[160,128]{1,0:T(8,128)S(1)}, f32[160,128]{1,0:T(8,128)S(1)}, u32[]{:S(2)}, u32[]{:S(2)}) %collective-permute-start.8) | collective-permute-done | bytes 81952 | tf_op jit(solution)/shard_map/ppermute | solution.py:186
  124.7 6.4 %collective-permute-done.9.refs_2_ = f32[160,128]{1,0:T(8,128)S(1)} collective-permute-done((f32[160,128]{1,0:T(8,128)S(1)}, f32[160,128]{1,0:T(8,128)S(1)}, u32[]{:S(2)}, u32[]{:S(2)}) %collective-permute-start.9) | collective-permute-done | bytes 81952 | tf_op jit(solution)/shard_map/ppermute | solution.py:186
  131.1 3.7 %collective-permute-start.11 = (f32[4,160,128]{2,1,0:T(8,128)S(1)}, f32[4,160,128]{2,1,0:T(8,128)S(1)}, u32[]{:S(2)}, u32[]{:S(2)}) collective-permute-start(f32[4,160,128]{2,1,0:T(8,128)S(1)} %shard_map.46.refs_1_), channel_id=1, source_target_pairs={{0,1},{1,0},{2,3},{3,2},{4,5},{5,4},{6,7},{7,6},{8,9},{9,8},{10,11... | collective-permute-start | bytes 983048 | tf_op jit(solution)/shard_map/ppermute | solution.py:177
  134.9 2.5 %shard_map.45.refs_0_ = bf16[512,512]{1,0:T(8,128)(2,1)S(1)} custom-call(f32[8,160,128]{2,1,0:T(8,128)S(1)} %all-to-all-done.2.refs_0_, bf16[512,512]{1,0:T(8,128)(2,1)S(1)} %copy-done), custom_call_target="tpu_custom_call" | custom-call | flops 1879048192 | bytes 1703936 | tf_op jit(solution)/shard_map/pallas_call | solution.py:160
  137.4 3.6 %shard_map.47 = f32[512,512]{1,0:T(8,128)} custom-call(bf16[512,512]{1,0:T(8,128)(2,1)S(1)} %shard_map.45.refs_0_, f32[4,160,128]{2,1,0:T(8,128)S(1)} %shard_map.46.refs_1_, f32[4,160,128]{2,1,0:T(8,128)S(1)} %collective-permute-done.11.refs_2_), custom_call_target="tpu_custom_call" | custom-call | flops 1879048192 | bytes 2228224 | tf_op jit(solution)/shard_map/pallas_call | solution.py:160
  (13 shorter events, 0.1 us)
Async XLA Ops:
  32.9 10.2 %copy-start.1 = (bf16[128,512]{1,0:T(8,128)(2,1)S(1)}, bf16[128,512]{1,0:T(8,128)(2,1)}, u32[]{:S(2)}) copy-start(bf16[128,512]{1,0:T(8,128)(2,1)} %refs_0_.1) | copy-start | bytes 393220
  33.0 39.4 %all-to-all-start = ((bf16[8,128,512]{2,1,0:T(8,128)(2,1)}), bf16[8,128,512]{2,1,0:T(8,128)(2,1)S(1)}, u32[]{:S(2)}, u32[]{:S(2)}) async-start(bf16[8,128,512]{2,1,0:T(8,128)(2,1)} %shard_map.37), calls=%async_computation | async-start | bytes 2097152 | tf_op jit(solution)/shard_map/all_to_all | solution.py:173
  43.1 6.0 %collective-permute-start = (bf16[128,512]{1,0:T(8,128)(2,1)S(1)}, bf16[128,512]{1,0:T(8,128)(2,1)S(1)}, u32[]{:S(2)}, u32[]{:S(2)}) collective-permute-start(bf16[128,512]{1,0:T(8,128)(2,1)S(1)} %copy-done.1), channel_id=1, source_target_pairs={{0,64},{64,0},{1,65},{65,1},{2,66},{66,2},{3,67},{67,3},{4,68},{68... | collective-permute-start | bytes 393224 | tf_op jit(solution)/shard_map/ppermute | solution.py:177
  49.5 7.9 %collective-permute-start.1 = (f32[320,128]{1,0:T(8,128)S(1)}, f32[320,128]{1,0:T(8,128)S(1)}, u32[]{:S(2)}, u32[]{:S(2)}) collective-permute-start(f32[320,128]{1,0:T(8,128)S(1)} %get-tuple-element.12), channel_id=1, source_target_pairs={{0,256},{128,384},{256,0},{384,128},{1,257},{129,385},{257,1},{385... | collective-permute-start | bytes 491528 | tf_op jit(solution)/shard_map/ppermute | solution.py:177
  57.4 5.5 %collective-permute-start.2 = (f32[160,128]{1,0:T(8,128)S(1)}, f32[160,128]{1,0:T(8,128)S(1)}, u32[]{:S(2)}, u32[]{:S(2)}) collective-permute-start(f32[160,128]{1,0:T(8,128)S(1)} %get-tuple-element.14), channel_id=1, source_target_pairs={{0,128},{128,0},{256,384},{384,256},{1,129},{129,1},{257,385},{385... | collective-permute-start | bytes 245768 | tf_op jit(solution)/shard_map/ppermute | solution.py:177
  62.9 6.5 %collective-permute-start.3 = (f32[160,128]{1,0:T(8,128)S(1)}, f32[160,128]{1,0:T(8,128)S(1)}, u32[]{:S(2)}, u32[]{:S(2)}) collective-permute-start(f32[160,128]{1,0:T(8,128)S(1)} %shard_map.40.refs_0_), channel_id=1, source_target_pairs={{0,8},{8,0},{16,24},{24,16},{32,40},{40,32},{48,56},{56,48},{1,9},... | collective-permute-start | bytes 245768 | tf_op jit(solution)/shard_map/ppermute | solution.py:177
  73.9 19.6 %all-to-all-start.1 = ((f32[8,160,128]{2,1,0:T(8,128)}), f32[8,160,128]{2,1,0:T(8,128)S(1)}, u32[]{:S(2)}, u32[]{:S(2)}) async-start(f32[8,160,128]{2,1,0:T(8,128)} %bitcast), calls=%async_computation.1 | async-start | bytes 1310720 | tf_op jit(solution)/shard_map/all_to_all | solution.py:173
  79.2 11.4 %collective-permute-start.4 = (f32[160,128]{1,0:T(8,128)S(1)}, f32[160,128]{1,0:T(8,128)S(1)}, u32[]{:S(2)}, u32[]{:S(2)}) collective-permute-start(f32[160,128]{1,0:T(8,128)S(1)} %shard_map.41.refs_1_.refs_0_), channel_id=1, source_target_pairs={{0,16},{8,24},{16,0},{24,8},{32,48},{40,56},{48,32},{56,40},{1,17}... | collective-permute-start | bytes 245768 | tf_op jit(solution)/shard_map/ppermute | solution.py:177
  81.1 10.8 %collective-permute-start.5 = (f32[160,128]{1,0:T(8,128)S(1)}, f32[160,128]{1,0:T(8,128)S(1)}, u32[]{:S(2)}, u32[]{:S(2)}) collective-permute-start(f32[160,128]{1,0:T(8,128)S(1)} %shard_map.41.refs_1_.refs_0_), channel_id=1, source_target_pairs={{0,32},{8,40},{16,48},{24,56},{32,0},{40,8},{48,16},{56,24},{1,33}... | collective-permute-start | bytes 245768 | tf_op jit(solution)/shard_map/ppermute | solution.py:177
  85.2 8.2 %collective-permute-start.6 = (f32[160,128]{1,0:T(8,128)S(1)}, f32[160,128]{1,0:T(8,128)S(1)}, u32[]{:S(2)}, u32[]{:S(2)}) collective-permute-start(f32[160,128]{1,0:T(8,128)S(1)} %shard_map.41.refs_1_.refs_0_), channel_id=1, source_target_pairs={{0,48},{8,56},{16,32},{24,40},{32,16},{40,24},{48,0},{56,8},{1,49}... | collective-permute-start | bytes 245768 | tf_op jit(solution)/shard_map/ppermute | solution.py:177
  94.4 40.5 %all-to-all-start.2 = ((f32[8,160,128]{2,1,0:T(8,128)}), f32[8,160,128]{2,1,0:T(8,128)S(1)}, u32[]{:S(2)}, u32[]{:S(2)}) async-start(f32[8,160,128]{2,1,0:T(8,128)} %get-tuple-element.15), calls=%async_computation.2 | async-start | bytes 1310720 | tf_op jit(solution)/shard_map/all_to_all | solution.py:173
  99.5 35.3 %copy-start = (bf16[512,512]{1,0:T(8,128)(2,1)S(1)}, bf16[512,512]{1,0:T(8,128)(2,1)}, u32[]{:S(2)}) copy-start(bf16[512,512]{1,0:T(8,128)(2,1)} %refs_1_.1) | copy-start | bytes 1572868
  99.5 22.0 %collective-permute-start.10 = (f32[160,128]{1,0:T(8,128)S(1)}, f32[160,128]{1,0:T(8,128)S(1)}, u32[]{:S(2)}, u32[]{:S(2)}) collective-permute-start(f32[160,128]{1,0:T(8,128)S(1)} %get-tuple-element.16), channel_id=1, source_target_pairs={{0,6},{1,70},{2,128},{3,192},{4,258},{5,322},{6,388},{7,452},{8,14... | collective-permute-start | bytes 245768 | tf_op jit(solution)/shard_map/ppermute | solution.py:186
  110.7 10.8 %collective-permute-start.7 = (f32[160,128]{1,0:T(8,128)S(1)}, f32[160,128]{1,0:T(8,128)S(1)}, u32[]{:S(2)}, u32[]{:S(2)}) collective-permute-start(f32[160,128]{1,0:T(8,128)S(1)} %get-tuple-element.16), channel_id=1, source_target_pairs={{0,0},{1,64},{2,130},{3,194},{4,260},{5,324},{6,390},{7,454},{8,8}... | collective-permute-start | bytes 245768 | tf_op jit(solution)/shard_map/ppermute | solution.py:186
  114.0 10.6 %collective-permute-start.8 = (f32[160,128]{1,0:T(8,128)S(1)}, f32[160,128]{1,0:T(8,128)S(1)}, u32[]{:S(2)}, u32[]{:S(2)}) collective-permute-start(f32[160,128]{1,0:T(8,128)S(1)} %get-tuple-element.16), channel_id=1, source_target_pairs={{0,2},{1,66},{2,132},{3,196},{4,262},{5,326},{6,384},{7,448},{8,10... | collective-permute-start | bytes 245768 | tf_op jit(solution)/shard_map/ppermute | solution.py:186
  119.6 11.5 %collective-permute-start.9 = (f32[160,128]{1,0:T(8,128)S(1)}, f32[160,128]{1,0:T(8,128)S(1)}, u32[]{:S(2)}, u32[]{:S(2)}) collective-permute-start(f32[160,128]{1,0:T(8,128)S(1)} %get-tuple-element.16), channel_id=1, source_target_pairs={{0,4},{1,68},{2,134},{3,198},{4,256},{5,320},{6,386},{7,450},{8,12... | collective-permute-start | bytes 245768 | tf_op jit(solution)/shard_map/ppermute | solution.py:186
  131.1 6.3 %collective-permute-start.11 = (f32[4,160,128]{2,1,0:T(8,128)S(1)}, f32[4,160,128]{2,1,0:T(8,128)S(1)}, u32[]{:S(2)}, u32[]{:S(2)}) collective-permute-start(f32[4,160,128]{2,1,0:T(8,128)S(1)} %shard_map.46.refs_1_), channel_id=1, source_target_pairs={{0,1},{1,0},{2,3},{3,2},{4,5},{5,4},{6,7},{7,6},{8,9},{9,8},{10,11... | collective-permute-start | bytes 983048 | tf_op jit(solution)/shard_map/ppermute | solution.py:177

commit v4 on v1

v4 whole, which is shorter than its diff:
```python
import jax
import jax.numpy as jnp
import numpy as np
from jax import lax
from jax.experimental import pallas as pl
from jax.experimental.pallas import tpu as pltpu
from jax.sharding import Mesh, PartitionSpec as P

TOKENS = 8192
DAMPING = 0.1
BLOCK = 512
TILE = 128
SIDE = BLOCK // TILE
TILES = [(a, b) for a in range(SIDE) for b in range(a, SIDE)]
PACKED = len(TILES) * TILE
HALF = PACKED // 2
PEERS = 8
SHARE = PACKED // PEERS
PIECE = 24
RAW = SIDE * TILE
DIAGONAL = 8
FIRST = RAW + SHARE + 2 * DIAGONAL
GATHER = SHARE + PIECE
SECOND = GATHER + DIAGONAL
BF16, F32 = jnp.bfloat16, jnp.float32
AXES = ("x", "yl", "z", "yh", "c")
SIZES = (4, 2, 8, 4, 2)
VMEM = pl.BlockSpec(memory_space=pltpu.VMEM)
PARAMS = pltpu.CompilerParams(vmem_limit_bytes=24 * 1024 * 1024)


def gram(data):
    return lax.dot_general(data, data, (((0,), (0,)), ((), ())), preferred_element_type=F32)


def pack(total, packed):
    for place, (a, b) in enumerate(TILES):
        tile = total[a * TILE : (a + 1) * TILE, b * TILE : (b + 1) * TILE]
        packed[place * TILE : (place + 1) * TILE, :] = tile


def unpack(packed, full):
    for place, (a, b) in enumerate(TILES):
        tile = packed[place * TILE : (place + 1) * TILE, :].astype(full.dtype)
        full[a * TILE : (a + 1) * TILE, b * TILE : (b + 1) * TILE] = tile
        if a != b:
            full[b * TILE : (b + 1) * TILE, a * TILE : (a + 1) * TILE] = tile.T


def rows(bit, count):
    return pl.ds(pl.multiple_of(bit * count, count), count)


def halves(values):
    high = values.astype(BF16)
    return high, (values - high.astype(F32)).astype(BF16)


def product(left, right):
    left_high, left_low = left
    right_high, right_low = right
    dot = lambda p, q: jnp.dot(p, q, preferred_element_type=F32)
    return dot(left_high, right_high) + (dot(left_high, right_low) + dot(left_low, right_high))


def on_diagonal(count):
    row = lax.broadcasted_iota(jnp.int32, (count, count), 0)
    return row == lax.broadcasted_iota(jnp.int32, (count, count), 1)


def diagonals(total):
    parts = []
    for a in range(SIDE):
        tile = total[a * TILE : (a + 1) * TILE, a * TILE : (a + 1) * TILE]
        parts.append(jnp.sum(jnp.where(on_diagonal(TILE), tile, 0.0), axis=0, keepdims=True))
    return jnp.concatenate(parts + [jnp.zeros((DIAGONAL - SIDE, TILE), F32)], axis=0)


def inverse_root(covariance):
    diagonal = on_diagonal(BLOCK)
    shifted = covariance * (1.0 / TOKENS) + jnp.where(diagonal, DAMPING, 0.0)
    squares = jnp.sum(jnp.sum(shifted * shifted, axis=0, keepdims=True), axis=1, keepdims=True)
    frob = jnp.sqrt(squares)
    y = shifted * (1.0 / frob)
    y_halves = halves(y)
    s = product(y_halves, y_halves)
    tail = product(halves(s), halves(0.0625 * s - 0.5625 * y))
    z = jnp.where(diagonal, 2.25, 0.0) - 2.4375 * y + 1.6875 * s + tail
    return (z * (1.0 / jnp.sqrt(frob))).astype(BF16)


def first_kernel(acts, grads, out, packed):
    total = gram(acts[...])
    pack(total, packed)
    high, low = halves(diagonals(total))
    ends = jnp.concatenate([high, low], axis=0)
    for peer in range(PEERS):
        for part in range(SIDE):
            column = peer * BLOCK + part * TILE
            out[peer, part * TILE : (part + 1) * TILE, :] = grads[:, column : column + TILE]
        share = packed[peer * SHARE : (peer + 1) * SHARE, :]
        out[peer, RAW : RAW + SHARE, :] = share.astype(BF16)
        out[peer, RAW + SHARE : FIRST, :] = ends


def second_kernel(got, out, packed, share):
    tokens = jnp.concatenate(
        [got[:, p * TILE : (p + 1) * TILE, :].reshape(PEERS * TILE, TILE) for p in range(SIDE)],
        axis=1,
    )
    pack(gram(tokens), packed)
    total = jnp.zeros((SHARE, TILE), F32)
    ends = jnp.zeros((2 * DIAGONAL, TILE), F32)
    for peer in range(PEERS):
        total += got[peer, RAW : RAW + SHARE, :].astype(F32)
        ends += got[peer, RAW + SHARE : FIRST, :].astype(F32)
    share[0:SHARE, :] = total
    share[SHARE:, :] = jnp.zeros((PEERS * PIECE - SHARE, TILE), F32)
    for peer in range(PEERS):
        out[peer, 0:SHARE, :] = packed[peer * SHARE : (peer + 1) * SHARE, :]
        out[peer, SHARE:GATHER, :] = share[peer * PIECE : (peer + 1) * PIECE, :]
        out[peer, GATHER:SECOND, :] = ends[0:DIAGONAL] + ends[DIAGONAL:]


def sum_kernel(got, out, ends):
    total = got[0]
    for peer in range(1, PEERS):
        total += got[peer]
    for peer in range(PEERS):
        out[peer] = total[0:GATHER]
    ends[...] = total[GATHER:SECOND]


def grad_root_kernel(got, out, copies, full, packed, half, share):
    for peer in range(PEERS):
        packed[peer * SHARE : (peer + 1) * SHARE, :] = got[peer, 0:SHARE, :]
        share[peer * PIECE : (peer + 1) * PIECE, :] = got[peer, SHARE:GATHER, :]
    unpack(packed, full)
    pack(inverse_root(full[...]), half)
    out[...] = half[rows(lax.axis_index("yl"), HALF), :]
    for peer in range(PEERS):
        copies[peer] = share[0:SHARE, :].astype(BF16)


def left_kernel(got, ends, grad, out, full):
    unpack(got, full)
    for a in range(SIDE):
        place = slice(a * TILE, (a + 1) * TILE)
        full[place, place] = jnp.where(on_diagonal(TILE), ends[a : a + 1, :], full[place, place])
    root = inverse_root(full[...])
    out[...] = jnp.dot(root, grad[...], preferred_element_type=F32).astype(BF16)


def last_kernel(left, mine, other, out, packed, full):
    bit = lax.axis_index("c")
    packed[rows(bit, HALF), :] = mine[...]
    packed[rows(1 - bit, HALF), :] = other[...]
    unpack(packed, full)
    out[...] = jnp.dot(left[...], full[...], preferred_element_type=F32)


def call(kernel, args, outs, scratch=(), flops=1 << 20):
    outs = [jax.ShapeDtypeStruct(dims, dtype) for dims, dtype in outs]
    data = sum(a.size * a.dtype.itemsize for a in [*args, *outs])
    got = pl.pallas_call(
        kernel,
        out_shape=outs,
        in_specs=[VMEM] * len(args),
        out_specs=[VMEM] * len(outs),
        scratch_shapes=[pltpu.VMEM(dims, dtype) for dims, dtype in scratch],
        compiler_params=PARAMS,
        cost_estimate=pl.CostEstimate(flops=flops, bytes_accessed=data, transcendentals=0),
    )(*args)
    return got if len(outs) > 1 else got[0]


def exchange(data, axes):
    return lax.all_to_all(data, axes, split_axis=0, concat_axis=0, tiled=True)


def swap(data, axis, size, distance):
    return lax.ppermute(data, axis, [(i, i ^ distance) for i in range(size)])


def transpose_places(data):
    places = np.arange(np.prod(SIZES)).reshape(SIZES)
    pairs = [
        (int(places[x, yl, z, yh, c]), int(places[yh, c, z, (x + yh) % 4, yl]))
        for x, yl, z, yh, c in np.ndindex(*SIZES)
    ]
    return lax.ppermute(data, AXES, pairs)


def on_device(acts, grads_out, grad):
    cube = 2 * BLOCK**3
    packed, full = (PACKED, TILE), (BLOCK, BLOCK)

    share = (PEERS * PIECE, TILE)
    sent = call(
        first_kernel,
        [acts, grads_out],
        [((PEERS, FIRST, TILE), BF16)],
        [(packed, F32)],
        cube // 4,
    )
    got = exchange(sent, "z")
    sent = call(
        second_kernel,
        [got],
        [((PEERS, SECOND, TILE), F32)],
        [(packed, F32), (share, F32)],
        2 * cube,
    )
    got = exchange(sent, ("x", "yl"))
    sent, ends = call(
        sum_kernel, [got], [((PEERS, GATHER, TILE), F32), ((DIAGONAL, TILE), F32)]
    )
    got = exchange(sent, ("x", "yl"))
    root, sent = call(
        grad_root_kernel,
        [got],
        [((HALF, TILE), BF16), ((PEERS, SHARE, TILE), BF16)],
        [(full, F32), (packed, F32), (packed, BF16), (share, F32)],
        6 * cube,
    )
    mine = transpose_places(root)
    act_cov = exchange(sent, "z").reshape(packed)
    left = call(left_kernel, [act_cov, ends, grad], [(full, BF16)], [(full, F32)], 7 * cube)
    other = swap(mine, "c", 2, 1)
    return call(
        last_kernel, [left, mine, other], [(full, F32)], [(packed, BF16), (full, BF16)], cube
    )


def solution(mesh):
    split = Mesh(mesh.devices.reshape(SIZES), AXES)
    dp, tensor = AXES[:3], AXES[3:]
    return jax.shard_map(
        on_device,
        mesh=split,
        in_specs=(P(dp, tensor), P(dp, tensor), P(tensor, dp)),
        out_specs=P(tensor, dp),
        check_vma=False,
    )
```

time: 136 us -> 107 us (0.79)
  the two profiles are of different devices: /device:TPU:48 before, /device:TPU:6 now
where the time goes in v4:
time: 107 us; the launch traced here: 105 us
  blocking collectives  74.1 us (69%)
  starting transfers between devices  12.6 us (12%)
  Pallas kernels  8.21 us (8%)
  waiting for transfers between devices  8.07 us (8%)
  local copies, waits for them, and re-layouts  2.13 us (2%)
    all_to_all x3, blocking collectives, exchange(): return lax.all_to_all(data, axes, split_axis=0, concat_axis=0, tiled=True)  74.1 us
    pallas_call x6, Pallas kernels, call(): pl.pallas_call(kernel, out_shape=outs, in_specs=[VMEM] * len(args), out_s...  8.21 us
    ppermute x1, waiting for transfers between devices, transpose_places(): return lax.ppermute(data, AXES, pairs)  8.07 us
    ppermute x1, starting transfers between devices, transpose_places(): return lax.ppermute(data, AXES, pairs)  7.08 us
    all_to_all x1, starting transfers between devices, exchange(): return lax.all_to_all(data, axes, split_axis=0, concat_axis=0, tiled=True)  3.63 us
  transfers between devices with their start and end apart: 3, of which 1 were waited for; matrix products, arithmetic and copies ran while one was open for 0% of the time, Pallas kernels for 2%

profile of v4, /device:TPU:6, one launch (start us, length us, event | category | flops | bytes accessed | tf_op | source)
XLA Modules:
  0.0 105.2 jit_solution(3304328313576457954)
XLA Ops:
  0.0 0.0 copy-start
  0.0 1.2 %copy-done = bf16[128,4096]{1,0:T(8,128)(2,1)S(1)} copy-done((bf16[128,4096]{1,0:T(8,128)(2,1)S(1)}, bf16[128,4096]{1,0:T(8,128)(2,1)}, u32[]{:S(2)}) %copy-start) | copy-done | bytes 1048600
  1.2 0.0 copy-start.1
  1.2 0.9 copy-done.1
  2.1 0.4 shard_map.37
  2.6 46.6 %all_to_all.20.got = bf16[8,688,128]{2,1,0:T(8,128)(2,1)S(1)} all-to-all(bf16[8,688,128]{2,1,0:T(8,128)(2,1)S(1)} %shard_map.37), channel_id=1, replica_groups=mesh['x'=4,'yl'=2,'z'=8,'yh'=4,'c'=2] {'z'}, dimensions={0} | all-to-all | bytes 2818048 | tf_op jit(solution)/shard_map/all_to_all | solution.py:178
  49.1 0.7 shard_map.38
  49.9 14.8 %all_to_all.21.got = f32[8,192,128]{2,1,0:T(8,128)S(1)} all-to-all(f32[8,192,128]{2,1,0:T(8,128)S(1)} %shard_map.38), channel_id=1, replica_groups=mesh['x'=4,'yl'=2,'z'=8,'yh'=4,'c'=2] {'x','yl'}, dimensions={0} | all-to-all | bytes 1572864 | tf_op jit(solution)/shard_map/all_to_all | solution.py:178
  64.7 0.1 shard_map.39
  64.7 12.7 %all_to_all.22.got = f32[8,184,128]{2,1,0:T(8,128)S(1)} all-to-all(f32[8,184,128]{2,1,0:T(8,128)S(1)} %get-tuple-element.9), channel_id=1, replica_groups=mesh['x'=4,'yl'=2,'z'=8,'yh'=4,'c'=2] {'x','yl'}, dimensions={0} | all-to-all | bytes 1507328 | tf_op jit(solution)/shard_map/all_to_all | solution.py:178
  77.5 0.0 copy-start.2
  77.5 2.9 %shard_map.40 = (bf16[640,128]{1,0:T(8,128)(2,1)S(1)}, bf16[8,160,128]{2,1,0:T(8,128)(2,1)}) custom-call(f32[8,184,128]{2,1,0:T(8,128)S(1)} %all_to_all.22.got), custom_call_target="tpu_custom_call" | custom-call | flops 1610612736 | bytes 1245184 | tf_op jit(solution)/shard_map/pallas_call | solution.py:165
  80.4 3.6 %all-to-all-start.3 = ((bf16[8,160,128]{2,1,0:T(8,128)(2,1)}), bf16[8,160,128]{2,1,0:T(8,128)(2,1)S(1)}, u32[]{:S(2)}, u32[]{:S(2)}) async-start(bf16[8,160,128]{2,1,0:T(8,128)(2,1)} %get-tuple-element.10), calls=%async_computation.3 | async-start | bytes 655360 | tf_op jit(solution)/shard_map/all_to_all | solution.py:178
  84.0 7.1 %collective-permute-start = (bf16[640,128]{1,0:T(8,128)(2,1)S(1)}, bf16[640,128]{1,0:T(8,128)(2,1)S(1)}, u32[]{:S(2)}, u32[]{:S(2)}) collective-permute-start(bf16[640,128]{1,0:T(8,128)(2,1)S(1)} %get-tuple-element.12), channel_id=1, source_target_pairs={{0,0},{1,64},{2,130},{3,194},{4,260},{5,324},{6,390},{7,454},{8,8}... | collective-permute-start | bytes 491528 | tf_op jit(solution)/shard_map/ppermute | solution.py:191
  91.1 8.1 %collective-permute-done.mine = bf16[640,128]{1,0:T(8,128)(2,1)S(1)} collective-permute-done((bf16[640,128]{1,0:T(8,128)(2,1)S(1)}, bf16[640,128]{1,0:T(8,128)(2,1)S(1)}, u32[]{:S(2)}, u32[]{:S(2)}) %collective-permute-start) | collective-permute-done | bytes 163872 | tf_op jit(solution)/shard_map/ppermute | solution.py:191
  99.2 1.9 %collective-permute-start.1 = (bf16[640,128]{1,0:T(8,128)(2,1)S(1)}, bf16[640,128]{1,0:T(8,128)(2,1)S(1)}, u32[]{:S(2)}, u32[]{:S(2)}) collective-permute-start(bf16[640,128]{1,0:T(8,128)(2,1)S(1)} %collective-permute-done.mine), channel_id=1, source_target_pairs={{0,1},{1,0},{2,3},{3,2},{4,5},{5,4},{6,7},{7,6},{8,9},{9,8},{10,11... | collective-permute-start | bytes 491528 | tf_op jit(solution)/shard_map/ppermute | solution.py:182
  101.1 0.0 all-to-all-done.3
  101.1 0.0 copy-done.2
  101.1 2.5 %shard_map.41.left = bf16[512,512]{1,0:T(8,128)(2,1)S(1)} custom-call(bf16[1280,128]{1,0:T(8,128)(2,1)S(1)} %bitcast.1, f32[8,128]{1,0:T(8,128)S(1)} %get-tuple-element.11.ends, bf16[512,512]{1,0:T(8,128)(2,1)S(1)} %copy-done.2), custom_call_target="tpu_custom_call" | custom-call | flops 1879048192 | bytes 1380352 | tf_op jit(solution)/shard_map/pallas_call | solution.py:165
  103.7 0.0 collective-permute-done.1.other
  103.7 1.5 %shard_map.42 = f32[512,512]{1,0:T(8,128)} custom-call(bf16[512,512]{1,0:T(8,128)(2,1)S(1)} %shard_map.41.left, bf16[640,128]{1,0:T(8,128)(2,1)S(1)} %collective-permute-done.mine, bf16[640,128]{1,0:T(8,128)(2,1)S(1)} %collective-permute-done.1.other), custom_call_target="tpu_custom_call" | custom-call | flops 268435456 | bytes 1900544 | tf_op jit(solution)/shard_map/pallas_call | solution.py:165
Async XLA Ops:
  0.0 1.2 %copy-start = (bf16[128,4096]{1,0:T(8,128)(2,1)S(1)}, bf16[128,4096]{1,0:T(8,128)(2,1)}, u32[]{:S(2)}) copy-start(bf16[128,4096]{1,0:T(8,128)(2,1)} %grads.1) | copy-start | bytes 3145732
  1.2 0.9 copy-start.1
  77.5 23.7 %copy-start.2 = (bf16[512,512]{1,0:T(8,128)(2,1)S(1)}, bf16[512,512]{1,0:T(8,128)(2,1)}, u32[]{:S(2)}) copy-start(bf16[512,512]{1,0:T(8,128)(2,1)} %grad.1) | copy-start | bytes 1572868
  80.4 20.7 %all-to-all-start.3 = ((bf16[8,160,128]{2,1,0:T(8,128)(2,1)}), bf16[8,160,128]{2,1,0:T(8,128)(2,1)S(1)}, u32[]{:S(2)}, u32[]{:S(2)}) async-start(bf16[8,160,128]{2,1,0:T(8,128)(2,1)} %get-tuple-element.10), calls=%async_computation.3 | async-start | bytes 655360 | tf_op jit(solution)/shard_map/all_to_all | solution.py:178
  84.0 15.2 %collective-permute-start = (bf16[640,128]{1,0:T(8,128)(2,1)S(1)}, bf16[640,128]{1,0:T(8,128)(2,1)S(1)}, u32[]{:S(2)}, u32[]{:S(2)}) collective-permute-start(bf16[640,128]{1,0:T(8,128)(2,1)S(1)} %get-tuple-element.12), channel_id=1, source_target_pairs={{0,0},{1,64},{2,130},{3,194},{4,260},{5,324},{6,390},{7,454},{8,8}... | collective-permute-start | bytes 491528 | tf_op jit(solution)/shard_map/ppermute | solution.py:191
  99.2 4.5 %collective-permute-start.1 = (bf16[640,128]{1,0:T(8,128)(2,1)S(1)}, bf16[640,128]{1,0:T(8,128)(2,1)S(1)}, u32[]{:S(2)}, u32[]{:S(2)}) collective-permute-start(bf16[640,128]{1,0:T(8,128)(2,1)S(1)} %collective-permute-done.mine), channel_id=1, source_target_pairs={{0,1},{1,0},{2,3},{3,2},{4,5},{5,4},{6,7},{7,6},{8,9},{9,8},{10,11... | collective-permute-start | bytes 491528 | tf_op jit(solution)/shard_map/ppermute | solution.py:182

commit v5 on v4

--- a/solution.py
+++ b/solution.py
@@ -16,16 +16,17 @@
 HALF = PACKED // 2
 PEERS = 8
 SHARE = PACKED // PEERS
-PIECE = 24
+PIECE = 32
 RAW = SIDE * TILE
 DIAGONAL = 8
 FIRST = RAW + SHARE + 2 * DIAGONAL
 GATHER = SHARE + PIECE
-SECOND = GATHER + DIAGONAL
+SECOND = GATHER + PIECE + 4 * DIAGONAL
 BF16, F32 = jnp.bfloat16, jnp.float32
 AXES = ("x", "yl", "z", "yh", "c")
 SIZES = (4, 2, 8, 4, 2)
 VMEM = pl.BlockSpec(memory_space=pltpu.VMEM)
+ANYWHERE = pl.BlockSpec(memory_space=pl.ANY)
 PARAMS = pltpu.CompilerParams(vmem_limit_bytes=24 * 1024 * 1024)
 
 
@@ -108,7 +109,8 @@
         [got[:, p * TILE : (p + 1) * TILE, :].reshape(PEERS * TILE, TILE) for p in range(SIDE)],
         axis=1,
     )
-    pack(gram(tokens), packed)
+    grad_total = gram(tokens)
+    pack(grad_total, packed)
     total = jnp.zeros((SHARE, TILE), F32)
     ends = jnp.zeros((2 * DIAGONAL, TILE), F32)
     for peer in range(PEERS):
@@ -116,37 +118,57 @@
         ends += got[peer, RAW + SHARE : FIRST, :].astype(F32)
     share[0:SHARE, :] = total
     share[SHARE:, :] = jnp.zeros((PEERS * PIECE - SHARE, TILE), F32)
-    for peer in range(PEERS):
-        out[peer, 0:SHARE, :] = packed[peer * SHARE : (peer + 1) * SHARE, :]
-        out[peer, SHARE:GATHER, :] = share[peer * PIECE : (peer + 1) * PIECE, :]
-        out[peer, GATHER:SECOND, :] = ends[0:DIAGONAL] + ends[DIAGONAL:]
+    grad_ends = halves(diagonals(grad_total))
+    act_ends = halves(ends[0:DIAGONAL] + ends[DIAGONAL:])
+    both = jnp.concatenate([*grad_ends, *act_ends], axis=0)
+    for peer in range(PEERS):
+        high, low = halves(share[peer * PIECE : (peer + 1) * PIECE, :])
+        out[peer, 0:SHARE, :] = packed[peer * SHARE : (peer + 1) * SHARE, :].astype(BF16)
+        out[peer, SHARE:GATHER, :] = high
+        out[peer, GATHER : GATHER + PIECE, :] = low
+        out[peer, GATHER + PIECE : SECOND, :] = both
 
 
 def sum_kernel(got, out, ends):
-    total = got[0]
+    total = got[0].astype(F32)
     for peer in range(1, PEERS):
-        total += got[peer]
-    for peer in range(PEERS):
-        out[peer] = total[0:GATHER]
-    ends[...] = total[GATHER:SECOND]
-
-
-def grad_root_kernel(got, out, copies, full, packed, half, share):
+        total += got[peer].astype(F32)
+    share = total[0:SHARE].astype(BF16)
+    piece = (total[SHARE:GATHER] + total[GATHER : GATHER + PIECE]).astype(BF16)
+    for peer in range(PEERS):
+        out[peer, 0:SHARE, :] = share
+        out[peer, SHARE:GATHER, :] = piece
+    both = total[GATHER + PIECE : SECOND]
+    ends[0:DIAGONAL, :] = both[0:DIAGONAL] + both[DIAGONAL : 2 * DIAGONAL]
+    ends[DIAGONAL:, :] = both[2 * DIAGONAL : 3 * DIAGONAL] + both[3 * DIAGONAL :]
+
+
+def set_diagonal(full, ends, first):
+    for a in range(SIDE):
+        place = slice(a * TILE, (a + 1) * TILE)
+        exact = ends[first + a : first + a + 1, :]
+        full[place, place] = jnp.where(on_diagonal(TILE), exact, full[place, place])
+
+
+def grad_root_kernel(got, ends, out, full, packed):
     for peer in range(PEERS):
         packed[peer * SHARE : (peer + 1) * SHARE, :] = got[peer, 0:SHARE, :]
-        share[peer * PIECE : (peer + 1) * PIECE, :] = got[peer, SHARE:GATHER, :]
     unpack(packed, full)
-    pack(inverse_root(full[...]), half)
-    out[...] = half[rows(lax.axis_index("yl"), HALF), :]
-    for peer in range(PEERS):
-        copies[peer] = share[0:SHARE, :].astype(BF16)
+    set_diagonal(full, ends, 0)
+    pack(inverse_root(full[...]), packed)
+    out[...] = packed[rows(lax.axis_index("yl"), HALF), :]
+
+
+def copies_kernel(got, out):
+    for place in range(SHARE // PIECE):
+        piece = got[place, SHARE:GATHER, :]
+        for peer in range(PEERS):
+            out[peer, place * PIECE : (place + 1) * PIECE, :] = piece
 
 
 def left_kernel(got, ends, grad, out, full):
     unpack(got, full)
-    for a in range(SIDE):
-        place = slice(a * TILE, (a + 1) * TILE)
-        full[place, place] = jnp.where(on_diagonal(TILE), ends[a : a + 1, :], full[place, place])
+    set_diagonal(full, ends, DIAGONAL)
     root = inverse_root(full[...])
     out[...] = jnp.dot(root, grad[...], preferred_element_type=F32).astype(BF16)
 
@@ -159,18 +181,22 @@
     out[...] = jnp.dot(left[...], full[...], preferred_element_type=F32)
 
 
-def call(kernel, args, outs, scratch=(), flops=1 << 20):
+def call(kernel, args, outs, scratch=(), flops=1 << 20, after=()):
     outs = [jax.ShapeDtypeStruct(dims, dtype) for dims, dtype in outs]
     data = sum(a.size * a.dtype.itemsize for a in [*args, *outs])
+
+    def body(*refs):
+        kernel(*refs[: len(args)], *refs[len(args) + len(after) :])
+
     got = pl.pallas_call(
-        kernel,
+        body,
         out_shape=outs,
-        in_specs=[VMEM] * len(args),
+        in_specs=[VMEM] * len(args) + [ANYWHERE] * len(after),
         out_specs=[VMEM] * len(outs),
         scratch_shapes=[pltpu.VMEM(dims, dtype) for dims, dtype in scratch],
         compiler_params=PARAMS,
         cost_estimate=pl.CostEstimate(flops=flops, bytes_accessed=data, transcendentals=0),
-    )(*args)
+    )(*args, *after)
     return got if len(outs) > 1 else got[0]
 
 
@@ -207,23 +233,24 @@
     sent = call(
         second_kernel,
         [got],
-        [((PEERS, SECOND, TILE), F32)],
+        [((PEERS, SECOND, TILE), BF16)],
         [(packed, F32), (share, F32)],
         2 * cube,
     )
     got = exchange(sent, ("x", "yl"))
     sent, ends = call(
-        sum_kernel, [got], [((PEERS, GATHER, TILE), F32), ((DIAGONAL, TILE), F32)]
+        sum_kernel, [got], [((PEERS, GATHER, TILE), BF16), ((2 * DIAGONAL, TILE), F32)]
     )
     got = exchange(sent, ("x", "yl"))
-    root, sent = call(
+    root = call(
         grad_root_kernel,
-        [got],
-        [((HALF, TILE), BF16), ((PEERS, SHARE, TILE), BF16)],
-        [(full, F32), (packed, F32), (packed, BF16), (share, F32)],
+        [got, ends],
+        [((HALF, TILE), BF16)],
+        [(full, F32), (packed, BF16)],
         6 * cube,
     )
     mine = transpose_places(root)
+    sent = call(copies_kernel, [got], [((PEERS, SHARE, TILE), BF16)], after=[root])
     act_cov = exchange(sent, "z").reshape(packed)
     left = call(left_kernel, [act_cov, ends, grad], [(full, BF16)], [(full, F32)], 7 * cube)
     other = swap(mine, "c", 2, 1)

time: 107 us -> 101 us (0.944); the launches traced: 105 us -> 100 us
  blocking collectives: 74.1 us -> 69.3 us
    all_to_all x3, blocking collectives: 74.1 us -> 69.3 us  [exchange(): return lax.all_to_all(data, axes, split_axis=0, concat_axis=0, tiled=True)]
    pallas_call x6 -> x7, Pallas kernels: 8.21 us -> 8.36 us  [call(): pl.pallas_call(body, out_shape=outs, in_specs=[VMEM] * len(args) + [ANYWH...]
  transfers between devices with their start and end apart: 3 -> 3, of which waited for: 1 -> 1; matrix products, arithmetic and copies ran while one was open for 0% -> 0% of each run, Pallas kernels for 2% -> 3%
where the time goes in v5:
time: 101 us; the launch traced here: 100 us
  blocking collectives  69.3 us (69%)
  starting transfers between devices  12.3 us (12%)
  Pallas kernels  8.36 us (8%)
  waiting for transfers between devices  8.08 us (8%)
  local copies, waits for them, and re-layouts  2.13 us (2%)
    all_to_all x3, blocking collectives, exchange(): return lax.all_to_all(data, axes, split_axis=0, concat_axis=0, tiled=True)  69.3 us
    pallas_call x7, Pallas kernels, call(): pl.pallas_call(body, out_shape=outs, in_specs=[VMEM] * len(args) + [ANYWH...  8.36 us
    ppermute x1, waiting for transfers between devices, transpose_places(): return lax.ppermute(data, AXES, pairs)  8.08 us
    ppermute x1, starting transfers between devices, transpose_places(): return lax.ppermute(data, AXES, pairs)  6.95 us
    all_to_all x1, starting transfers between devices, exchange(): return lax.all_to_all(data, axes, split_axis=0, concat_axis=0, tiled=True)  3.43 us
    unnamed x6, local copies, waits for them, and re-layouts  2.13 us
  transfers between devices with their start and end apart: 3, of which 1 were waited for; matrix products, arithmetic and copies ran while one was open for 0% of the time, Pallas kernels for 3%

profile of v5, /device:TPU:6, one launch (start us, length us, event | category | flops | bytes accessed | tf_op | source)
XLA Modules:
  0.0 100.3 jit_solution(7708400613969740853)
XLA Ops:
  0.0 0.0 copy-start
  0.0 1.2 %copy-done = bf16[128,4096]{1,0:T(8,128)(2,1)S(1)} copy-done((bf16[128,4096]{1,0:T(8,128)(2,1)S(1)}, bf16[128,4096]{1,0:T(8,128)(2,1)}, u32[]{:S(2)}) %copy-start) | copy-done | bytes 1048600
  1.2 0.0 copy-start.1
  1.2 0.9 copy-done.1
  2.1 0.4 shard_map.37
  2.6 46.6 %all_to_all.20.refs_0_ = bf16[8,688,128]{2,1,0:T(8,128)(2,1)S(1)} all-to-all(bf16[8,688,128]{2,1,0:T(8,128)(2,1)S(1)} %shard_map.37), channel_id=1, replica_groups=mesh['x'=4,'yl'=2,'z'=8,'yh'=4,'c'=2] {'z'}, dimensions={0} | all-to-all | bytes 2818048 | tf_op jit(solution)/shard_map/all_to_all | solution.py:204
  49.1 0.8 shard_map.38
  49.9 12.0 %all_to_all.21.refs_0_ = bf16[8,256,128]{2,1,0:T(8,128)(2,1)S(1)} all-to-all(bf16[8,256,128]{2,1,0:T(8,128)(2,1)S(1)} %shard_map.38), channel_id=1, replica_groups=mesh['x'=4,'yl'=2,'z'=8,'yh'=4,'c'=2] {'x','yl'}, dimensions={0} | all-to-all | bytes 1048576 | tf_op jit(solution)/shard_map/all_to_all | solution.py:204
  61.9 0.1 shard_map.39
  62.0 10.7 %all_to_all.22.refs_0_ = bf16[8,192,128]{2,1,0:T(8,128)(2,1)S(1)} all-to-all(bf16[8,192,128]{2,1,0:T(8,128)(2,1)S(1)} %get-tuple-element.7), channel_id=1, replica_groups=mesh['x'=4,'yl'=2,'z'=8,'yh'=4,'c'=2] {'x','yl'}, dimensions={0} | all-to-all | bytes 786432 | tf_op jit(solution)/shard_map/all_to_all | solution.py:204
  72.7 2.3 %shard_map.40.refs_1_ = bf16[640,128]{1,0:T(8,128)(2,1)S(1)} custom-call(bf16[8,192,128]{2,1,0:T(8,128)(2,1)S(1)} %all_to_all.22.refs_0_, f32[16,128]{1,0:T(8,128)S(1)} %get-tuple-element.8.refs_1_), custom_call_target="tpu_custom_call" | custom-call | flops 1610612736 | bytes 565248 | tf_op jit(solution)/shard_map/pallas_call | solution.py:191
  75.0 0.0 copy-start.2
  75.0 0.8 shard_map.41
  75.8 3.4 %all-to-all-start.3 = ((bf16[8,160,128]{2,1,0:T(8,128)(2,1)}), bf16[8,160,128]{2,1,0:T(8,128)(2,1)S(1)}, u32[]{:S(2)}, u32[]{:S(2)}) async-start(bf16[8,160,128]{2,1,0:T(8,128)(2,1)} %shard_map.41), calls=%async_computation.3 | async-start | bytes 655360 | tf_op jit(solution)/shard_map/all_to_all | solution.py:204
  79.2 7.0 %collective-permute-start = (bf16[640,128]{1,0:T(8,128)(2,1)S(1)}, bf16[640,128]{1,0:T(8,128)(2,1)S(1)}, u32[]{:S(2)}, u32[]{:S(2)}) collective-permute-start(bf16[640,128]{1,0:T(8,128)(2,1)S(1)} %shard_map.40.refs_1_), channel_id=1, source_target_pairs={{0,0},{1,64},{2,130},{3,194},{4,260},{5,324},{6,390},{7,454},{8,8}... | collective-permute-start | bytes 491528 | tf_op jit(solution)/shard_map/ppermute | solution.py:217
  86.2 8.1 %collective-permute-done.refs_1_ = bf16[640,128]{1,0:T(8,128)(2,1)S(1)} collective-permute-done((bf16[640,128]{1,0:T(8,128)(2,1)S(1)}, bf16[640,128]{1,0:T(8,128)(2,1)S(1)}, u32[]{:S(2)}, u32[]{:S(2)}) %collective-permute-start) | collective-permute-done | bytes 163872 | tf_op jit(solution)/shard_map/ppermute | solution.py:217
  94.3 1.9 %collective-permute-start.1 = (bf16[640,128]{1,0:T(8,128)(2,1)S(1)}, bf16[640,128]{1,0:T(8,128)(2,1)S(1)}, u32[]{:S(2)}, u32[]{:S(2)}) collective-permute-start(bf16[640,128]{1,0:T(8,128)(2,1)S(1)} %collective-permute-done.refs_1_), channel_id=1, source_target_pairs={{0,1},{1,0},{2,3},{3,2},{4,5},{5,4},{6,7},{7,6},{8,9},{9,8},{10,11... | collective-permute-start | bytes 491528 | tf_op jit(solution)/shard_map/ppermute | solution.py:208
  96.2 0.0 all-to-all-done.3
  96.2 0.0 copy-done.2
  96.2 2.5 %shard_map.42.refs_0_ = bf16[512,512]{1,0:T(8,128)(2,1)S(1)} custom-call(bf16[1280,128]{1,0:T(8,128)(2,1)S(1)} %bitcast.1, f32[16,128]{1,0:T(8,128)S(1)} %get-tuple-element.8.refs_1_, bf16[512,512]{1,0:T(8,128)(2,1)S(1)} %copy-done.2), custom_call_target="tpu_custom_call" | custom-call | flops 1879048192 | bytes 1384448 | tf_op jit(solution)/shard_map/pallas_call | solution.py:191
  98.8 0.0 collective-permute-done.1.refs_2_
  98.8 1.5 %shard_map.43 = f32[512,512]{1,0:T(8,128)} custom-call(bf16[512,512]{1,0:T(8,128)(2,1)S(1)} %shard_map.42.refs_0_, bf16[640,128]{1,0:T(8,128)(2,1)S(1)} %collective-permute-done.refs_1_, bf16[640,128]{1,0:T(8,128)(2,1)S(1)} %collective-permute-done.1.refs_2_), custom_call_target="tpu_custom_call" | custom-call | flops 268435456 | bytes 1900544 | tf_op jit(solution)/shard_map/pallas_call | solution.py:191
Async XLA Ops:
  0.0 1.2 %copy-start = (bf16[128,4096]{1,0:T(8,128)(2,1)S(1)}, bf16[128,4096]{1,0:T(8,128)(2,1)}, u32[]{:S(2)}) copy-start(bf16[128,4096]{1,0:T(8,128)(2,1)} %refs_1_.1) | copy-start | bytes 3145732
  1.2 0.9 copy-start.1
  75.0 21.2 %copy-start.2 = (bf16[512,512]{1,0:T(8,128)(2,1)S(1)}, bf16[512,512]{1,0:T(8,128)(2,1)}, u32[]{:S(2)}) copy-start(bf16[512,512]{1,0:T(8,128)(2,1)} %refs_2_.1) | copy-start | bytes 1572868
  75.8 20.4 %all-to-all-start.3 = ((bf16[8,160,128]{2,1,0:T(8,128)(2,1)}), bf16[8,160,128]{2,1,0:T(8,128)(2,1)S(1)}, u32[]{:S(2)}, u32[]{:S(2)}) async-start(bf16[8,160,128]{2,1,0:T(8,128)(2,1)} %shard_map.41), calls=%async_computation.3 | async-start | bytes 655360 | tf_op jit(solution)/shard_map/all_to_all | solution.py:204
  79.2 15.0 %collective-permute-start = (bf16[640,128]{1,0:T(8,128)(2,1)S(1)}, bf16[640,128]{1,0:T(8,128)(2,1)S(1)}, u32[]{:S(2)}, u32[]{:S(2)}) collective-permute-start(bf16[640,128]{1,0:T(8,128)(2,1)S(1)} %shard_map.40.refs_1_), channel_id=1, source_target_pairs={{0,0},{1,64},{2,130},{3,194},{4,260},{5,324},{6,390},{7,454},{8,8}... | collective-permute-start | bytes 491528 | tf_op jit(solution)/shard_map/ppermute | solution.py:217
  94.3 4.5 %collective-permute-start.1 = (bf16[640,128]{1,0:T(8,128)(2,1)S(1)}, bf16[640,128]{1,0:T(8,128)(2,1)S(1)}, u32[]{:S(2)}, u32[]{:S(2)}) collective-permute-start(bf16[640,128]{1,0:T(8,128)(2,1)S(1)} %collective-permute-done.refs_1_), channel_id=1, source_target_pairs={{0,1},{1,0},{2,3},{3,2},{4,5},{5,4},{6,7},{7,6},{8,9},{9,8},{10,11... | collective-permute-start | bytes 491528 | tf_op jit(solution)/shard_map/ppermute | solution.py:208

commit v6 on v4

--- a/solution.py
+++ b/solution.py
@@ -16,12 +16,11 @@
 HALF = PACKED // 2
 PEERS = 8
 SHARE = PACKED // PEERS
-PIECE = 24
 RAW = SIDE * TILE
 DIAGONAL = 8
 FIRST = RAW + SHARE + 2 * DIAGONAL
-GATHER = SHARE + PIECE
-SECOND = GATHER + DIAGONAL
+SECOND = 2 * SHARE + 4 * DIAGONAL
+COLUMN = SHARE + 2 * DIAGONAL
 BF16, F32 = jnp.bfloat16, jnp.float32
 AXES = ("x", "yl", "z", "yh", "c")
 SIZES = (4, 2, 8, 4, 2)
@@ -103,60 +102,73 @@
         out[peer, RAW + SHARE : FIRST, :] = ends
 
 
-def second_kernel(got, out, packed, share):
+def second_kernel(got, out, packed):
     tokens = jnp.concatenate(
         [got[:, p * TILE : (p + 1) * TILE, :].reshape(PEERS * TILE, TILE) for p in range(SIDE)],
         axis=1,
     )
-    pack(gram(tokens), packed)
+    grad_total = gram(tokens)
+    pack(grad_total, packed)
     total = jnp.zeros((SHARE, TILE), F32)
     ends = jnp.zeros((2 * DIAGONAL, TILE), F32)
     for peer in range(PEERS):
         total += got[peer, RAW : RAW + SHARE, :].astype(F32)
         ends += got[peer, RAW + SHARE : FIRST, :].astype(F32)
-    share[0:SHARE, :] = total
-    share[SHARE:, :] = jnp.zeros((PEERS * PIECE - SHARE, TILE), F32)
-    for peer in range(PEERS):
-        out[peer, 0:SHARE, :] = packed[peer * SHARE : (peer + 1) * SHARE, :]
-        out[peer, SHARE:GATHER, :] = share[peer * PIECE : (peer + 1) * PIECE, :]
-        out[peer, GATHER:SECOND, :] = ends[0:DIAGONAL] + ends[DIAGONAL:]
-
-
-def sum_kernel(got, out, ends):
-    total = got[0]
+    act_share = total.astype(BF16)
+    grad_ends = halves(diagonals(grad_total))
+    act_ends = halves(ends[0:DIAGONAL] + ends[DIAGONAL:])
+    both = jnp.concatenate([*grad_ends, *act_ends], axis=0)
+    for peer in range(PEERS):
+        out[peer, 0:SHARE, :] = packed[peer * SHARE : (peer + 1) * SHARE, :].astype(BF16)
+        out[peer, SHARE : 2 * SHARE, :] = act_share
+        out[peer, 2 * SHARE : SECOND, :] = both
+
+
+def sum_kernel(got, grad_share, copies, ends):
+    total = got[0].astype(F32)
     for peer in range(1, PEERS):
-        total += got[peer]
-    for peer in range(PEERS):
-        out[peer] = total[0:GATHER]
-    ends[...] = total[GATHER:SECOND]
-
-
-def grad_root_kernel(got, out, copies, full, packed, half, share):
-    for peer in range(PEERS):
-        packed[peer * SHARE : (peer + 1) * SHARE, :] = got[peer, 0:SHARE, :]
-        share[peer * PIECE : (peer + 1) * PIECE, :] = got[peer, SHARE:GATHER, :]
-    unpack(packed, full)
-    pack(inverse_root(full[...]), half)
-    out[...] = half[rows(lax.axis_index("yl"), HALF), :]
-    for peer in range(PEERS):
-        copies[peer] = share[0:SHARE, :].astype(BF16)
-
-
-def left_kernel(got, ends, grad, out, full):
-    unpack(got, full)
+        total += got[peer].astype(F32)
+    act_share = total[SHARE : 2 * SHARE].astype(BF16)
+    for peer in range(PEERS):
+        copies[peer] = act_share
+    both = total[2 * SHARE : SECOND]
+    high, low = halves(both[0:DIAGONAL] + both[DIAGONAL : 2 * DIAGONAL])
+    grad_share[0:SHARE, :] = total[0:SHARE].astype(BF16)
+    grad_share[SHARE:, :] = jnp.concatenate([high, low], axis=0)
+    ends[...] = both[2 * DIAGONAL : 3 * DIAGONAL] + both[3 * DIAGONAL :]
+
+
+def set_diagonal(full, ends):
     for a in range(SIDE):
         place = slice(a * TILE, (a + 1) * TILE)
         full[place, place] = jnp.where(on_diagonal(TILE), ends[a : a + 1, :], full[place, place])
+
+
+def join_kernel(*refs):
+    *parts, out = refs
+    for place, part in enumerate(parts):
+        out[place] = part[...]
+
+
+def left_kernel(got, ends, grad, out, full):
+    unpack(got, full)
+    set_diagonal(full, ends[...])
     root = inverse_root(full[...])
     out[...] = jnp.dot(root, grad[...], preferred_element_type=F32).astype(BF16)
 
 
 def last_kernel(left, mine, other, out, packed, full):
     bit = lax.axis_index("c")
-    packed[rows(bit, HALF), :] = mine[...]
-    packed[rows(1 - bit, HALF), :] = other[...]
+    turn = lax.axis_index("yh") - lax.axis_index("x") + 4
+    for step in range(4):
+        owner = 2 * lax.rem(turn + 4 - step, 4)
+        packed[rows(owner + bit, SHARE), :] = mine[step, 0:SHARE, :]
+        packed[rows(owner + 1 - bit, SHARE), :] = other[step, 0:SHARE, :]
     unpack(packed, full)
-    out[...] = jnp.dot(left[...], full[...], preferred_element_type=F32)
+    ends = mine[0, SHARE:COLUMN, :].astype(F32)
+    set_diagonal(full, ends[0:DIAGONAL] + ends[DIAGONAL:])
+    root = inverse_root(full[...])
+    out[...] = jnp.dot(left[...], root, preferred_element_type=F32)
 
 
 def call(kernel, args, outs, scratch=(), flops=1 << 20):
@@ -182,10 +194,10 @@
     return lax.ppermute(data, axis, [(i, i ^ distance) for i in range(size)])
 
 
-def transpose_places(data):
+def to_column(data, step):
     places = np.arange(np.prod(SIZES)).reshape(SIZES)
     pairs = [
-        (int(places[x, yl, z, yh, c]), int(places[yh, c, z, (x + yh) % 4, yl]))
+        (int(places[x, yl, z, yh, c]), int(places[yh, c, z, (x + yh + step) % 4, yl]))
         for x, yl, z, yh, c in np.ndindex(*SIZES)
     ]
     return lax.ppermute(data, AXES, pairs)
@@ -195,7 +207,6 @@
     cube = 2 * BLOCK**3
     packed, full = (PACKED, TILE), (BLOCK, BLOCK)
 
-    share = (PEERS * PIECE, TILE)
     sent = call(
         first_kernel,
         [acts, grads_out],
@@ -207,28 +218,23 @@
     sent = call(
         second_kernel,
         [got],
-        [((PEERS, SECOND, TILE), F32)],
-        [(packed, F32), (share, F32)],
+        [((PEERS, SECOND, TILE), BF16)],
+        [(packed, F32)],
         2 * cube,
     )
     got = exchange(sent, ("x", "yl"))
-    sent, ends = call(
-        sum_kernel, [got], [((PEERS, GATHER, TILE), F32), ((DIAGONAL, TILE), F32)]
-    )
-    got = exchange(sent, ("x", "yl"))
-    root, sent = call(
-        grad_root_kernel,
+    grad_share, sent, ends = call(
+        sum_kernel,
         [got],
-        [((HALF, TILE), BF16), ((PEERS, SHARE, TILE), BF16)],
-        [(full, F32), (packed, F32), (packed, BF16), (share, F32)],
-        6 * cube,
-    )
-    mine = transpose_places(root)
+        [((COLUMN, TILE), BF16), ((PEERS, SHARE, TILE), BF16), ((DIAGONAL, TILE), F32)],
+    )
+    parts = [to_column(grad_share, step) for step in range(4)]
+    mine = call(join_kernel, parts, [((4, COLUMN, TILE), BF16)])
+    other = swap(mine, "c", 2, 1)
     act_cov = exchange(sent, "z").reshape(packed)
     left = call(left_kernel, [act_cov, ends, grad], [(full, BF16)], [(full, F32)], 7 * cube)
-    other = swap(mine, "c", 2, 1)
     return call(
-        last_kernel, [left, mine, other], [(full, F32)], [(packed, BF16), (full, BF16)], cube
+        last_kernel, [left, mine, other], [(full, F32)], [(packed, BF16), (full, F32)], 7 * cube
     )
 
 

time: 107 us -> 106 us (level)
  the two profiles are of different devices: /device:TPU:6 before, /device:TPU:5 now
where the time goes in v6:
time: 106 us
  blocking collectives  58.1 us (55%)
  starting transfers between devices  31.6 us (30%)
  Pallas kernels  8.12 us (8%)
  waiting for transfers between devices  6.01 us (6%)
  local copies, waits for them, and re-layouts  2.13 us (2%)
    all_to_all x2, blocking collectives, exchange(): return lax.all_to_all(data, axes, split_axis=0, concat_axis=0, tiled=True)  58.1 us
    ppermute x4, starting transfers between devices, to_column(): return lax.ppermute(data, AXES, pairs)  22.5 us
    pallas_call x6, Pallas kernels, call(): pl.pallas_call(kernel, out_shape=outs, in_specs=[VMEM] * len(args), out_s...  8.12 us
    ppermute x4, waiting for transfers between devices, to_column(): return lax.ppermute(data, AXES, pairs)  6.01 us
    ppermute x1, starting transfers between devices, swap(): return lax.ppermute(data, axis, [(i, i ^ distance) for i in range(size)])  5.64 us
    all_to_all x1, starting transfers between devices, exchange(): return lax.all_to_all(data, axes, split_axis=0, concat_axis=0, tiled=True)  3.43 us
    unnamed x6, local copies, waits for them, and re-layouts  2.13 us
  transfers between devices with their start and end apart: 6, of which 1 were waited for; matrix products, arithmetic and copies ran while one was open for 0% of the time, Pallas kernels for 2%

profile of v6, /device:TPU:5, one launch (start us, length us, event | category | flops | bytes accessed | tf_op | source)
XLA Modules:
  0.0 106.1 jit_solution(15743470383122803354)
XLA Ops:
  0.0 0.0 copy-start
  0.0 1.2 %copy-done = bf16[128,4096]{1,0:T(8,128)(2,1)S(1)} copy-done((bf16[128,4096]{1,0:T(8,128)(2,1)S(1)}, bf16[128,4096]{1,0:T(8,128)(2,1)}, u32[]{:S(2)}) %copy-start) | copy-done | bytes 1048600
  1.2 0.0 copy-start.1
  1.2 0.9 copy-done.1
  2.1 0.4 shard_map.37
  2.6 45.3 %all_to_all.15.got = bf16[8,688,128]{2,1,0:T(8,128)(2,1)S(1)} all-to-all(bf16[8,688,128]{2,1,0:T(8,128)(2,1)S(1)} %shard_map.37), channel_id=1, replica_groups=mesh['x'=4,'yl'=2,'z'=8,'yh'=4,'c'=2] {'z'}, dimensions={0} | all-to-all | bytes 2818048 | tf_op jit(solution)/shard_map/all_to_all | solution.py:190
  47.8 0.8 shard_map.38
  48.6 0.0 copy-start.2
  48.6 12.8 %all_to_all.16.got = bf16[8,352,128]{2,1,0:T(8,128)(2,1)S(1)} all-to-all(bf16[8,352,128]{2,1,0:T(8,128)(2,1)S(1)} %shard_map.38), channel_id=1, replica_groups=mesh['x'=4,'yl'=2,'z'=8,'yh'=4,'c'=2] {'x','yl'}, dimensions={0} | all-to-all | bytes 1441792 | tf_op jit(solution)/shard_map/all_to_all | solution.py:190
  61.4 0.8 shard_map.39
  62.2 3.4 %all-to-all-start.2 = ((bf16[8,160,128]{2,1,0:T(8,128)(2,1)}), bf16[8,160,128]{2,1,0:T(8,128)(2,1)S(1)}, u32[]{:S(2)}, u32[]{:S(2)}) async-start(bf16[8,160,128]{2,1,0:T(8,128)(2,1)} %get-tuple-element.8), calls=%async_computation.2 | async-start | bytes 655360 | tf_op jit(solution)/shard_map/all_to_all | solution.py:190
  65.6 9.6 %collective-permute-start.3 = (bf16[176,128]{1,0:T(8,128)(2,1)S(1)}, bf16[176,128]{1,0:T(8,128)(2,1)S(1)}, u32[]{:S(2)}, u32[]{:S(2)}) collective-permute-start(bf16[176,128]{1,0:T(8,128)(2,1)S(1)} %get-tuple-element.10), channel_id=1, source_target_pairs={{0,6},{1,70},{2,128},{3,192},{4,258},{5,322},{6,388},{7,452},{8,14... | collective-permute-start | bytes 135176 | tf_op jit(solution)/shard_map/ppermute | solution.py:203
  75.3 1.9 %collective-permute-start.2 = (bf16[176,128]{1,0:T(8,128)(2,1)S(1)}, bf16[176,128]{1,0:T(8,128)(2,1)S(1)}, u32[]{:S(2)}, u32[]{:S(2)}) collective-permute-start(bf16[176,128]{1,0:T(8,128)(2,1)S(1)} %get-tuple-element.10), channel_id=1, source_target_pairs={{0,4},{1,68},{2,134},{3,198},{4,256},{5,320},{6,386},{7,450},{8,12... | collective-permute-start | bytes 135176 | tf_op jit(solution)/shard_map/ppermute | solution.py:203
  77.2 8.6 %collective-permute-start.1 = (bf16[176,128]{1,0:T(8,128)(2,1)S(1)}, bf16[176,128]{1,0:T(8,128)(2,1)S(1)}, u32[]{:S(2)}, u32[]{:S(2)}) collective-permute-start(bf16[176,128]{1,0:T(8,128)(2,1)S(1)} %get-tuple-element.10), channel_id=1, source_target_pairs={{0,2},{1,66},{2,132},{3,196},{4,262},{5,326},{6,384},{7,448},{8,10... | collective-permute-start | bytes 135176 | tf_op jit(solution)/shard_map/ppermute | solution.py:203
  85.8 2.3 %collective-permute-start = (bf16[176,128]{1,0:T(8,128)(2,1)S(1)}, bf16[176,128]{1,0:T(8,128)(2,1)S(1)}, u32[]{:S(2)}, u32[]{:S(2)}) collective-permute-start(bf16[176,128]{1,0:T(8,128)(2,1)S(1)} %get-tuple-element.10), channel_id=1, source_target_pairs={{0,0},{1,64},{2,130},{3,194},{4,260},{5,324},{6,390},{7,454},{8,8}... | collective-permute-start | bytes 135176 | tf_op jit(solution)/shard_map/ppermute | solution.py:203
  88.2 0.0 collective-permute-done.3.refs_3_
  88.2 0.0 collective-permute-done.2.refs_2_
  88.2 0.0 collective-permute-done.1.refs_1_
  88.2 6.0 %collective-permute-done.refs_0_ = bf16[176,128]{1,0:T(8,128)(2,1)S(1)} collective-permute-done((bf16[176,128]{1,0:T(8,128)(2,1)S(1)}, bf16[176,128]{1,0:T(8,128)(2,1)S(1)}, u32[]{:S(2)}, u32[]{:S(2)}) %collective-permute-start) | collective-permute-done | bytes 45088 | tf_op jit(solution)/shard_map/ppermute | solution.py:203
  94.2 5.6 %collective-permute-start.4 = (bf16[4,176,128]{2,1,0:T(8,128)(2,1)S(1)}, bf16[4,176,128]{2,1,0:T(8,128)(2,1)S(1)}, u32[]{:S(2)}, u32[]{:S(2)}) collective-permute-start(bf16[4,176,128]{2,1,0:T(8,128)(2,1)S(1)} %shard_map.41.mine), channel_id=1, source_target_pairs={{0,1},{1,0},{2,3},{3,2},{4,5},{5,4},{6,7},{7,6},{8,9},{9,8},{10,11... | collective-permute-start | bytes 540680 | tf_op jit(solution)/shard_map/ppermute | solution.py:194
  99.9 0.0 all-to-all-done.2
  99.9 0.0 copy-done.2
  99.9 2.5 %shard_map.40.left = bf16[512,512]{1,0:T(8,128)(2,1)S(1)} custom-call(bf16[1280,128]{1,0:T(8,128)(2,1)S(1)} %bitcast.1, f32[8,128]{1,0:T(8,128)S(1)} %get-tuple-element.9.ends, bf16[512,512]{1,0:T(8,128)(2,1)S(1)} %copy-done.2), custom_call_target="tpu_custom_call" | custom-call | flops 1879048192 | bytes 1380352 | tf_op jit(solution)/shard_map/pallas_call | solution.py:177
  102.4 0.0 collective-permute-done.4.other
  102.5 3.6 %shard_map.42 = f32[512,512]{1,0:T(8,128)} custom-call(bf16[512,512]{1,0:T(8,128)(2,1)S(1)} %shard_map.40.left, bf16[4,176,128]{2,1,0:T(8,128)(2,1)S(1)} %shard_map.41.mine, bf16[4,176,128]{2,1,0:T(8,128)(2,1)S(1)} %collective-permute-done.4.other), custom_call_target="tpu_custom_call" | custom-call | flops 1879048192 | bytes 1933312 | tf_op jit(solution)/shard_map/pallas_call | solution.py:177
  (1 shorter events, 0.0 us)
Async XLA Ops:
  0.0 1.2 %copy-start = (bf16[128,4096]{1,0:T(8,128)(2,1)S(1)}, bf16[128,4096]{1,0:T(8,128)(2,1)}, u32[]{:S(2)}) copy-start(bf16[128,4096]{1,0:T(8,128)(2,1)} %grads.1) | copy-start | bytes 3145732
  1.2 0.9 copy-start.1
  48.6 51.3 %copy-start.2 = (bf16[512,512]{1,0:T(8,128)(2,1)S(1)}, bf16[512,512]{1,0:T(8,128)(2,1)}, u32[]{:S(2)}) copy-start(bf16[512,512]{1,0:T(8,128)(2,1)} %grad.1) | copy-start | bytes 1572868
  62.2 37.7 %all-to-all-start.2 = ((bf16[8,160,128]{2,1,0:T(8,128)(2,1)}), bf16[8,160,128]{2,1,0:T(8,128)(2,1)S(1)}, u32[]{:S(2)}, u32[]{:S(2)}) async-start(bf16[8,160,128]{2,1,0:T(8,128)(2,1)} %get-tuple-element.8), calls=%async_computation.2 | async-start | bytes 655360 | tf_op jit(solution)/shard_map/all_to_all | solution.py:190
  65.6 22.5 %collective-permute-start.3 = (bf16[176,128]{1,0:T(8,128)(2,1)S(1)}, bf16[176,128]{1,0:T(8,128)(2,1)S(1)}, u32[]{:S(2)}, u32[]{:S(2)}) collective-permute-start(bf16[176,128]{1,0:T(8,128)(2,1)S(1)} %get-tuple-element.10), channel_id=1, source_target_pairs={{0,6},{1,70},{2,128},{3,192},{4,258},{5,322},{6,388},{7,452},{8,14... | collective-permute-start | bytes 135176 | tf_op jit(solution)/shard_map/ppermute | solution.py:203
  75.3 12.9 %collective-permute-start.2 = (bf16[176,128]{1,0:T(8,128)(2,1)S(1)}, bf16[176,128]{1,0:T(8,128)(2,1)S(1)}, u32[]{:S(2)}, u32[]{:S(2)}) collective-permute-start(bf16[176,128]{1,0:T(8,128)(2,1)S(1)} %get-tuple-element.10), channel_id=1, source_target_pairs={{0,4},{1,68},{2,134},{3,198},{4,256},{5,320},{6,386},{7,450},{8,12... | collective-permute-start | bytes 135176 | tf_op jit(solution)/shard_map/ppermute | solution.py:203
  77.2 11.0 %collective-permute-start.1 = (bf16[176,128]{1,0:T(8,128)(2,1)S(1)}, bf16[176,128]{1,0:T(8,128)(2,1)S(1)}, u32[]{:S(2)}, u32[]{:S(2)}) collective-permute-start(bf16[176,128]{1,0:T(8,128)(2,1)S(1)} %get-tuple-element.10), channel_id=1, source_target_pairs={{0,2},{1,66},{2,132},{3,196},{4,262},{5,326},{6,384},{7,448},{8,10... | collective-permute-start | bytes 135176 | tf_op jit(solution)/shard_map/ppermute | solution.py:203
  85.8 8.4 %collective-permute-start = (bf16[176,128]{1,0:T(8,128)(2,1)S(1)}, bf16[176,128]{1,0:T(8,128)(2,1)S(1)}, u32[]{:S(2)}, u32[]{:S(2)}) collective-permute-start(bf16[176,128]{1,0:T(8,128)(2,1)S(1)} %get-tuple-element.10), channel_id=1, source_target_pairs={{0,0},{1,64},{2,130},{3,194},{4,260},{5,324},{6,390},{7,454},{8,8}... | collective-permute-start | bytes 135176 | tf_op jit(solution)/shard_map/ppermute | solution.py:203
  94.2 8.2 %collective-permute-start.4 = (bf16[4,176,128]{2,1,0:T(8,128)(2,1)S(1)}, bf16[4,176,128]{2,1,0:T(8,128)(2,1)S(1)}, u32[]{:S(2)}, u32[]{:S(2)}) collective-permute-start(bf16[4,176,128]{2,1,0:T(8,128)(2,1)S(1)} %shard_map.41.mine), channel_id=1, source_target_pairs={{0,1},{1,0},{2,3},{3,2},{4,5},{5,4},{6,7},{7,6},{8,9},{9,8},{10,11... | collective-permute-start | bytes 540680 | tf_op jit(solution)/shard_map/ppermute | solution.py:194

commit v7 on v5

--- a/solution.py
+++ b/solution.py
@@ -11,17 +11,19 @@
 BLOCK = 512
 TILE = 128
 SIDE = BLOCK // TILE
-TILES = [(a, b) for a in range(SIDE) for b in range(a, SIDE)]
-PACKED = len(TILES) * TILE
+UPPER = [(a, b) for a in range(SIDE) for b in range(a + 1, SIDE)]
+PAIRS = range(0, SIDE, 2)
+PACKED = (len(UPPER) + len(PAIRS)) * TILE
 HALF = PACKED // 2
 PEERS = 8
 SHARE = PACKED // PEERS
-PIECE = 32
+PIECE = SHARE // PEERS
 RAW = SIDE * TILE
 DIAGONAL = 8
 FIRST = RAW + SHARE + 2 * DIAGONAL
 GATHER = SHARE + PIECE
 SECOND = GATHER + PIECE + 4 * DIAGONAL
+ROOT = HALF + 2 * DIAGONAL
 BF16, F32 = jnp.bfloat16, jnp.float32
 AXES = ("x", "yl", "z", "yh", "c")
 SIZES = (4, 2, 8, 4, 2)
@@ -34,18 +36,36 @@
     return lax.dot_general(data, data, (((0,), (0,)), ((), ())), preferred_element_type=F32)
 
 
+def tile_at(a, b):
+    return slice(a * TILE, (a + 1) * TILE), slice(b * TILE, (b + 1) * TILE)
+
+
+def over_diagonal():
+    row = lax.broadcasted_iota(jnp.int32, (TILE, TILE), 0)
+    return row < lax.broadcasted_iota(jnp.int32, (TILE, TILE), 1)
+
+
 def pack(total, packed):
-    for place, (a, b) in enumerate(TILES):
-        tile = total[a * TILE : (a + 1) * TILE, b * TILE : (b + 1) * TILE]
-        packed[place * TILE : (place + 1) * TILE, :] = tile
-
-
-def unpack(packed, full):
-    for place, (a, b) in enumerate(TILES):
-        tile = packed[place * TILE : (place + 1) * TILE, :].astype(full.dtype)
-        full[a * TILE : (a + 1) * TILE, b * TILE : (b + 1) * TILE] = tile
-        if a != b:
-            full[b * TILE : (b + 1) * TILE, a * TILE : (a + 1) * TILE] = tile.T
+    tiles = [total[tile_at(a, b)] for a, b in UPPER]
+    for a in PAIRS:
+        first, second = total[tile_at(a, a)], total[tile_at(a + 1, a + 1)]
+        tiles.append(jnp.where(over_diagonal(), first, second))
+    for place, tile in enumerate(tiles):
+        packed[place * TILE : (place + 1) * TILE, :] = tile.astype(packed.dtype)
+
+
+def unpack(packed, full, ends):
+    tiles = [packed[start : start + TILE, :].astype(F32) for start in range(0, PACKED, TILE)]
+    for (a, b), tile in zip(UPPER, tiles):
+        full[tile_at(a, b)] = tile.astype(full.dtype)
+        full[tile_at(b, a)] = tile.T.astype(full.dtype)
+    for a, tile in zip(PAIRS, tiles[len(UPPER) :]):
+        turned = tile.T
+        both = (tile, turned), (turned, tile)
+        for place, (above, below) in enumerate(both, start=a):
+            whole = jnp.where(over_diagonal(), above, below)
+            whole = jnp.where(on_diagonal(TILE), ends[place : place + 1, :], whole)
+            full[tile_at(place, place)] = whole.astype(full.dtype)
 
 
 def rows(bit, count):
@@ -72,8 +92,8 @@
 def diagonals(total):
     parts = []
     for a in range(SIDE):
-        tile = total[a * TILE : (a + 1) * TILE, a * TILE : (a + 1) * TILE]
-        parts.append(jnp.sum(jnp.where(on_diagonal(TILE), tile, 0.0), axis=0, keepdims=True))
+        tile = jnp.where(on_diagonal(TILE), total[tile_at(a, a)], 0.0)
+        parts.append(jnp.sum(tile, axis=0, keepdims=True))
     return jnp.concatenate(parts + [jnp.zeros((DIAGONAL - SIDE, TILE), F32)], axis=0)
 
 
@@ -87,7 +107,7 @@
     s = product(y_halves, y_halves)
     tail = product(halves(s), halves(0.0625 * s - 0.5625 * y))
     z = jnp.where(diagonal, 2.25, 0.0) - 2.4375 * y + 1.6875 * s + tail
-    return (z * (1.0 / jnp.sqrt(frob))).astype(BF16)
+    return z * (1.0 / jnp.sqrt(frob))
 
 
 def first_kernel(acts, grads, out, packed):
@@ -116,8 +136,7 @@
     for peer in range(PEERS):
         total += got[peer, RAW : RAW + SHARE, :].astype(F32)
         ends += got[peer, RAW + SHARE : FIRST, :].astype(F32)
-    share[0:SHARE, :] = total
-    share[SHARE:, :] = jnp.zeros((PEERS * PIECE - SHARE, TILE), F32)
+    share[...] = total
     grad_ends = halves(diagonals(grad_total))
     act_ends = halves(ends[0:DIAGONAL] + ends[DIAGONAL:])
     both = jnp.concatenate([*grad_ends, *act_ends], axis=0)
@@ -143,41 +162,35 @@
     ends[DIAGONAL:, :] = both[2 * DIAGONAL : 3 * DIAGONAL] + both[3 * DIAGONAL :]
 
 
-def set_diagonal(full, ends, first):
-    for a in range(SIDE):
-        place = slice(a * TILE, (a + 1) * TILE)
-        exact = ends[first + a : first + a + 1, :]
-        full[place, place] = jnp.where(on_diagonal(TILE), exact, full[place, place])
-
-
 def grad_root_kernel(got, ends, out, full, packed):
     for peer in range(PEERS):
         packed[peer * SHARE : (peer + 1) * SHARE, :] = got[peer, 0:SHARE, :]
-    unpack(packed, full)
-    set_diagonal(full, ends, 0)
-    pack(inverse_root(full[...]), packed)
-    out[...] = packed[rows(lax.axis_index("yl"), HALF), :]
+    unpack(packed, full, ends[0:DIAGONAL, :])
+    root = inverse_root(full[...])
+    pack(root, packed)
+    out[0:HALF, :] = packed[rows(lax.axis_index("yl"), HALF), :]
+    root_ends = diagonals(root)
+    out[HALF:, :] = jnp.concatenate([root_ends, root_ends], axis=0).astype(BF16)
 
 
 def copies_kernel(got, out):
-    for place in range(SHARE // PIECE):
+    for place in range(PEERS):
         piece = got[place, SHARE:GATHER, :]
         for peer in range(PEERS):
             out[peer, place * PIECE : (place + 1) * PIECE, :] = piece
 
 
 def left_kernel(got, ends, grad, out, full):
-    unpack(got, full)
-    set_diagonal(full, ends, DIAGONAL)
-    root = inverse_root(full[...])
+    unpack(got, full, ends[DIAGONAL:, :])
+    root = inverse_root(full[...]).astype(BF16)
     out[...] = jnp.dot(root, grad[...], preferred_element_type=F32).astype(BF16)
 
 
 def last_kernel(left, mine, other, out, packed, full):
     bit = lax.axis_index("c")
-    packed[rows(bit, HALF), :] = mine[...]
-    packed[rows(1 - bit, HALF), :] = other[...]
-    unpack(packed, full)
+    packed[rows(bit, HALF), :] = mine[0:HALF, :]
+    packed[rows(1 - bit, HALF), :] = other[0:HALF, :]
+    unpack(packed, full, mine[HALF:ROOT, :].astype(F32))
     out[...] = jnp.dot(left[...], full[...], preferred_element_type=F32)
 
 
@@ -221,7 +234,7 @@
     cube = 2 * BLOCK**3
     packed, full = (PACKED, TILE), (BLOCK, BLOCK)
 
-    share = (PEERS * PIECE, TILE)
+    share = (SHARE, TILE)
     sent = call(
         first_kernel,
         [acts, grads_out],
@@ -245,7 +258,7 @@
     root = call(
         grad_root_kernel,
         [got, ends],
-        [((HALF, TILE), BF16)],
+        [((ROOT, TILE), BF16)],
         [(full, F32), (packed, BF16)],
         6 * cube,
     )

time: 101 us -> 99.4 us (0.984)
  the two profiles are of different devices: /device:TPU:6 before, /device:TPU:33 now
where the time goes in v7:
time: 99.4 us; the launch traced here: 99 us
  blocking collectives  62.9 us (63%)
  starting transfers between devices  19.9 us (20%)
  Pallas kernels  8.63 us (9%)
  waiting for transfers between devices  5.36 us (5%)
  local copies, waits for them, and re-layouts  2.13 us (2%)
    all_to_all x3, blocking collectives, exchange(): return lax.all_to_all(data, axes, split_axis=0, concat_axis=0, tiled=True)  62.9 us
    pallas_call x7, Pallas kernels, call(): pl.pallas_call(body, out_shape=outs, in_specs=[VMEM] * len(args) + [ANYWH...  8.63 us
    ppermute x1, starting transfers between devices, swap(): return lax.ppermute(data, axis, [(i, i ^ distance) for i in range(size)])  8.47 us
    ppermute x1, starting transfers between devices, transpose_places(): return lax.ppermute(data, AXES, pairs)  7.82 us
    ppermute x1, waiting for transfers between devices, transpose_places(): return lax.ppermute(data, AXES, pairs)  5.35 us
    all_to_all x1, starting transfers between devices, exchange(): return lax.all_to_all(data, axes, split_axis=0, concat_axis=0, tiled=True)  3.6 us
    unnamed x6, local copies, waits for them, and re-layouts  2.13 us
  transfers between devices with their start and end apart: 3, of which 1 were waited for; matrix products, arithmetic and copies ran while one was open for 0% of the time, Pallas kernels for 3%

profile of v7, /device:TPU:33, one launch (start us, length us, event | category | flops | bytes accessed | tf_op | source)
XLA Modules:
  0.0 99.0 jit_solution(18262259478382298412)
XLA Ops:
  0.0 0.0 copy-start
  0.0 1.2 %copy-done = bf16[128,4096]{1,0:T(8,128)(2,1)S(1)} copy-done((bf16[128,4096]{1,0:T(8,128)(2,1)S(1)}, bf16[128,4096]{1,0:T(8,128)(2,1)}, u32[]{:S(2)}) %copy-start) | copy-done | bytes 1048600
  1.2 0.0 copy-start.1
  1.2 0.9 copy-done.1
  2.1 0.4 shard_map.37
  2.6 43.2 %all_to_all.20.refs_0_ = bf16[8,656,128]{2,1,0:T(8,128)(2,1)S(1)} all-to-all(bf16[8,656,128]{2,1,0:T(8,128)(2,1)S(1)} %shard_map.37), channel_id=1, replica_groups=mesh['x'=4,'yl'=2,'z'=8,'yh'=4,'c'=2] {'z'}, dimensions={0} | all-to-all | bytes 2686976 | tf_op jit(solution)/shard_map/all_to_all | solution.py:217
  45.7 0.8 shard_map.38
  46.5 10.8 %all_to_all.21.refs_0_ = bf16[8,192,128]{2,1,0:T(8,128)(2,1)S(1)} all-to-all(bf16[8,192,128]{2,1,0:T(8,128)(2,1)S(1)} %shard_map.38), channel_id=1, replica_groups=mesh['x'=4,'yl'=2,'z'=8,'yh'=4,'c'=2] {'x','yl'}, dimensions={0} | all-to-all | bytes 786432 | tf_op jit(solution)/shard_map/all_to_all | solution.py:217
  57.3 0.1 shard_map.39
  57.4 8.9 %all_to_all.22.refs_0_ = bf16[8,144,128]{2,1,0:T(8,128)(2,1)S(1)} all-to-all(bf16[8,144,128]{2,1,0:T(8,128)(2,1)S(1)} %get-tuple-element.7), channel_id=1, replica_groups=mesh['x'=4,'yl'=2,'z'=8,'yh'=4,'c'=2] {'x','yl'}, dimensions={0} | all-to-all | bytes 589824 | tf_op jit(solution)/shard_map/all_to_all | solution.py:217
  66.3 0.0 copy-start.2
  66.3 2.4 %shard_map.40.refs_1_ = bf16[528,128]{1,0:T(8,128)(2,1)S(1)} custom-call(bf16[8,144,128]{2,1,0:T(8,128)(2,1)S(1)} %all_to_all.22.refs_0_, f32[16,128]{1,0:T(8,128)S(1)} %get-tuple-element.8.refs_1_), custom_call_target="tpu_custom_call" | custom-call | flops 1610612736 | bytes 438272 | tf_op jit(solution)/shard_map/pallas_call | solution.py:204
  68.7 0.7 shard_map.41
  69.5 3.6 %all-to-all-start.3 = ((bf16[8,128,128]{2,1,0:T(8,128)(2,1)}), bf16[8,128,128]{2,1,0:T(8,128)(2,1)S(1)}, u32[]{:S(2)}, u32[]{:S(2)}) async-start(bf16[8,128,128]{2,1,0:T(8,128)(2,1)} %shard_map.41), calls=%async_computation.3 | async-start | bytes 524288 | tf_op jit(solution)/shard_map/all_to_all | solution.py:217
  73.1 7.8 %collective-permute-start = (bf16[528,128]{1,0:T(8,128)(2,1)S(1)}, bf16[528,128]{1,0:T(8,128)(2,1)S(1)}, u32[]{:S(2)}, u32[]{:S(2)}) collective-permute-start(bf16[528,128]{1,0:T(8,128)(2,1)S(1)} %shard_map.40.refs_1_), channel_id=1, source_target_pairs={{0,0},{1,64},{2,130},{3,194},{4,260},{5,324},{6,390},{7,454},{8,8}... | collective-permute-start | bytes 405512 | tf_op jit(solution)/shard_map/ppermute | solution.py:230
  80.9 5.4 %collective-permute-done.refs_1_ = bf16[528,128]{1,0:T(8,128)(2,1)S(1)} collective-permute-done((bf16[528,128]{1,0:T(8,128)(2,1)S(1)}, bf16[528,128]{1,0:T(8,128)(2,1)S(1)}, u32[]{:S(2)}, u32[]{:S(2)}) %collective-permute-start) | collective-permute-done | bytes 135200 | tf_op jit(solution)/shard_map/ppermute | solution.py:230
  86.3 8.5 %collective-permute-start.1 = (bf16[528,128]{1,0:T(8,128)(2,1)S(1)}, bf16[528,128]{1,0:T(8,128)(2,1)S(1)}, u32[]{:S(2)}, u32[]{:S(2)}) collective-permute-start(bf16[528,128]{1,0:T(8,128)(2,1)S(1)} %collective-permute-done.refs_1_), channel_id=1, source_target_pairs={{0,1},{1,0},{2,3},{3,2},{4,5},{5,4},{6,7},{7,6},{8,9},{9,8},{10,11... | collective-permute-start | bytes 405512 | tf_op jit(solution)/shard_map/ppermute | solution.py:221
  94.7 0.0 all-to-all-done.3
  94.7 0.0 copy-done.2
  94.8 2.6 %shard_map.42.refs_0_ = bf16[512,512]{1,0:T(8,128)(2,1)S(1)} custom-call(bf16[1024,128]{1,0:T(8,128)(2,1)S(1)} %bitcast.1, f32[16,128]{1,0:T(8,128)S(1)} %get-tuple-element.8.refs_1_, bf16[512,512]{1,0:T(8,128)(2,1)S(1)} %copy-done.2), custom_call_target="tpu_custom_call" | custom-call | flops 1879048192 | bytes 1318912 | tf_op jit(solution)/shard_map/pallas_call | solution.py:204
  97.4 0.0 collective-permute-done.1.refs_2_
  97.4 1.6 %shard_map.43 = f32[512,512]{1,0:T(8,128)} custom-call(bf16[512,512]{1,0:T(8,128)(2,1)S(1)} %shard_map.42.refs_0_, bf16[528,128]{1,0:T(8,128)(2,1)S(1)} %collective-permute-done.refs_1_, bf16[528,128]{1,0:T(8,128)(2,1)S(1)} %collective-permute-done.1.refs_2_), custom_call_target="tpu_custom_call" | custom-call | flops 268435456 | bytes 1843200 | tf_op jit(solution)/shard_map/pallas_call | solution.py:204
Async XLA Ops:
  0.0 1.2 %copy-start = (bf16[128,4096]{1,0:T(8,128)(2,1)S(1)}, bf16[128,4096]{1,0:T(8,128)(2,1)}, u32[]{:S(2)}) copy-start(bf16[128,4096]{1,0:T(8,128)(2,1)} %refs_1_.1) | copy-start | bytes 3145732
  1.2 0.9 copy-start.1
  66.3 28.4 %copy-start.2 = (bf16[512,512]{1,0:T(8,128)(2,1)S(1)}, bf16[512,512]{1,0:T(8,128)(2,1)}, u32[]{:S(2)}) copy-start(bf16[512,512]{1,0:T(8,128)(2,1)} %refs_2_.1) | copy-start | bytes 1572868
  69.5 25.3 %all-to-all-start.3 = ((bf16[8,128,128]{2,1,0:T(8,128)(2,1)}), bf16[8,128,128]{2,1,0:T(8,128)(2,1)S(1)}, u32[]{:S(2)}, u32[]{:S(2)}) async-start(bf16[8,128,128]{2,1,0:T(8,128)(2,1)} %shard_map.41), calls=%async_computation.3 | async-start | bytes 524288 | tf_op jit(solution)/shard_map/all_to_all | solution.py:217
  73.1 13.2 %collective-permute-start = (bf16[528,128]{1,0:T(8,128)(2,1)S(1)}, bf16[528,128]{1,0:T(8,128)(2,1)S(1)}, u32[]{:S(2)}, u32[]{:S(2)}) collective-permute-start(bf16[528,128]{1,0:T(8,128)(2,1)S(1)} %shard_map.40.refs_1_), channel_id=1, source_target_pairs={{0,0},{1,64},{2,130},{3,194},{4,260},{5,324},{6,390},{7,454},{8,8}... | collective-permute-start | bytes 405512 | tf_op jit(solution)/shard_map/ppermute | solution.py:230
  86.3 11.2 %collective-permute-start.1 = (bf16[528,128]{1,0:T(8,128)(2,1)S(1)}, bf16[528,128]{1,0:T(8,128)(2,1)S(1)}, u32[]{:S(2)}, u32[]{:S(2)}) collective-permute-start(bf16[528,128]{1,0:T(8,128)(2,1)S(1)} %collective-permute-done.refs_1_), channel_id=1, source_target_pairs={{0,1},{1,0},{2,3},{3,2},{4,5},{5,4},{6,7},{7,6},{8,9},{9,8},{10,11... | collective-permute-start | bytes 405512 | tf_op jit(solution)/shard_map/ppermute | solution.py:221

commit v8 on v7

--- a/solution.py
+++ b/solution.py
@@ -14,7 +14,6 @@
 UPPER = [(a, b) for a in range(SIDE) for b in range(a + 1, SIDE)]
 PAIRS = range(0, SIDE, 2)
 PACKED = (len(UPPER) + len(PAIRS)) * TILE
-HALF = PACKED // 2
 PEERS = 8
 SHARE = PACKED // PEERS
 PIECE = SHARE // PEERS
@@ -23,7 +22,7 @@
 FIRST = RAW + SHARE + 2 * DIAGONAL
 GATHER = SHARE + PIECE
 SECOND = GATHER + PIECE + 4 * DIAGONAL
-ROOT = HALF + 2 * DIAGONAL
+ROOT = PACKED + 2 * DIAGONAL
 BF16, F32 = jnp.bfloat16, jnp.float32
 AXES = ("x", "yl", "z", "yh", "c")
 SIZES = (4, 2, 8, 4, 2)
@@ -68,10 +67,6 @@
             full[tile_at(place, place)] = whole.astype(full.dtype)
 
 
-def rows(bit, count):
-    return pl.ds(pl.multiple_of(bit * count, count), count)
-
-
 def halves(values):
     high = values.astype(BF16)
     return high, (values - high.astype(F32)).astype(BF16)
@@ -167,10 +162,9 @@
         packed[peer * SHARE : (peer + 1) * SHARE, :] = got[peer, 0:SHARE, :]
     unpack(packed, full, ends[0:DIAGONAL, :])
     root = inverse_root(full[...])
-    pack(root, packed)
-    out[0:HALF, :] = packed[rows(lax.axis_index("yl"), HALF), :]
+    pack(root, out)
     root_ends = diagonals(root)
-    out[HALF:, :] = jnp.concatenate([root_ends, root_ends], axis=0).astype(BF16)
+    out[PACKED:, :] = jnp.concatenate([root_ends, root_ends], axis=0).astype(BF16)
 
 
 def copies_kernel(got, out):
@@ -186,11 +180,8 @@
     out[...] = jnp.dot(root, grad[...], preferred_element_type=F32).astype(BF16)
 
 
-def last_kernel(left, mine, other, out, packed, full):
-    bit = lax.axis_index("c")
-    packed[rows(bit, HALF), :] = mine[0:HALF, :]
-    packed[rows(1 - bit, HALF), :] = other[0:HALF, :]
-    unpack(packed, full, mine[HALF:ROOT, :].astype(F32))
+def last_kernel(left, root, out, full):
+    unpack(root, full, root[PACKED:, :].astype(F32))
     out[...] = jnp.dot(left[...], full[...], preferred_element_type=F32)
 
 
@@ -217,10 +208,6 @@
     return lax.all_to_all(data, axes, split_axis=0, concat_axis=0, tiled=True)
 
 
-def swap(data, axis, size, distance):
-    return lax.ppermute(data, axis, [(i, i ^ distance) for i in range(size)])
-
-
 def transpose_places(data):
     places = np.arange(np.prod(SIZES)).reshape(SIZES)
     pairs = [
@@ -262,14 +249,11 @@
         [(full, F32), (packed, BF16)],
         6 * cube,
     )
-    mine = transpose_places(root)
+    grad_root = transpose_places(root)
     sent = call(copies_kernel, [got], [((PEERS, SHARE, TILE), BF16)], after=[root])
     act_cov = exchange(sent, "z").reshape(packed)
     left = call(left_kernel, [act_cov, ends, grad], [(full, BF16)], [(full, F32)], 7 * cube)
-    other = swap(mine, "c", 2, 1)
-    return call(
-        last_kernel, [left, mine, other], [(full, F32)], [(packed, BF16), (full, BF16)], cube
-    )
+    return call(last_kernel, [left, grad_root], [(full, F32)], [(full, BF16)], cube)
 
 
 def solution(mesh):

time: 99.4 us -> 97.3 us (0.979)
  the two profiles are of different devices: /device:TPU:33 before, /device:TPU:6 now
where the time goes in v8:
time: 97.3 us; the launch traced here: 96.4 us
  blocking collectives  66.9 us (69%)
  starting transfers between devices  10.2 us (10%)
  waiting for transfers between devices  8.6 us (9%)
  Pallas kernels  8.54 us (9%)
  local copies, waits for them, and re-layouts  2.13 us (2%)
    all_to_all x3, blocking collectives, exchange(): return lax.all_to_all(data, axes, split_axis=0, concat_axis=0, tiled=True)  66.9 us
    pallas_call x7, Pallas kernels, call(): pl.pallas_call(body, out_shape=outs, in_specs=[VMEM] * len(args) + [ANYWH...  8.54 us
    ppermute x1, starting transfers between devices, transpose_places(): return lax.ppermute(data, AXES, pairs)  6.77 us
    ppermute x1, waiting for transfers between devices, transpose_places(): return lax.ppermute(data, AXES, pairs)  4.99 us
    all_to_all x1, waiting for transfers between devices, exchange(): return lax.all_to_all(data, axes, split_axis=0, concat_axis=0, tiled=True)  3.61 us
    all_to_all x1, starting transfers between devices, exchange(): return lax.all_to_all(data, axes, split_axis=0, concat_axis=0, tiled=True)  3.41 us
    unnamed x6, local copies, waits for them, and re-layouts  2.13 us
  transfers between devices with their start and end apart: 2, of which 2 were waited for; matrix products, arithmetic and copies ran while one was open for 0% of the time, Pallas kernels for 3%

profile of v8, /device:TPU:6, one launch (start us, length us, event | category | flops | bytes accessed | tf_op | source)
XLA Modules:
  0.0 96.4 jit_solution(3007060039787145702)
XLA Ops:
  0.0 0.0 copy-start
  0.0 1.2 %copy-done = bf16[128,4096]{1,0:T(8,128)(2,1)S(1)} copy-done((bf16[128,4096]{1,0:T(8,128)(2,1)S(1)}, bf16[128,4096]{1,0:T(8,128)(2,1)}, u32[]{:S(2)}) %copy-start) | copy-done | bytes 1048600
  1.2 0.0 copy-start.1
  1.2 0.9 copy-done.1
  2.1 0.4 shard_map.37
  2.6 45.2 %all_to_all.20.refs_0_ = bf16[8,656,128]{2,1,0:T(8,128)(2,1)S(1)} all-to-all(bf16[8,656,128]{2,1,0:T(8,128)(2,1)S(1)} %shard_map.37), channel_id=1, replica_groups=mesh['x'=4,'yl'=2,'z'=8,'yh'=4,'c'=2] {'z'}, dimensions={0} | all-to-all | bytes 2686976 | tf_op jit(solution)/shard_map/all_to_all | solution.py:208
  47.7 0.8 shard_map.38
  48.5 11.4 %all_to_all.21.refs_0_ = bf16[8,192,128]{2,1,0:T(8,128)(2,1)S(1)} all-to-all(bf16[8,192,128]{2,1,0:T(8,128)(2,1)S(1)} %shard_map.38), channel_id=1, replica_groups=mesh['x'=4,'yl'=2,'z'=8,'yh'=4,'c'=2] {'x','yl'}, dimensions={0} | all-to-all | bytes 786432 | tf_op jit(solution)/shard_map/all_to_all | solution.py:208
  59.9 0.1 shard_map.39
  60.0 10.3 %all_to_all.22.refs_0_ = bf16[8,144,128]{2,1,0:T(8,128)(2,1)S(1)} all-to-all(bf16[8,144,128]{2,1,0:T(8,128)(2,1)S(1)} %get-tuple-element.7), channel_id=1, replica_groups=mesh['x'=4,'yl'=2,'z'=8,'yh'=4,'c'=2] {'x','yl'}, dimensions={0} | all-to-all | bytes 589824 | tf_op jit(solution)/shard_map/all_to_all | solution.py:208
  70.3 2.4 %shard_map.40.refs_1_ = bf16[1040,128]{1,0:T(8,128)(2,1)S(1)} custom-call(bf16[8,144,128]{2,1,0:T(8,128)(2,1)S(1)} %all_to_all.22.refs_0_, f32[16,128]{1,0:T(8,128)S(1)} %get-tuple-element.8.refs_1_), custom_call_target="tpu_custom_call" | custom-call | flops 1610612736 | bytes 569344 | tf_op jit(solution)/shard_map/pallas_call | solution.py:195
  72.6 0.0 copy-start.2
  72.7 0.7 shard_map.41
  73.4 3.4 %all-to-all-start.3 = ((bf16[8,128,128]{2,1,0:T(8,128)(2,1)}), bf16[8,128,128]{2,1,0:T(8,128)(2,1)S(1)}, u32[]{:S(2)}, u32[]{:S(2)}) async-start(bf16[8,128,128]{2,1,0:T(8,128)(2,1)} %shard_map.41), calls=%async_computation.3 | async-start | bytes 524288 | tf_op jit(solution)/shard_map/all_to_all | solution.py:208
  76.8 6.8 %collective-permute-start = (bf16[1040,128]{1,0:T(8,128)(2,1)S(1)}, bf16[1040,128]{1,0:T(8,128)(2,1)S(1)}, u32[]{:S(2)}, u32[]{:S(2)}) collective-permute-start(bf16[1040,128]{1,0:T(8,128)(2,1)S(1)} %shard_map.40.refs_1_), channel_id=1, source_target_pairs={{0,0},{1,64},{2,130},{3,194},{4,260},{5,324},{6,390},{7,454},{8,8}... | collective-permute-start | bytes 798728 | tf_op jit(solution)/shard_map/ppermute | solution.py:217
  83.6 3.6 %all-to-all-done.3 = bf16[8,128,128]{2,1,0:T(8,128)(2,1)S(1)} async-done(((bf16[8,128,128]{2,1,0:T(8,128)(2,1)}), bf16[8,128,128]{2,1,0:T(8,128)(2,1)S(1)}, u32[]{:S(2)}, u32[]{:S(2)}) %all-to-all-start.3) | async-done | bytes 262176 | tf_op jit(solution)/shard_map/all_to_all | solution.py:208
  87.2 0.0 copy-done.2
  87.2 2.6 %shard_map.42.refs_0_ = bf16[512,512]{1,0:T(8,128)(2,1)S(1)} custom-call(bf16[1024,128]{1,0:T(8,128)(2,1)S(1)} %bitcast.1, f32[16,128]{1,0:T(8,128)S(1)} %get-tuple-element.8.refs_1_, bf16[512,512]{1,0:T(8,128)(2,1)S(1)} %copy-done.2), custom_call_target="tpu_custom_call" | custom-call | flops 1879048192 | bytes 1318912 | tf_op jit(solution)/shard_map/pallas_call | solution.py:195
  89.9 5.0 %collective-permute-done.refs_1_ = bf16[1040,128]{1,0:T(8,128)(2,1)S(1)} collective-permute-done((bf16[1040,128]{1,0:T(8,128)(2,1)S(1)}, bf16[1040,128]{1,0:T(8,128)(2,1)S(1)}, u32[]{:S(2)}, u32[]{:S(2)}) %collective-permute-start) | collective-permute-done | bytes 266272 | tf_op jit(solution)/shard_map/ppermute | solution.py:217
  94.9 1.5 %shard_map.43 = f32[512,512]{1,0:T(8,128)} custom-call(bf16[512,512]{1,0:T(8,128)(2,1)S(1)} %shard_map.42.refs_0_, bf16[1040,128]{1,0:T(8,128)(2,1)S(1)} %collective-permute-done.refs_1_), custom_call_target="tpu_custom_call" | custom-call | flops 268435456 | bytes 1839104 | tf_op jit(solution)/shard_map/pallas_call | solution.py:195
Async XLA Ops:
  0.0 1.2 %copy-start = (bf16[128,4096]{1,0:T(8,128)(2,1)S(1)}, bf16[128,4096]{1,0:T(8,128)(2,1)}, u32[]{:S(2)}) copy-start(bf16[128,4096]{1,0:T(8,128)(2,1)} %refs_1_.1) | copy-start | bytes 3145732
  1.2 0.9 copy-start.1
  72.6 14.6 %copy-start.2 = (bf16[512,512]{1,0:T(8,128)(2,1)S(1)}, bf16[512,512]{1,0:T(8,128)(2,1)}, u32[]{:S(2)}) copy-start(bf16[512,512]{1,0:T(8,128)(2,1)} %refs_2_.1) | copy-start | bytes 1572868
  73.4 13.8 %all-to-all-start.3 = ((bf16[8,128,128]{2,1,0:T(8,128)(2,1)}), bf16[8,128,128]{2,1,0:T(8,128)(2,1)S(1)}, u32[]{:S(2)}, u32[]{:S(2)}) async-start(bf16[8,128,128]{2,1,0:T(8,128)(2,1)} %shard_map.41), calls=%async_computation.3 | async-start | bytes 524288 | tf_op jit(solution)/shard_map/all_to_all | solution.py:208
  76.8 18.0 %collective-permute-start = (bf16[1040,128]{1,0:T(8,128)(2,1)S(1)}, bf16[1040,128]{1,0:T(8,128)(2,1)S(1)}, u32[]{:S(2)}, u32[]{:S(2)}) collective-permute-start(bf16[1040,128]{1,0:T(8,128)(2,1)S(1)} %shard_map.40.refs_1_), channel_id=1, source_target_pairs={{0,0},{1,64},{2,130},{3,194},{4,260},{5,324},{6,390},{7,454},{8,8}... | collective-permute-start | bytes 798728 | tf_op jit(solution)/shard_map/ppermute | solution.py:217

commit v9 on v8

--- a/solution.py
+++ b/solution.py
@@ -174,15 +174,18 @@
             out[peer, place * PIECE : (place + 1) * PIECE, :] = piece
 
 
+def unpack_kernel(root, out):
+    unpack(root, out, root[PACKED:, :].astype(F32))
+
+
 def left_kernel(got, ends, grad, out, full):
     unpack(got, full, ends[DIAGONAL:, :])
     root = inverse_root(full[...]).astype(BF16)
     out[...] = jnp.dot(root, grad[...], preferred_element_type=F32).astype(BF16)
 
 
-def last_kernel(left, root, out, full):
-    unpack(root, full, root[PACKED:, :].astype(F32))
-    out[...] = jnp.dot(left[...], full[...], preferred_element_type=F32)
+def last_kernel(left, root, out):
+    out[...] = jnp.dot(left[...], root[...], preferred_element_type=F32)
 
 
 def call(kernel, args, outs, scratch=(), flops=1 << 20, after=()):
@@ -252,8 +255,11 @@
     grad_root = transpose_places(root)
     sent = call(copies_kernel, [got], [((PEERS, SHARE, TILE), BF16)], after=[root])
     act_cov = exchange(sent, "z").reshape(packed)
-    left = call(left_kernel, [act_cov, ends, grad], [(full, BF16)], [(full, F32)], 7 * cube)
-    return call(last_kernel, [left, grad_root], [(full, F32)], [(full, BF16)], cube)
+    grad_root = call(unpack_kernel, [grad_root], [(full, BF16)], (), 14 * cube)
+    left = call(
+        left_kernel, [act_cov, ends, grad], [(full, BF16)], [(full, F32)], 7 * cube, [grad_root]
+    )
+    return call(last_kernel, [left, grad_root], [(full, F32)], (), cube)
 
 
 def solution(mesh):

time: 97.3 us -> 101 us (1.038)
  waiting for transfers between devices: 8.6 us -> 11.4 us
    ppermute x1, waiting for transfers between devices: 4.99 us -> 7.09 us  [transpose_places(): return lax.ppermute(data, AXES, pairs)]
    pallas_call x7 -> x8, Pallas kernels: 8.54 us -> 8.57 us  [call(): pl.pallas_call(body, out_shape=outs, in_specs=[VMEM] * len(args) + [ANYWH...]
  transfers between devices with their start and end apart: 2 -> 2, of which waited for: 2 -> 2; matrix products, arithmetic and copies ran while one was open for 0% -> 0% of each run, Pallas kernels for 3% -> 1%
where the time goes in v9:
time: 101 us; the launch traced here: 99.2 us
  blocking collectives  66.9 us (66%)
  waiting for transfers between devices  11.4 us (11%)
  starting transfers between devices  10.2 us (10%)
  Pallas kernels  8.57 us (8%)
  local copies, waits for them, and re-layouts  2.13 us (2%)
    all_to_all x3, blocking collectives, exchange(): return lax.all_to_all(data, axes, split_axis=0, concat_axis=0, tiled=True)  66.9 us
    pallas_call x8, Pallas kernels, call(): pl.pallas_call(body, out_shape=outs, in_specs=[VMEM] * len(args) + [ANYWH...  8.57 us
    ppermute x1, waiting for transfers between devices, transpose_places(): return lax.ppermute(data, AXES, pairs)  7.09 us
    ppermute x1, starting transfers between devices, transpose_places(): return lax.ppermute(data, AXES, pairs)  6.77 us
    all_to_all x1, waiting for transfers between devices, exchange(): return lax.all_to_all(data, axes, split_axis=0, concat_axis=0, tiled=True)  4.28 us
    all_to_all x1, starting transfers between devices, exchange(): return lax.all_to_all(data, axes, split_axis=0, concat_axis=0, tiled=True)  3.41 us
    unnamed x6, local copies, waits for them, and re-layouts  2.13 us
  transfers between devices with their start and end apart: 2, of which 2 were waited for; matrix products, arithmetic and copies ran while one was open for 0% of the time, Pallas kernels for 1%

profile of v9, /device:TPU:6, one launch (start us, length us, event | category | flops | bytes accessed | tf_op | source)
XLA Modules:
  0.0 99.2 jit_solution(8955256944253265752)
XLA Ops:
  0.0 0.0 copy-start
  0.0 1.2 %copy-done = bf16[128,4096]{1,0:T(8,128)(2,1)S(1)} copy-done((bf16[128,4096]{1,0:T(8,128)(2,1)S(1)}, bf16[128,4096]{1,0:T(8,128)(2,1)}, u32[]{:S(2)}) %copy-start) | copy-done | bytes 1048600
  1.2 0.0 copy-start.1
  1.2 0.9 copy-done.1
  2.1 0.4 shard_map.37
  2.6 45.2 %all_to_all.20.refs_0_ = bf16[8,656,128]{2,1,0:T(8,128)(2,1)S(1)} all-to-all(bf16[8,656,128]{2,1,0:T(8,128)(2,1)S(1)} %shard_map.37), channel_id=1, replica_groups=mesh['x'=4,'yl'=2,'z'=8,'yh'=4,'c'=2] {'z'}, dimensions={0} | all-to-all | bytes 2686976 | tf_op jit(solution)/shard_map/all_to_all | solution.py:211
  47.7 0.8 shard_map.38
  48.5 11.4 %all_to_all.21.refs_0_ = bf16[8,192,128]{2,1,0:T(8,128)(2,1)S(1)} all-to-all(bf16[8,192,128]{2,1,0:T(8,128)(2,1)S(1)} %shard_map.38), channel_id=1, replica_groups=mesh['x'=4,'yl'=2,'z'=8,'yh'=4,'c'=2] {'x','yl'}, dimensions={0} | all-to-all | bytes 786432 | tf_op jit(solution)/shard_map/all_to_all | solution.py:211
  59.9 0.1 shard_map.39
  60.0 10.3 %all_to_all.22.refs_0_ = bf16[8,144,128]{2,1,0:T(8,128)(2,1)S(1)} all-to-all(bf16[8,144,128]{2,1,0:T(8,128)(2,1)S(1)} %get-tuple-element.7), channel_id=1, replica_groups=mesh['x'=4,'yl'=2,'z'=8,'yh'=4,'c'=2] {'x','yl'}, dimensions={0} | all-to-all | bytes 589824 | tf_op jit(solution)/shard_map/all_to_all | solution.py:211
  70.3 2.4 %shard_map.40.refs_1_ = bf16[1040,128]{1,0:T(8,128)(2,1)S(1)} custom-call(bf16[8,144,128]{2,1,0:T(8,128)(2,1)S(1)} %all_to_all.22.refs_0_, f32[16,128]{1,0:T(8,128)S(1)} %get-tuple-element.8.refs_1_), custom_call_target="tpu_custom_call" | custom-call | flops 1610612736 | bytes 569344 | tf_op jit(solution)/shard_map/pallas_call | solution.py:198
  72.6 6.8 %collective-permute-start = (bf16[1040,128]{1,0:T(8,128)(2,1)S(1)}, bf16[1040,128]{1,0:T(8,128)(2,1)S(1)}, u32[]{:S(2)}, u32[]{:S(2)}) collective-permute-start(bf16[1040,128]{1,0:T(8,128)(2,1)S(1)} %shard_map.40.refs_1_), channel_id=1, source_target_pairs={{0,0},{1,64},{2,130},{3,194},{4,260},{5,324},{6,390},{7,454},{8,8}... | collective-permute-start | bytes 798728 | tf_op jit(solution)/shard_map/ppermute | solution.py:220
  79.4 0.7 shard_map.41
  80.2 3.4 %all-to-all-start.3 = ((bf16[8,128,128]{2,1,0:T(8,128)(2,1)}), bf16[8,128,128]{2,1,0:T(8,128)(2,1)S(1)}, u32[]{:S(2)}, u32[]{:S(2)}) async-start(bf16[8,128,128]{2,1,0:T(8,128)(2,1)} %shard_map.41), calls=%async_computation.3 | async-start | bytes 524288 | tf_op jit(solution)/shard_map/all_to_all | solution.py:211
  83.6 0.0 copy-start.2
  83.6 7.1 %collective-permute-done.refs_0_ = bf16[1040,128]{1,0:T(8,128)(2,1)S(1)} collective-permute-done((bf16[1040,128]{1,0:T(8,128)(2,1)S(1)}, bf16[1040,128]{1,0:T(8,128)(2,1)S(1)}, u32[]{:S(2)}, u32[]{:S(2)}) %collective-permute-start) | collective-permute-done | bytes 266272 | tf_op jit(solution)/shard_map/ppermute | solution.py:220
  90.7 0.1 shard_map.42.refs_3_.refs_1_
  90.8 4.3 %all-to-all-done.3 = bf16[8,128,128]{2,1,0:T(8,128)(2,1)S(1)} async-done(((bf16[8,128,128]{2,1,0:T(8,128)(2,1)}), bf16[8,128,128]{2,1,0:T(8,128)(2,1)S(1)}, u32[]{:S(2)}, u32[]{:S(2)}) %all-to-all-start.3) | async-done | bytes 262176 | tf_op jit(solution)/shard_map/all_to_all | solution.py:211
  95.1 0.0 copy-done.2
  95.1 2.7 %shard_map.43.refs_0_ = bf16[512,512]{1,0:T(8,128)(2,1)S(1)} custom-call(bf16[1024,128]{1,0:T(8,128)(2,1)S(1)} %bitcast.1, f32[16,128]{1,0:T(8,128)S(1)} %get-tuple-element.8.refs_1_, bf16[512,512]{1,0:T(8,128)(2,1)S(1)} %copy-done.2, bf16[512,512]{1,0:T(8,128)(2,1)S(1)} %shard_map.42.refs_3_.refs_1_), custom_call_target="tpu_custom_call" | custom-call | flops 1879048192 | bytes 1318912 | tf_op jit(solution)/shard_map/pallas_call | solution.py:198
  97.8 1.4 %shard_map.44 = f32[512,512]{1,0:T(8,128)} custom-call(bf16[512,512]{1,0:T(8,128)(2,1)S(1)} %shard_map.43.refs_0_, bf16[512,512]{1,0:T(8,128)(2,1)S(1)} %shard_map.42.refs_3_.refs_1_), custom_call_target="tpu_custom_call" | custom-call | flops 268435456 | bytes 2097152 | tf_op jit(solution)/shard_map/pallas_call | solution.py:198
Async XLA Ops:
  0.0 1.2 %copy-start = (bf16[128,4096]{1,0:T(8,128)(2,1)S(1)}, bf16[128,4096]{1,0:T(8,128)(2,1)}, u32[]{:S(2)}) copy-start(bf16[128,4096]{1,0:T(8,128)(2,1)} %refs_1_.1) | copy-start | bytes 3145732
  1.2 0.9 copy-start.1
  72.6 18.0 %collective-permute-start = (bf16[1040,128]{1,0:T(8,128)(2,1)S(1)}, bf16[1040,128]{1,0:T(8,128)(2,1)S(1)}, u32[]{:S(2)}, u32[]{:S(2)}) collective-permute-start(bf16[1040,128]{1,0:T(8,128)(2,1)S(1)} %shard_map.40.refs_1_), channel_id=1, source_target_pairs={{0,0},{1,64},{2,130},{3,194},{4,260},{5,324},{6,390},{7,454},{8,8}... | collective-permute-start | bytes 798728 | tf_op jit(solution)/shard_map/ppermute | solution.py:220
  80.2 15.0 %all-to-all-start.3 = ((bf16[8,128,128]{2,1,0:T(8,128)(2,1)}), bf16[8,128,128]{2,1,0:T(8,128)(2,1)S(1)}, u32[]{:S(2)}, u32[]{:S(2)}) async-start(bf16[8,128,128]{2,1,0:T(8,128)(2,1)} %shard_map.41), calls=%async_computation.3 | async-start | bytes 524288 | tf_op jit(solution)/shard_map/all_to_all | solution.py:211
  83.6 11.5 %copy-start.2 = (bf16[512,512]{1,0:T(8,128)(2,1)S(1)}, bf16[512,512]{1,0:T(8,128)(2,1)}, u32[]{:S(2)}) copy-start(bf16[512,512]{1,0:T(8,128)(2,1)} %refs_2_.1) | copy-start | bytes 1572868

commit v10 on v7

--- a/solution.py
+++ b/solution.py
@@ -186,6 +186,10 @@
     out[...] = jnp.dot(root, grad[...], preferred_element_type=F32).astype(BF16)
 
 
+def keep_kernel(got, out):
+    out[...] = got[...]
+
+
 def last_kernel(left, mine, other, out, packed, full):
     bit = lax.axis_index("c")
     packed[rows(bit, HALF), :] = mine[0:HALF, :]
@@ -266,7 +270,8 @@
     sent = call(copies_kernel, [got], [((PEERS, SHARE, TILE), BF16)], after=[root])
     act_cov = exchange(sent, "z").reshape(packed)
     left = call(left_kernel, [act_cov, ends, grad], [(full, BF16)], [(full, F32)], 7 * cube)
-    other = swap(mine, "c", 2, 1)
+    kept = call(keep_kernel, [mine], [((ROOT, TILE), BF16)], after=[left])
+    other = swap(kept, "c", 2, 1)
     return call(
         last_kernel, [left, mine, other], [(full, F32)], [(packed, BF16), (full, BF16)], cube
     )

time: 99.4 us -> 97.9 us (0.985)
  the two profiles are of different devices: /device:TPU:33 before, /device:TPU:1 now
where the time goes in v10:
time: 97.9 us; the launch traced here: 97.5 us
  blocking collectives  64.7 us (66%)
  starting transfers between devices  18.9 us (19%)
  Pallas kernels  8.63 us (9%)
  waiting for transfers between devices  3 us (3%)
  local copies, waits for them, and re-layouts  2.13 us (2%)
    all_to_all x3, blocking collectives, exchange(): return lax.all_to_all(data, axes, split_axis=0, concat_axis=0, tiled=True)  64.7 us
    pallas_call x8, Pallas kernels, call(): pl.pallas_call(body, out_shape=outs, in_specs=[VMEM] * len(args) + [ANYWH...  8.63 us
    ppermute x1, starting transfers between devices, swap(): return lax.ppermute(data, axis, [(i, i ^ distance) for i in range(size)])  8.07 us
    ppermute x1, starting transfers between devices, transpose_places(): return lax.ppermute(data, AXES, pairs)  7.3 us
    all_to_all x1, starting transfers between devices, exchange(): return lax.all_to_all(data, axes, split_axis=0, concat_axis=0, tiled=True)  3.55 us
    unnamed x6, local copies, waits for them, and re-layouts  2.13 us
    all_to_all x1, waiting for transfers between devices, exchange(): return lax.all_to_all(data, axes, split_axis=0, concat_axis=0, tiled=True)  2.03 us
  transfers between devices with their start and end apart: 3, of which 2 were waited for; matrix products, arithmetic and copies ran while one was open for 0% of the time, Pallas kernels for 3%

profile of v10, /device:TPU:1, one launch (start us, length us, event | category | flops | bytes accessed | tf_op | source)
XLA Modules:
  0.0 97.5 jit_solution(3433717899790302844)
XLA Ops:
  0.0 0.0 copy-start
  0.0 1.2 %copy-done = bf16[128,4096]{1,0:T(8,128)(2,1)S(1)} copy-done((bf16[128,4096]{1,0:T(8,128)(2,1)S(1)}, bf16[128,4096]{1,0:T(8,128)(2,1)}, u32[]{:S(2)}) %copy-start) | copy-done | bytes 1048600
  1.2 0.0 copy-start.1
  1.2 0.9 copy-done.1
  2.1 0.4 shard_map.37
  2.6 43.9 %all_to_all.20.refs_0_ = bf16[8,656,128]{2,1,0:T(8,128)(2,1)S(1)} all-to-all(bf16[8,656,128]{2,1,0:T(8,128)(2,1)S(1)} %shard_map.37), channel_id=1, replica_groups=mesh['x'=4,'yl'=2,'z'=8,'yh'=4,'c'=2] {'z'}, dimensions={0} | all-to-all | bytes 2686976 | tf_op jit(solution)/shard_map/all_to_all | solution.py:221
  46.5 0.8 shard_map.38
  47.3 11.8 %all_to_all.21.refs_0_ = bf16[8,192,128]{2,1,0:T(8,128)(2,1)S(1)} all-to-all(bf16[8,192,128]{2,1,0:T(8,128)(2,1)S(1)} %shard_map.38), channel_id=1, replica_groups=mesh['x'=4,'yl'=2,'z'=8,'yh'=4,'c'=2] {'x','yl'}, dimensions={0} | all-to-all | bytes 786432 | tf_op jit(solution)/shard_map/all_to_all | solution.py:221
  59.1 0.1 shard_map.39
  59.2 8.9 %all_to_all.22.refs_0_ = bf16[8,144,128]{2,1,0:T(8,128)(2,1)S(1)} all-to-all(bf16[8,144,128]{2,1,0:T(8,128)(2,1)S(1)} %get-tuple-element.7), channel_id=1, replica_groups=mesh['x'=4,'yl'=2,'z'=8,'yh'=4,'c'=2] {'x','yl'}, dimensions={0} | all-to-all | bytes 589824 | tf_op jit(solution)/shard_map/all_to_all | solution.py:221
  68.1 0.0 copy-start.2
  68.1 2.4 %shard_map.40.refs_1_ = bf16[528,128]{1,0:T(8,128)(2,1)S(1)} custom-call(bf16[8,144,128]{2,1,0:T(8,128)(2,1)S(1)} %all_to_all.22.refs_0_, f32[16,128]{1,0:T(8,128)S(1)} %get-tuple-element.8.refs_1_), custom_call_target="tpu_custom_call" | custom-call | flops 1610612736 | bytes 438272 | tf_op jit(solution)/shard_map/pallas_call | solution.py:208
  70.5 0.7 shard_map.41
  71.3 3.6 %all-to-all-start.3 = ((bf16[8,128,128]{2,1,0:T(8,128)(2,1)}), bf16[8,128,128]{2,1,0:T(8,128)(2,1)S(1)}, u32[]{:S(2)}, u32[]{:S(2)}) async-start(bf16[8,128,128]{2,1,0:T(8,128)(2,1)} %shard_map.41), calls=%async_computation.3 | async-start | bytes 524288 | tf_op jit(solution)/shard_map/all_to_all | solution.py:221
  74.8 7.3 %collective-permute-start = (bf16[528,128]{1,0:T(8,128)(2,1)S(1)}, bf16[528,128]{1,0:T(8,128)(2,1)S(1)}, u32[]{:S(2)}, u32[]{:S(2)}) collective-permute-start(bf16[528,128]{1,0:T(8,128)(2,1)S(1)} %shard_map.40.refs_1_), channel_id=1, source_target_pairs={{0,0},{1,64},{2,130},{3,194},{4,260},{5,324},{6,390},{7,454},{8,8}... | collective-permute-start | bytes 405512 | tf_op jit(solution)/shard_map/ppermute | solution.py:234
  82.1 2.0 %all-to-all-done.3 = bf16[8,128,128]{2,1,0:T(8,128)(2,1)S(1)} async-done(((bf16[8,128,128]{2,1,0:T(8,128)(2,1)}), bf16[8,128,128]{2,1,0:T(8,128)(2,1)S(1)}, u32[]{:S(2)}, u32[]{:S(2)}) %all-to-all-start.3) | async-done | bytes 262176 | tf_op jit(solution)/shard_map/all_to_all | solution.py:221
  84.2 0.0 copy-done.2
  84.2 2.6 %shard_map.42.refs_1_.refs_0_ = bf16[512,512]{1,0:T(8,128)(2,1)S(1)} custom-call(bf16[1024,128]{1,0:T(8,128)(2,1)S(1)} %bitcast.1, f32[16,128]{1,0:T(8,128)S(1)} %get-tuple-element.8.refs_1_, bf16[512,512]{1,0:T(8,128)(2,1)S(1)} %copy-done.2), custom_call_target="tpu_custom_call" | custom-call | flops 1879048192 | bytes 1318912 | tf_op jit(solution)/shard_map/pallas_call | solution.py:208
  86.8 0.0 collective-permute-done.refs_0_.refs_1_
  86.8 8.1 %collective-permute-start.1 = (bf16[528,128]{1,0:T(8,128)(2,1)S(1)}, bf16[528,128]{1,0:T(8,128)(2,1)S(1)}, u32[]{:S(2)}, u32[]{:S(2)}) collective-permute-start(bf16[528,128]{1,0:T(8,128)(2,1)S(1)} %shard_map.43), channel_id=1, source_target_pairs={{0,1},{1,0},{2,3},{3,2},{4,5},{5,4},{6,7},{7,6},{8,9},{9,8},{10,11... | collective-permute-start | bytes 405512 | tf_op jit(solution)/shard_map/ppermute | solution.py:225
  94.9 1.0 collective-permute-done.1.refs_2_
  95.9 1.6 %shard_map.44 = f32[512,512]{1,0:T(8,128)} custom-call(bf16[512,512]{1,0:T(8,128)(2,1)S(1)} %shard_map.42.refs_1_.refs_0_, bf16[528,128]{1,0:T(8,128)(2,1)S(1)} %collective-permute-done.refs_0_.refs_1_, bf16[528,128]{1,0:T(8,128)(2,1)S(1)} %collective-permute-done.1.refs_2_), custom_call_target="tpu_custom_call" | custom-call | flops 268435456 | bytes 1843200 | tf_op jit(solution)/shard_map/pallas_call | solution.py:208
  (1 shorter events, 0.0 us)
Async XLA Ops:
  0.0 1.2 %copy-start = (bf16[128,4096]{1,0:T(8,128)(2,1)S(1)}, bf16[128,4096]{1,0:T(8,128)(2,1)}, u32[]{:S(2)}) copy-start(bf16[128,4096]{1,0:T(8,128)(2,1)} %refs_1_.1) | copy-start | bytes 3145732
  1.2 0.9 copy-start.1
  68.1 16.0 %copy-start.2 = (bf16[512,512]{1,0:T(8,128)(2,1)S(1)}, bf16[512,512]{1,0:T(8,128)(2,1)}, u32[]{:S(2)}) copy-start(bf16[512,512]{1,0:T(8,128)(2,1)} %refs_2_.1) | copy-start | bytes 1572868
  71.3 12.9 %all-to-all-start.3 = ((bf16[8,128,128]{2,1,0:T(8,128)(2,1)}), bf16[8,128,128]{2,1,0:T(8,128)(2,1)S(1)}, u32[]{:S(2)}, u32[]{:S(2)}) async-start(bf16[8,128,128]{2,1,0:T(8,128)(2,1)} %shard_map.41), calls=%async_computation.3 | async-start | bytes 524288 | tf_op jit(solution)/shard_map/all_to_all | solution.py:221
  74.8 12.0 %collective-permute-start = (bf16[528,128]{1,0:T(8,128)(2,1)S(1)}, bf16[528,128]{1,0:T(8,128)(2,1)S(1)}, u32[]{:S(2)}, u32[]{:S(2)}) collective-permute-start(bf16[528,128]{1,0:T(8,128)(2,1)S(1)} %shard_map.40.refs_1_), channel_id=1, source_target_pairs={{0,0},{1,64},{2,130},{3,194},{4,260},{5,324},{6,390},{7,454},{8,8}... | collective-permute-start | bytes 405512 | tf_op jit(solution)/shard_map/ppermute | solution.py:234
  86.8 9.0 %collective-permute-start.1 = (bf16[528,128]{1,0:T(8,128)(2,1)S(1)}, bf16[528,128]{1,0:T(8,128)(2,1)S(1)}, u32[]{:S(2)}, u32[]{:S(2)}) collective-permute-start(bf16[528,128]{1,0:T(8,128)(2,1)S(1)} %shard_map.43), channel_id=1, source_target_pairs={{0,1},{1,0},{2,3},{3,2},{4,5},{5,4},{6,7},{7,6},{8,9},{9,8},{10,11... | collective-permute-start | bytes 405512 | tf_op jit(solution)/shard_map/ppermute | solution.py:225

commit v11 on v10

--- a/solution.py
+++ b/solution.py
@@ -259,15 +259,16 @@
         sum_kernel, [got], [((PEERS, GATHER, TILE), BF16), ((2 * DIAGONAL, TILE), F32)]
     )
     got = exchange(sent, ("x", "yl"))
+    sent = call(copies_kernel, [got], [((PEERS, SHARE, TILE), BF16)])
     root = call(
         grad_root_kernel,
         [got, ends],
         [((ROOT, TILE), BF16)],
         [(full, F32), (packed, BF16)],
         6 * cube,
+        [sent],
     )
     mine = transpose_places(root)
-    sent = call(copies_kernel, [got], [((PEERS, SHARE, TILE), BF16)], after=[root])
     act_cov = exchange(sent, "z").reshape(packed)
     left = call(left_kernel, [act_cov, ends, grad], [(full, BF16)], [(full, F32)], 7 * cube)
     kept = call(keep_kernel, [mine], [((ROOT, TILE), BF16)], after=[left])

time: 97.9 us -> 97.7 us (level)
  the two profiles are of different devices: /device:TPU:1 before, /device:TPU:33 now
where the time goes in v11:
time: 97.7 us; the launch traced here: 97.3 us
  blocking collectives  62.9 us (64%)
  starting transfers between devices  19.9 us (20%)
  Pallas kernels  8.63 us (9%)
  waiting for transfers between devices  3.66 us (4%)
  local copies, waits for them, and re-layouts  2.13 us (2%)
    all_to_all x3, blocking collectives, exchange(): return lax.all_to_all(data, axes, split_axis=0, concat_axis=0, tiled=True)  62.9 us
    pallas_call x8, Pallas kernels, call(): pl.pallas_call(body, out_shape=outs, in_specs=[VMEM] * len(args) + [ANYWH...  8.63 us
    ppermute x1, starting transfers between devices, swap(): return lax.ppermute(data, axis, [(i, i ^ distance) for i in range(size)])  8.47 us
    ppermute x1, starting transfers between devices, transpose_places(): return lax.ppermute(data, AXES, pairs)  7.82 us
    all_to_all x1, starting transfers between devices, exchange(): return lax.all_to_all(data, axes, split_axis=0, concat_axis=0, tiled=True)  3.61 us
    ppermute x1, waiting for transfers between devices, transpose_places(): return lax.ppermute(data, AXES, pairs)  2.69 us
    unnamed x6, local copies, waits for them, and re-layouts  2.13 us
  transfers between devices with their start and end apart: 3, of which 2 were waited for; matrix products, arithmetic and copies ran while one was open for 0% of the time, Pallas kernels for 5%

profile of v11, /device:TPU:33, one launch (start us, length us, event | category | flops | bytes accessed | tf_op | source)
XLA Modules:
  0.0 97.3 jit_solution(2002788058643128621)
XLA Ops:
  0.0 0.0 copy-start
  0.0 1.2 %copy-done = bf16[128,4096]{1,0:T(8,128)(2,1)S(1)} copy-done((bf16[128,4096]{1,0:T(8,128)(2,1)S(1)}, bf16[128,4096]{1,0:T(8,128)(2,1)}, u32[]{:S(2)}) %copy-start) | copy-done | bytes 1048600
  1.2 0.0 copy-start.1
  1.2 0.9 copy-done.1
  2.1 0.4 shard_map.37
  2.6 43.2 %all_to_all.20.refs_0_ = bf16[8,656,128]{2,1,0:T(8,128)(2,1)S(1)} all-to-all(bf16[8,656,128]{2,1,0:T(8,128)(2,1)S(1)} %shard_map.37), channel_id=1, replica_groups=mesh['x'=4,'yl'=2,'z'=8,'yh'=4,'c'=2] {'z'}, dimensions={0} | all-to-all | bytes 2686976 | tf_op jit(solution)/shard_map/all_to_all | solution.py:221
  45.7 0.8 shard_map.38
  46.5 10.8 %all_to_all.21.refs_0_ = bf16[8,192,128]{2,1,0:T(8,128)(2,1)S(1)} all-to-all(bf16[8,192,128]{2,1,0:T(8,128)(2,1)S(1)} %shard_map.38), channel_id=1, replica_groups=mesh['x'=4,'yl'=2,'z'=8,'yh'=4,'c'=2] {'x','yl'}, dimensions={0} | all-to-all | bytes 786432 | tf_op jit(solution)/shard_map/all_to_all | solution.py:221
  57.3 0.1 shard_map.39
  57.4 8.9 %all_to_all.22.refs_0_ = bf16[8,144,128]{2,1,0:T(8,128)(2,1)S(1)} all-to-all(bf16[8,144,128]{2,1,0:T(8,128)(2,1)S(1)} %get-tuple-element.7), channel_id=1, replica_groups=mesh['x'=4,'yl'=2,'z'=8,'yh'=4,'c'=2] {'x','yl'}, dimensions={0} | all-to-all | bytes 589824 | tf_op jit(solution)/shard_map/all_to_all | solution.py:221
  66.3 0.7 shard_map.40.refs_2_
  67.1 3.6 %all-to-all-start.3 = ((bf16[8,128,128]{2,1,0:T(8,128)(2,1)}), bf16[8,128,128]{2,1,0:T(8,128)(2,1)S(1)}, u32[]{:S(2)}, u32[]{:S(2)}) async-start(bf16[8,128,128]{2,1,0:T(8,128)(2,1)} %shard_map.40.refs_2_), calls=%async_computation.3 | async-start | bytes 524288 | tf_op jit(solution)/shard_map/all_to_all | solution.py:221
  70.7 0.0 copy-start.2
  70.7 2.4 %shard_map.42 = bf16[528,128]{1,0:T(8,128)(2,1)S(1)} custom-call(bf16[8,144,128]{2,1,0:T(8,128)(2,1)S(1)} %all_to_all.22.refs_0_, f32[16,128]{1,0:T(8,128)S(1)} %get-tuple-element.8.refs_1_, bf16[8,128,128]{2,1,0:T(8,128)(2,1)} %shard_map.40.refs_2_), custom_call_target="tpu_custom_call" | custom-call | flops 1610612736 | bytes 438272 | tf_op jit(solution)/shard_map/pallas_call | solution.py:208
  73.1 7.8 %collective-permute-start = (bf16[528,128]{1,0:T(8,128)(2,1)S(1)}, bf16[528,128]{1,0:T(8,128)(2,1)S(1)}, u32[]{:S(2)}, u32[]{:S(2)}) collective-permute-start(bf16[528,128]{1,0:T(8,128)(2,1)S(1)} %shard_map.42), channel_id=1, source_target_pairs={{0,0},{1,64},{2,130},{3,194},{4,260},{5,324},{6,390},{7,454},{8,8}... | collective-permute-start | bytes 405512 | tf_op jit(solution)/shard_map/ppermute | solution.py:234
  80.9 0.0 all-to-all-done.3
  80.9 0.0 copy-done.2
  80.9 2.6 %shard_map.41.refs_1_.refs_0_ = bf16[512,512]{1,0:T(8,128)(2,1)S(1)} custom-call(bf16[1024,128]{1,0:T(8,128)(2,1)S(1)} %bitcast.1, f32[16,128]{1,0:T(8,128)S(1)} %get-tuple-element.8.refs_1_, bf16[512,512]{1,0:T(8,128)(2,1)S(1)} %copy-done.2), custom_call_target="tpu_custom_call" | custom-call | flops 1879048192 | bytes 1318912 | tf_op jit(solution)/shard_map/pallas_call | solution.py:208
  83.6 2.7 %collective-permute-done.refs_0_.refs_1_ = bf16[528,128]{1,0:T(8,128)(2,1)S(1)} collective-permute-done((bf16[528,128]{1,0:T(8,128)(2,1)S(1)}, bf16[528,128]{1,0:T(8,128)(2,1)S(1)}, u32[]{:S(2)}, u32[]{:S(2)}) %collective-permute-start) | collective-permute-done | bytes 135200 | tf_op jit(solution)/shard_map/ppermute | solution.py:234
  86.3 8.5 %collective-permute-start.1 = (bf16[528,128]{1,0:T(8,128)(2,1)S(1)}, bf16[528,128]{1,0:T(8,128)(2,1)S(1)}, u32[]{:S(2)}, u32[]{:S(2)}) collective-permute-start(bf16[528,128]{1,0:T(8,128)(2,1)S(1)} %shard_map.43), channel_id=1, source_target_pairs={{0,1},{1,0},{2,3},{3,2},{4,5},{5,4},{6,7},{7,6},{8,9},{9,8},{10,11... | collective-permute-start | bytes 405512 | tf_op jit(solution)/shard_map/ppermute | solution.py:225
  94.8 1.0 collective-permute-done.1.refs_2_
  95.7 1.6 %shard_map.44 = f32[512,512]{1,0:T(8,128)} custom-call(bf16[512,512]{1,0:T(8,128)(2,1)S(1)} %shard_map.41.refs_1_.refs_0_, bf16[528,128]{1,0:T(8,128)(2,1)S(1)} %collective-permute-done.refs_0_.refs_1_, bf16[528,128]{1,0:T(8,128)(2,1)S(1)} %collective-permute-done.1.refs_2_), custom_call_target="tpu_custom_call" | custom-call | flops 268435456 | bytes 1843200 | tf_op jit(solution)/shard_map/pallas_call | solution.py:208
  (1 shorter events, 0.0 us)
Async XLA Ops:
  0.0 1.2 %copy-start = (bf16[128,4096]{1,0:T(8,128)(2,1)S(1)}, bf16[128,4096]{1,0:T(8,128)(2,1)}, u32[]{:S(2)}) copy-start(bf16[128,4096]{1,0:T(8,128)(2,1)} %refs_1_.1) | copy-start | bytes 3145732
  1.2 0.9 copy-start.1
  67.1 13.9 %all-to-all-start.3 = ((bf16[8,128,128]{2,1,0:T(8,128)(2,1)}), bf16[8,128,128]{2,1,0:T(8,128)(2,1)S(1)}, u32[]{:S(2)}, u32[]{:S(2)}) async-start(bf16[8,128,128]{2,1,0:T(8,128)(2,1)} %shard_map.40.refs_2_), calls=%async_computation.3 | async-start | bytes 524288 | tf_op jit(solution)/shard_map/all_to_all | solution.py:221
  70.7 10.3 %copy-start.2 = (bf16[512,512]{1,0:T(8,128)(2,1)S(1)}, bf16[512,512]{1,0:T(8,128)(2,1)}, u32[]{:S(2)}) copy-start(bf16[512,512]{1,0:T(8,128)(2,1)} %refs_2_.1) | copy-start | bytes 1572868
  73.1 13.2 %collective-permute-start = (bf16[528,128]{1,0:T(8,128)(2,1)S(1)}, bf16[528,128]{1,0:T(8,128)(2,1)S(1)}, u32[]{:S(2)}, u32[]{:S(2)}) collective-permute-start(bf16[528,128]{1,0:T(8,128)(2,1)S(1)} %shard_map.42), channel_id=1, source_target_pairs={{0,0},{1,64},{2,130},{3,194},{4,260},{5,324},{6,390},{7,454},{8,8}... | collective-permute-start | bytes 405512 | tf_op jit(solution)/shard_map/ppermute | solution.py:234
  86.3 9.5 %collective-permute-start.1 = (bf16[528,128]{1,0:T(8,128)(2,1)S(1)}, bf16[528,128]{1,0:T(8,128)(2,1)S(1)}, u32[]{:S(2)}, u32[]{:S(2)}) collective-permute-start(bf16[528,128]{1,0:T(8,128)(2,1)S(1)} %shard_map.43), channel_id=1, source_target_pairs={{0,1},{1,0},{2,3},{3,2},{4,5},{5,4},{6,7},{7,6},{8,9},{9,8},{10,11... | collective-permute-start | bytes 405512 | tf_op jit(solution)/shard_map/ppermute | solution.py:225

commit v12 on v8

--- a/solution.py
+++ b/solution.py
@@ -105,18 +105,24 @@
     return z * (1.0 / jnp.sqrt(frob))
 
 
-def first_kernel(acts, grads, out, packed):
-    total = gram(acts[...])
-    pack(total, packed)
-    high, low = halves(diagonals(total))
-    ends = jnp.concatenate([high, low], axis=0)
-    for peer in range(PEERS):
+def first_kernel(acts, grads, out, packed, ends):
+    step = pl.program_id(0)
+
+    @pl.when(step == 0)
+    def _():
+        total = gram(acts[...])
+        pack(total, packed)
+        high, low = halves(diagonals(total))
+        ends[...] = jnp.concatenate([high, low], axis=0)
+
+    count = out.shape[0]
+    for place in range(count):
         for part in range(SIDE):
-            column = peer * BLOCK + part * TILE
-            out[peer, part * TILE : (part + 1) * TILE, :] = grads[:, column : column + TILE]
-        share = packed[peer * SHARE : (peer + 1) * SHARE, :]
-        out[peer, RAW : RAW + SHARE, :] = share.astype(BF16)
-        out[peer, RAW + SHARE : FIRST, :] = ends
+            column = place * BLOCK + part * TILE
+            out[place, part * TILE : (part + 1) * TILE, :] = grads[:, column : column + TILE]
+        start = pl.multiple_of((step * count + place) * SHARE, SHARE)
+        out[place, RAW : RAW + SHARE, :] = packed[pl.ds(start, SHARE), :].astype(BF16)
+        out[place, RAW + SHARE : FIRST, :] = ends[...]
 
 
 def second_kernel(got, out, packed, share):
@@ -222,13 +228,18 @@
     packed, full = (PACKED, TILE), (BLOCK, BLOCK)
 
     share = (SHARE, TILE)
-    sent = call(
+    sent = pl.pallas_call(
         first_kernel,
-        [acts, grads_out],
-        [((PEERS, FIRST, TILE), BF16)],
-        [(packed, F32)],
-        cube // 4,
-    )
+        grid=(4,),
+        out_shape=jax.ShapeDtypeStruct((PEERS, FIRST, TILE), BF16),
+        in_specs=[
+            pl.BlockSpec((TILE, BLOCK), lambda step: (0, 0)),
+            pl.BlockSpec((TILE, 2 * BLOCK), lambda step: (0, step)),
+        ],
+        out_specs=pl.BlockSpec((2, FIRST, TILE), lambda step: (step, 0, 0)),
+        scratch_shapes=[pltpu.VMEM(packed, F32), pltpu.VMEM((2 * DIAGONAL, TILE), BF16)],
+        cost_estimate=pl.CostEstimate(flops=cube // 4, bytes_accessed=3 << 20, transcendentals=0),
+    )(acts, grads_out)
     got = exchange(sent, "z")
     sent = call(
         second_kernel,

time: 97.3 us -> 98.8 us (1.015)
  Pallas kernels: 8.54 us -> 12 us
  local copies, waits for them, and re-layouts: 2.13 us -> 0.01 us
    pallas_call x0 -> x1, Pallas kernels: none -> 3.84 us  [on_device(): pl.pallas_call(first_kernel, grid=(4,), out_shape=jax.ShapeDtypeStruct((P...]
    unnamed x6 -> x2, local copies, waits for them, and re-layouts: 2.13 us -> 0.01 us
    pallas_call x7 -> x6, Pallas kernels: 8.54 us -> 8.14 us  [call(): pl.pallas_call(body, out_shape=outs, in_specs=[VMEM] * len(args) + [ANYWH...]
where the time goes in v12:
time: 98.8 us; the launch traced here: 97.9 us
  blocking collectives  67.1 us (68%)
  Pallas kernels  12 us (12%)
  starting transfers between devices  10.2 us (10%)
  waiting for transfers between devices  8.57 us (9%)
    all_to_all x3, blocking collectives, exchange(): return lax.all_to_all(data, axes, split_axis=0, concat_axis=0, tiled=True)  67.1 us
    pallas_call x6, Pallas kernels, call(): pl.pallas_call(body, out_shape=outs, in_specs=[VMEM] * len(args) + [ANYWH...  8.14 us
    ppermute x1, starting transfers between devices, transpose_places(): return lax.ppermute(data, AXES, pairs)  6.77 us
    ppermute x1, waiting for transfers between devices, transpose_places(): return lax.ppermute(data, AXES, pairs)  4.96 us
    pallas_call x1, Pallas kernels, on_device(): pl.pallas_call(first_kernel, grid=(4,), out_shape=jax.ShapeDtypeStruct((P...  3.84 us
    all_to_all x1, waiting for transfers between devices, exchange(): return lax.all_to_all(data, axes, split_axis=0, concat_axis=0, tiled=True)  3.62 us
    all_to_all x1, starting transfers between devices, exchange(): return lax.all_to_all(data, axes, split_axis=0, concat_axis=0, tiled=True)  3.41 us
  transfers between devices with their start and end apart: 2, of which 2 were waited for; matrix products, arithmetic and copies ran while one was open for 0% of the time, Pallas kernels for 3%

profile of v12, /device:TPU:6, one launch (start us, length us, event | category | flops | bytes accessed | tf_op | source)
XLA Modules:
  0.0 97.9 jit_solution(17412774633695186701)
XLA Ops:
  0.0 3.8 %shard_map.37 = bf16[8,656,128]{2,1,0:T(8,128)(2,1)} custom-call(bf16[128,512]{1,0:T(8,128)(2,1)} %acts.1, bf16[128,4096]{1,0:T(8,128)(2,1)} %grads.1), custom_call_target="tpu_custom_call" | custom-call | flops 67108864 | bytes 3145728 | tf_op jit(solution)/shard_map/pallas_call | solution.py:231
  3.8 45.4 %all_to_all.20.refs_0_ = bf16[8,656,128]{2,1,0:T(8,128)(2,1)S(1)} all-to-all(bf16[8,656,128]{2,1,0:T(8,128)(2,1)} %shard_map.37), channel_id=1, replica_groups=mesh['x'=4,'yl'=2,'z'=8,'yh'=4,'c'=2] {'z'}, dimensions={0} | all-to-all | bytes 2686976 | tf_op jit(solution)/shard_map/all_to_all | solution.py:214
  49.2 0.8 shard_map.38
  50.0 11.4 %all_to_all.21.refs_0_ = bf16[8,192,128]{2,1,0:T(8,128)(2,1)S(1)} all-to-all(bf16[8,192,128]{2,1,0:T(8,128)(2,1)S(1)} %shard_map.38), channel_id=1, replica_groups=mesh['x'=4,'yl'=2,'z'=8,'yh'=4,'c'=2] {'x','yl'}, dimensions={0} | all-to-all | bytes 786432 | tf_op jit(solution)/shard_map/all_to_all | solution.py:214
  61.4 0.1 shard_map.39
  61.5 10.3 %all_to_all.22.refs_0_ = bf16[8,144,128]{2,1,0:T(8,128)(2,1)S(1)} all-to-all(bf16[8,144,128]{2,1,0:T(8,128)(2,1)S(1)} %get-tuple-element.7), channel_id=1, replica_groups=mesh['x'=4,'yl'=2,'z'=8,'yh'=4,'c'=2] {'x','yl'}, dimensions={0} | all-to-all | bytes 589824 | tf_op jit(solution)/shard_map/all_to_all | solution.py:214
  71.7 2.4 %shard_map.40.refs_1_ = bf16[1040,128]{1,0:T(8,128)(2,1)S(1)} custom-call(bf16[8,144,128]{2,1,0:T(8,128)(2,1)S(1)} %all_to_all.22.refs_0_, f32[16,128]{1,0:T(8,128)S(1)} %get-tuple-element.8.refs_1_), custom_call_target="tpu_custom_call" | custom-call | flops 1610612736 | bytes 569344 | tf_op jit(solution)/shard_map/pallas_call | solution.py:201
  74.1 0.0 copy-start
  74.1 0.7 shard_map.41
  74.9 3.4 %all-to-all-start.3 = ((bf16[8,128,128]{2,1,0:T(8,128)(2,1)}), bf16[8,128,128]{2,1,0:T(8,128)(2,1)S(1)}, u32[]{:S(2)}, u32[]{:S(2)}) async-start(bf16[8,128,128]{2,1,0:T(8,128)(2,1)} %shard_map.41), calls=%async_computation.3 | async-start | bytes 524288 | tf_op jit(solution)/shard_map/all_to_all | solution.py:214
  78.3 6.8 %collective-permute-start = (bf16[1040,128]{1,0:T(8,128)(2,1)S(1)}, bf16[1040,128]{1,0:T(8,128)(2,1)S(1)}, u32[]{:S(2)}, u32[]{:S(2)}) collective-permute-start(bf16[1040,128]{1,0:T(8,128)(2,1)S(1)} %shard_map.40.refs_1_), channel_id=1, source_target_pairs={{0,0},{1,64},{2,130},{3,194},{4,260},{5,324},{6,390},{7,454},{8,8}... | collective-permute-start | bytes 798728 | tf_op jit(solution)/shard_map/ppermute | solution.py:223
  85.1 3.6 %all-to-all-done.3 = bf16[8,128,128]{2,1,0:T(8,128)(2,1)S(1)} async-done(((bf16[8,128,128]{2,1,0:T(8,128)(2,1)}), bf16[8,128,128]{2,1,0:T(8,128)(2,1)S(1)}, u32[]{:S(2)}, u32[]{:S(2)}) %all-to-all-start.3) | async-done | bytes 262176 | tf_op jit(solution)/shard_map/all_to_all | solution.py:214
  88.7 0.0 copy-done
  88.7 2.7 %shard_map.42.refs_0_ = bf16[512,512]{1,0:T(8,128)(2,1)S(1)} custom-call(bf16[1024,128]{1,0:T(8,128)(2,1)S(1)} %bitcast.1, f32[16,128]{1,0:T(8,128)S(1)} %get-tuple-element.8.refs_1_, bf16[512,512]{1,0:T(8,128)(2,1)S(1)} %copy-done), custom_call_target="tpu_custom_call" | custom-call | flops 1879048192 | bytes 1318912 | tf_op jit(solution)/shard_map/pallas_call | solution.py:201
  91.4 5.0 %collective-permute-done.refs_1_ = bf16[1040,128]{1,0:T(8,128)(2,1)S(1)} collective-permute-done((bf16[1040,128]{1,0:T(8,128)(2,1)S(1)}, bf16[1040,128]{1,0:T(8,128)(2,1)S(1)}, u32[]{:S(2)}, u32[]{:S(2)}) %collective-permute-start) | collective-permute-done | bytes 266272 | tf_op jit(solution)/shard_map/ppermute | solution.py:223
  96.3 1.5 %shard_map.43 = f32[512,512]{1,0:T(8,128)} custom-call(bf16[512,512]{1,0:T(8,128)(2,1)S(1)} %shard_map.42.refs_0_, bf16[1040,128]{1,0:T(8,128)(2,1)S(1)} %collective-permute-done.refs_1_), custom_call_target="tpu_custom_call" | custom-call | flops 268435456 | bytes 1839104 | tf_op jit(solution)/shard_map/pallas_call | solution.py:201
Async XLA Ops:
  74.1 14.6 %copy-start = (bf16[512,512]{1,0:T(8,128)(2,1)S(1)}, bf16[512,512]{1,0:T(8,128)(2,1)}, u32[]{:S(2)}) copy-start(bf16[512,512]{1,0:T(8,128)(2,1)} %refs_2_.1) | copy-start | bytes 1572868
  74.9 13.8 %all-to-all-start.3 = ((bf16[8,128,128]{2,1,0:T(8,128)(2,1)}), bf16[8,128,128]{2,1,0:T(8,128)(2,1)S(1)}, u32[]{:S(2)}, u32[]{:S(2)}) async-start(bf16[8,128,128]{2,1,0:T(8,128)(2,1)} %shard_map.41), calls=%async_computation.3 | async-start | bytes 524288 | tf_op jit(solution)/shard_map/all_to_all | solution.py:214
  78.3 18.0 %collective-permute-start = (bf16[1040,128]{1,0:T(8,128)(2,1)S(1)}, bf16[1040,128]{1,0:T(8,128)(2,1)S(1)}, u32[]{:S(2)}, u32[]{:S(2)}) collective-permute-start(bf16[1040,128]{1,0:T(8,128)(2,1)S(1)} %shard_map.40.refs_1_), channel_id=1, source_target_pairs={{0,0},{1,64},{2,130},{3,194},{4,260},{5,324},{6,390},{7,454},{8,8}... | collective-permute-start | bytes 798728 | tf_op jit(solution)/shard_map/ppermute | solution.py:223

commit v13 on v8

--- a/solution.py
+++ b/solution.py
@@ -208,10 +208,13 @@
     return lax.all_to_all(data, axes, split_axis=0, concat_axis=0, tiled=True)
 
 
+MOVES = ((0, 2, 0, 2), (1, 1, 1, 1), (2, 0, 2, 0), (3, 3, 3, 3))
+
+
 def transpose_places(data):
     places = np.arange(np.prod(SIZES)).reshape(SIZES)
     pairs = [
-        (int(places[x, yl, z, yh, c]), int(places[yh, c, z, (x + yh) % 4, yl]))
+        (int(places[x, yl, z, yh, c]), int(places[yh, c, z, (yh + MOVES[x][yh]) % 4, yl]))
         for x, yl, z, yh, c in np.ndindex(*SIZES)
     ]
     return lax.ppermute(data, AXES, pairs)

time: 97.3 us -> 96.8 us (level)
  no operation moved by 1% of the time
where the time goes in v13:
time: 96.8 us; the launch traced here: 96.4 us
  blocking collectives  66.9 us (69%)
  starting transfers between devices  10.2 us (11%)
  waiting for transfers between devices  8.6 us (9%)
  Pallas kernels  8.54 us (9%)
  local copies, waits for them, and re-layouts  2.13 us (2%)
    all_to_all x3, blocking collectives, exchange(): return lax.all_to_all(data, axes, split_axis=0, concat_axis=0, tiled=True)  66.9 us
    pallas_call x7, Pallas kernels, call(): pl.pallas_call(body, out_shape=outs, in_specs=[VMEM] * len(args) + [ANYWH...  8.54 us
    ppermute x1, starting transfers between devices, transpose_places(): return lax.ppermute(data, AXES, pairs)  6.77 us
    ppermute x1, waiting for transfers between devices, transpose_places(): return lax.ppermute(data, AXES, pairs)  4.99 us
    all_to_all x1, waiting for transfers between devices, exchange(): return lax.all_to_all(data, axes, split_axis=0, concat_axis=0, tiled=True)  3.61 us
    all_to_all x1, starting transfers between devices, exchange(): return lax.all_to_all(data, axes, split_axis=0, concat_axis=0, tiled=True)  3.41 us
    unnamed x6, local copies, waits for them, and re-layouts  2.13 us
  transfers between devices with their start and end apart: 2, of which 2 were waited for; matrix products, arithmetic and copies ran while one was open for 0% of the time, Pallas kernels for 3%

profile of v13, /device:TPU:6, one launch (start us, length us, event | category | flops | bytes accessed | tf_op | source)
XLA Modules:
  0.0 96.4 jit_solution(210285456405139029)
XLA Ops:
  0.0 0.0 copy-start
  0.0 1.2 %copy-done = bf16[128,4096]{1,0:T(8,128)(2,1)S(1)} copy-done((bf16[128,4096]{1,0:T(8,128)(2,1)S(1)}, bf16[128,4096]{1,0:T(8,128)(2,1)}, u32[]{:S(2)}) %copy-start) | copy-done | bytes 1048600
  1.2 0.0 copy-start.1
  1.2 0.9 copy-done.1
  2.1 0.4 shard_map.37
  2.6 45.2 %all_to_all.20.refs_0_ = bf16[8,656,128]{2,1,0:T(8,128)(2,1)S(1)} all-to-all(bf16[8,656,128]{2,1,0:T(8,128)(2,1)S(1)} %shard_map.37), channel_id=1, replica_groups=mesh['x'=4,'yl'=2,'z'=8,'yh'=4,'c'=2] {'z'}, dimensions={0} | all-to-all | bytes 2686976 | tf_op jit(solution)/shard_map/all_to_all | solution.py:208
  47.7 0.8 shard_map.38
  48.5 11.4 %all_to_all.21.refs_0_ = bf16[8,192,128]{2,1,0:T(8,128)(2,1)S(1)} all-to-all(bf16[8,192,128]{2,1,0:T(8,128)(2,1)S(1)} %shard_map.38), channel_id=1, replica_groups=mesh['x'=4,'yl'=2,'z'=8,'yh'=4,'c'=2] {'x','yl'}, dimensions={0} | all-to-all | bytes 786432 | tf_op jit(solution)/shard_map/all_to_all | solution.py:208
  59.9 0.1 shard_map.39
  60.0 10.3 %all_to_all.22.refs_0_ = bf16[8,144,128]{2,1,0:T(8,128)(2,1)S(1)} all-to-all(bf16[8,144,128]{2,1,0:T(8,128)(2,1)S(1)} %get-tuple-element.7), channel_id=1, replica_groups=mesh['x'=4,'yl'=2,'z'=8,'yh'=4,'c'=2] {'x','yl'}, dimensions={0} | all-to-all | bytes 589824 | tf_op jit(solution)/shard_map/all_to_all | solution.py:208
  70.3 2.4 %shard_map.40.refs_1_ = bf16[1040,128]{1,0:T(8,128)(2,1)S(1)} custom-call(bf16[8,144,128]{2,1,0:T(8,128)(2,1)S(1)} %all_to_all.22.refs_0_, f32[16,128]{1,0:T(8,128)S(1)} %get-tuple-element.8.refs_1_), custom_call_target="tpu_custom_call" | custom-call | flops 1610612736 | bytes 569344 | tf_op jit(solution)/shard_map/pallas_call | solution.py:195
  72.6 0.0 copy-start.2
  72.7 0.7 shard_map.41
  73.4 3.4 %all-to-all-start.3 = ((bf16[8,128,128]{2,1,0:T(8,128)(2,1)}), bf16[8,128,128]{2,1,0:T(8,128)(2,1)S(1)}, u32[]{:S(2)}, u32[]{:S(2)}) async-start(bf16[8,128,128]{2,1,0:T(8,128)(2,1)} %shard_map.41), calls=%async_computation.3 | async-start | bytes 524288 | tf_op jit(solution)/shard_map/all_to_all | solution.py:208
  76.8 6.8 %collective-permute-start = (bf16[1040,128]{1,0:T(8,128)(2,1)S(1)}, bf16[1040,128]{1,0:T(8,128)(2,1)S(1)}, u32[]{:S(2)}, u32[]{:S(2)}) collective-permute-start(bf16[1040,128]{1,0:T(8,128)(2,1)S(1)} %shard_map.40.refs_1_), channel_id=1, source_target_pairs={{0,0},{1,64},{2,134},{3,198},{4,260},{5,324},{6,386},{7,450},{8,8}... | collective-permute-start | bytes 798728 | tf_op jit(solution)/shard_map/ppermute | solution.py:220
  83.6 3.6 %all-to-all-done.3 = bf16[8,128,128]{2,1,0:T(8,128)(2,1)S(1)} async-done(((bf16[8,128,128]{2,1,0:T(8,128)(2,1)}), bf16[8,128,128]{2,1,0:T(8,128)(2,1)S(1)}, u32[]{:S(2)}, u32[]{:S(2)}) %all-to-all-start.3) | async-done | bytes 262176 | tf_op jit(solution)/shard_map/all_to_all | solution.py:208
  87.2 0.0 copy-done.2
  87.2 2.6 %shard_map.42.refs_0_ = bf16[512,512]{1,0:T(8,128)(2,1)S(1)} custom-call(bf16[1024,128]{1,0:T(8,128)(2,1)S(1)} %bitcast.1, f32[16,128]{1,0:T(8,128)S(1)} %get-tuple-element.8.refs_1_, bf16[512,512]{1,0:T(8,128)(2,1)S(1)} %copy-done.2), custom_call_target="tpu_custom_call" | custom-call | flops 1879048192 | bytes 1318912 | tf_op jit(solution)/shard_map/pallas_call | solution.py:195
  89.9 5.0 %collective-permute-done.refs_1_ = bf16[1040,128]{1,0:T(8,128)(2,1)S(1)} collective-permute-done((bf16[1040,128]{1,0:T(8,128)(2,1)S(1)}, bf16[1040,128]{1,0:T(8,128)(2,1)S(1)}, u32[]{:S(2)}, u32[]{:S(2)}) %collective-permute-start) | collective-permute-done | bytes 266272 | tf_op jit(solution)/shard_map/ppermute | solution.py:220
  94.9 1.5 %shard_map.43 = f32[512,512]{1,0:T(8,128)} custom-call(bf16[512,512]{1,0:T(8,128)(2,1)S(1)} %shard_map.42.refs_0_, bf16[1040,128]{1,0:T(8,128)(2,1)S(1)} %collective-permute-done.refs_1_), custom_call_target="tpu_custom_call" | custom-call | flops 268435456 | bytes 1839104 | tf_op jit(solution)/shard_map/pallas_call | solution.py:195
Async XLA Ops:
  0.0 1.2 %copy-start = (bf16[128,4096]{1,0:T(8,128)(2,1)S(1)}, bf16[128,4096]{1,0:T(8,128)(2,1)}, u32[]{:S(2)}) copy-start(bf16[128,4096]{1,0:T(8,128)(2,1)} %refs_1_.1) | copy-start | bytes 3145732
  1.2 0.9 copy-start.1
  72.6 14.6 %copy-start.2 = (bf16[512,512]{1,0:T(8,128)(2,1)S(1)}, bf16[512,512]{1,0:T(8,128)(2,1)}, u32[]{:S(2)}) copy-start(bf16[512,512]{1,0:T(8,128)(2,1)} %refs_2_.1) | copy-start | bytes 1572868
  73.4 13.8 %all-to-all-start.3 = ((bf16[8,128,128]{2,1,0:T(8,128)(2,1)}), bf16[8,128,128]{2,1,0:T(8,128)(2,1)S(1)}, u32[]{:S(2)}, u32[]{:S(2)}) async-start(bf16[8,128,128]{2,1,0:T(8,128)(2,1)} %shard_map.41), calls=%async_computation.3 | async-start | bytes 524288 | tf_op jit(solution)/shard_map/all_to_all | solution.py:208
  76.8 18.0 %collective-permute-start = (bf16[1040,128]{1,0:T(8,128)(2,1)S(1)}, bf16[1040,128]{1,0:T(8,128)(2,1)S(1)}, u32[]{:S(2)}, u32[]{:S(2)}) collective-permute-start(bf16[1040,128]{1,0:T(8,128)(2,1)S(1)} %shard_map.40.refs_1_), channel_id=1, source_target_pairs={{0,0},{1,64},{2,134},{3,198},{4,260},{5,324},{6,386},{7,450},{8,8}... | collective-permute-start | bytes 798728 | tf_op jit(solution)/shard_map/ppermute | solution.py:220

commit v14 on v13

--- a/solution.py
+++ b/solution.py
@@ -245,15 +245,16 @@
         sum_kernel, [got], [((PEERS, GATHER, TILE), BF16), ((2 * DIAGONAL, TILE), F32)]
     )
     got = exchange(sent, ("x", "yl"))
+    sent = call(copies_kernel, [got], [((PEERS, SHARE, TILE), BF16)])
     root = call(
         grad_root_kernel,
         [got, ends],
         [((ROOT, TILE), BF16)],
         [(full, F32), (packed, BF16)],
         6 * cube,
+        [sent],
     )
     grad_root = transpose_places(root)
-    sent = call(copies_kernel, [got], [((PEERS, SHARE, TILE), BF16)], after=[root])
     act_cov = exchange(sent, "z").reshape(packed)
     left = call(left_kernel, [act_cov, ends, grad], [(full, BF16)], [(full, F32)], 7 * cube)
     return call(last_kernel, [left, grad_root], [(full, F32)], [(full, BF16)], cube)

time: 96.8 us -> 96.7 us (level)
    all_to_all x1, waiting for transfers between devices: 3.61 us -> 1.2 us  [exchange(): return lax.all_to_all(data, axes, split_axis=0, concat_axis=0, tiled=True)]
    ppermute x1, waiting for transfers between devices: 4.99 us -> 7.39 us  [transpose_places(): return lax.ppermute(data, AXES, pairs)]
  transfers between devices with their start and end apart: 2 -> 2, of which waited for: 2 -> 2; matrix products, arithmetic and copies ran while one was open for 0% -> 0% of each run, Pallas kernels for 3% -> 5%
where the time goes in v14:
time: 96.7 us; the launch traced here: 96.4 us
  blocking collectives  66.9 us (69%)
  starting transfers between devices  10.2 us (11%)
  waiting for transfers between devices  8.59 us (9%)
  Pallas kernels  8.54 us (9%)
  local copies, waits for them, and re-layouts  2.13 us (2%)
    all_to_all x3, blocking collectives, exchange(): return lax.all_to_all(data, axes, split_axis=0, concat_axis=0, tiled=True)  66.9 us
    pallas_call x7, Pallas kernels, call(): pl.pallas_call(body, out_shape=outs, in_specs=[VMEM] * len(args) + [ANYWH...  8.54 us
    ppermute x1, waiting for transfers between devices, transpose_places(): return lax.ppermute(data, AXES, pairs)  7.39 us
    ppermute x1, starting transfers between devices, transpose_places(): return lax.ppermute(data, AXES, pairs)  6.78 us
    all_to_all x1, starting transfers between devices, exchange(): return lax.all_to_all(data, axes, split_axis=0, concat_axis=0, tiled=True)  3.41 us
    unnamed x6, local copies, waits for them, and re-layouts  2.13 us
  transfers between devices with their start and end apart: 2, of which 2 were waited for; matrix products, arithmetic and copies ran while one was open for 0% of the time, Pallas kernels for 5%

profile of v14, /device:TPU:6, one launch (start us, length us, event | category | flops | bytes accessed | tf_op | source)
XLA Modules:
  0.0 96.4 jit_solution(12543056861188583821)
XLA Ops:
  0.0 0.0 copy-start
  0.0 1.2 %copy-done = bf16[128,4096]{1,0:T(8,128)(2,1)S(1)} copy-done((bf16[128,4096]{1,0:T(8,128)(2,1)S(1)}, bf16[128,4096]{1,0:T(8,128)(2,1)}, u32[]{:S(2)}) %copy-start) | copy-done | bytes 1048600
  1.2 0.0 copy-start.1
  1.2 0.9 copy-done.1
  2.1 0.4 shard_map.37
  2.6 45.2 %all_to_all.20.refs_0_ = bf16[8,656,128]{2,1,0:T(8,128)(2,1)S(1)} all-to-all(bf16[8,656,128]{2,1,0:T(8,128)(2,1)S(1)} %shard_map.37), channel_id=1, replica_groups=mesh['x'=4,'yl'=2,'z'=8,'yh'=4,'c'=2] {'z'}, dimensions={0} | all-to-all | bytes 2686976 | tf_op jit(solution)/shard_map/all_to_all | solution.py:208
  47.7 0.8 shard_map.38
  48.5 11.4 %all_to_all.21.refs_0_ = bf16[8,192,128]{2,1,0:T(8,128)(2,1)S(1)} all-to-all(bf16[8,192,128]{2,1,0:T(8,128)(2,1)S(1)} %shard_map.38), channel_id=1, replica_groups=mesh['x'=4,'yl'=2,'z'=8,'yh'=4,'c'=2] {'x','yl'}, dimensions={0} | all-to-all | bytes 786432 | tf_op jit(solution)/shard_map/all_to_all | solution.py:208
  59.9 0.1 shard_map.39
  60.0 10.3 %all_to_all.22.refs_0_ = bf16[8,144,128]{2,1,0:T(8,128)(2,1)S(1)} all-to-all(bf16[8,144,128]{2,1,0:T(8,128)(2,1)S(1)} %get-tuple-element.7), channel_id=1, replica_groups=mesh['x'=4,'yl'=2,'z'=8,'yh'=4,'c'=2] {'x','yl'}, dimensions={0} | all-to-all | bytes 589824 | tf_op jit(solution)/shard_map/all_to_all | solution.py:208
  70.3 0.7 shard_map.40.refs_2_
  71.0 3.4 %all-to-all-start.3 = ((bf16[8,128,128]{2,1,0:T(8,128)(2,1)}), bf16[8,128,128]{2,1,0:T(8,128)(2,1)S(1)}, u32[]{:S(2)}, u32[]{:S(2)}) async-start(bf16[8,128,128]{2,1,0:T(8,128)(2,1)} %shard_map.40.refs_2_), calls=%async_computation.3 | async-start | bytes 524288 | tf_op jit(solution)/shard_map/all_to_all | solution.py:208
  74.4 0.0 copy-start.2
  74.4 2.4 %shard_map.42 = bf16[1040,128]{1,0:T(8,128)(2,1)S(1)} custom-call(bf16[8,144,128]{2,1,0:T(8,128)(2,1)S(1)} %all_to_all.22.refs_0_, f32[16,128]{1,0:T(8,128)S(1)} %get-tuple-element.8.refs_1_, bf16[8,128,128]{2,1,0:T(8,128)(2,1)} %shard_map.40.refs_2_), custom_call_target="tpu_custom_call" | custom-call | flops 1610612736 | bytes 569344 | tf_op jit(solution)/shard_map/pallas_call | solution.py:195
  76.8 6.8 %collective-permute-start = (bf16[1040,128]{1,0:T(8,128)(2,1)S(1)}, bf16[1040,128]{1,0:T(8,128)(2,1)S(1)}, u32[]{:S(2)}, u32[]{:S(2)}) collective-permute-start(bf16[1040,128]{1,0:T(8,128)(2,1)S(1)} %shard_map.42), channel_id=1, source_target_pairs={{0,0},{1,64},{2,134},{3,198},{4,260},{5,324},{6,386},{7,450},{8,8}... | collective-permute-start | bytes 798728 | tf_op jit(solution)/shard_map/ppermute | solution.py:220
  83.6 1.2 %all-to-all-done.3 = bf16[8,128,128]{2,1,0:T(8,128)(2,1)S(1)} async-done(((bf16[8,128,128]{2,1,0:T(8,128)(2,1)}), bf16[8,128,128]{2,1,0:T(8,128)(2,1)S(1)}, u32[]{:S(2)}, u32[]{:S(2)}) %all-to-all-start.3) | async-done | bytes 262176 | tf_op jit(solution)/shard_map/all_to_all | solution.py:208
  84.8 0.0 copy-done.2
  84.8 2.6 %shard_map.41.refs_0_ = bf16[512,512]{1,0:T(8,128)(2,1)S(1)} custom-call(bf16[1024,128]{1,0:T(8,128)(2,1)S(1)} %bitcast.1, f32[16,128]{1,0:T(8,128)S(1)} %get-tuple-element.8.refs_1_, bf16[512,512]{1,0:T(8,128)(2,1)S(1)} %copy-done.2), custom_call_target="tpu_custom_call" | custom-call | flops 1879048192 | bytes 1318912 | tf_op jit(solution)/shard_map/pallas_call | solution.py:195
  87.5 7.4 %collective-permute-done.refs_1_ = bf16[1040,128]{1,0:T(8,128)(2,1)S(1)} collective-permute-done((bf16[1040,128]{1,0:T(8,128)(2,1)S(1)}, bf16[1040,128]{1,0:T(8,128)(2,1)S(1)}, u32[]{:S(2)}, u32[]{:S(2)}) %collective-permute-start) | collective-permute-done | bytes 266272 | tf_op jit(solution)/shard_map/ppermute | solution.py:220
  94.8 1.5 %shard_map.43 = f32[512,512]{1,0:T(8,128)} custom-call(bf16[512,512]{1,0:T(8,128)(2,1)S(1)} %shard_map.41.refs_0_, bf16[1040,128]{1,0:T(8,128)(2,1)S(1)} %collective-permute-done.refs_1_), custom_call_target="tpu_custom_call" | custom-call | flops 268435456 | bytes 1839104 | tf_op jit(solution)/shard_map/pallas_call | solution.py:195
Async XLA Ops:
  0.0 1.2 %copy-start = (bf16[128,4096]{1,0:T(8,128)(2,1)S(1)}, bf16[128,4096]{1,0:T(8,128)(2,1)}, u32[]{:S(2)}) copy-start(bf16[128,4096]{1,0:T(8,128)(2,1)} %refs_1_.1) | copy-start | bytes 3145732
  1.2 0.9 copy-start.1
  71.0 13.8 %all-to-all-start.3 = ((bf16[8,128,128]{2,1,0:T(8,128)(2,1)}), bf16[8,128,128]{2,1,0:T(8,128)(2,1)S(1)}, u32[]{:S(2)}, u32[]{:S(2)}) async-start(bf16[8,128,128]{2,1,0:T(8,128)(2,1)} %shard_map.40.refs_2_), calls=%async_computation.3 | async-start | bytes 524288 | tf_op jit(solution)/shard_map/all_to_all | solution.py:208
  74.4 10.4 %copy-start.2 = (bf16[512,512]{1,0:T(8,128)(2,1)S(1)}, bf16[512,512]{1,0:T(8,128)(2,1)}, u32[]{:S(2)}) copy-start(bf16[512,512]{1,0:T(8,128)(2,1)} %refs_2_.1) | copy-start | bytes 1572868
  76.8 18.0 %collective-permute-start = (bf16[1040,128]{1,0:T(8,128)(2,1)S(1)}, bf16[1040,128]{1,0:T(8,128)(2,1)S(1)}, u32[]{:S(2)}, u32[]{:S(2)}) collective-permute-start(bf16[1040,128]{1,0:T(8,128)(2,1)S(1)} %shard_map.42), channel_id=1, source_target_pairs={{0,0},{1,64},{2,134},{3,198},{4,260},{5,324},{6,386},{7,450},{8,8}... | collective-permute-start | bytes 798728 | tf_op jit(solution)/shard_map/ppermute | solution.py:220
